TPU v7x, 32 devices: a whole 2x2x4 slice. The times are simulated.
32 devices in a mesh: expert: 8 (over z, x), dp: 4 (over y, core).
Axes of the slice: x: 2, y: 2, z: 4, core: 2. Of those that a mesh axis runs over, the one named last changes fastest.
Arguments:
- tokens: bfloat16 [4096, 2048], P(('expert', 'dp')), may hold values from -6 to 6
- doc_ids: int32 [32, 128], P(('expert', 'dp')), may hold values from 0 to 3, never falling along the last dimension, each value on 1 to 64 neighbouring positions
- routes: int32 [4096, 6], P(('expert', 'dp')), may hold values from 0 to 15, all different within a row; in each aligned block of 128 rows (0 to 127, 128 to 255, ...) at most 64 rows name the same one
- gain_attn: bfloat16 [2048], P(('expert', 'dp')), may hold values from 0.25 to 1.75
- w_query: bfloat16 [2048, 2048], P(('expert', 'dp')), may hold values from -0.125 to 0.125
- w_key: bfloat16 [2048, 512], P(('expert', 'dp')), may hold values from -0.125 to 0.125
- w_value: bfloat16 [2048, 512], P(('expert', 'dp')), may hold values from -0.125 to 0.125
- w_out: bfloat16 [2048, 2048], P(('expert', 'dp')), may hold values from -0.5 to 0.5
- gain_moe: bfloat16 [2048], P(('expert', 'dp')), may hold values from 0.25 to 1.75
- w_router: bfloat16 [2048, 16], P(('expert', 'dp')), may hold values from -0.0625 to 0.0625
- shared_gate: bfloat16 [2048, 2816], P(('expert', 'dp')), may hold values from -0.125 to 0.125
- shared_up: bfloat16 [2048, 2816], P(('expert', 'dp')), may hold values from -0.125 to 0.125
- shared_down: bfloat16 [2816, 2048], P(('expert', 'dp')), may hold values from -0.109375 to 0.109375
- expert_gate: bfloat16 [16, 2048, 1408], P('expert', 'dp'), may hold values from -0.125 to 0.125
- expert_up: bfloat16 [16, 2048, 1408], P('expert', 'dp'), may hold values from -0.125 to 0.125
- expert_down: bfloat16 [16, 2048, 1408], P('expert', 'dp'), may hold values from -0.4375 to 0.4375
- cotangent: bfloat16 [4096, 2048], P(('expert', 'dp')), may hold values from -6 to 6
Outputs:
- output: bfloat16 [4096, 2048], P(('expert', 'dp'))
- grad_tokens: float32 [4096, 2048], P(('expert', 'dp'))
- grad_gain_attn: float32 [2048], P(('expert', 'dp'))
- grad_w_query: float32 [2048, 2048], P(('expert', 'dp'))
- grad_w_key: float32 [2048, 512], P(('expert', 'dp'))
- grad_w_value: float32 [2048, 512], P(('expert', 'dp'))
- grad_w_out: float32 [2048, 2048], P(('expert', 'dp'))
- grad_gain_moe: float32 [2048], P(('expert', 'dp'))
- grad_w_router: float32 [2048, 16], P(('expert', 'dp'))
- grad_shared_gate: float32 [2048, 2816], P(('expert', 'dp'))
- grad_shared_up: float32 [2048, 2816], P(('expert', 'dp'))
- grad_shared_down: float32 [2816, 2048], P(('expert', 'dp'))
- grad_expert_gate: float32 [16, 2048, 1408], P('expert', 'dp')
- grad_expert_up: float32 [16, 2048, 1408], P('expert', 'dp')
- grad_expert_down: float32 [16, 2048, 1408], P('expert', 'dp')
Inputs may be any that keep to these rules, and one draw needn't show every extreme that they name: `doc_ids`: within each sequence the document numbers never fall, each document has 1 to 64 positions. `routes`: A token's 6 experts differ. Among the 128 rows of one sequence no expert is named by more than 64 rows; in some sequences one is named by exactly 64.
All inputs are finite; a program needn't handle non-finite values.
Results may differ from a plain program's by a relative error of at most 0.015.
Values may be sent and summed in bfloat16 or wider, within the bound.
A program may use at most 384 MiB of HBM per device.

v0:
```python
import jax
import jax.numpy as jnp
from jax import lax
from jax.sharding import PartitionSpec as P

HEADS = 16
KV_HEADS = 4
HEAD_DIM = 128
TOP = 6


epsilon = 1e-06
rope_base = 10000.0


def product(left, right):
    return jnp.dot(left, right, preferred_element_type=jnp.float32)


def contract_rows(left, right):
    return lax.dot_general(
        left, right, (((0,), (0,)), ((), ())), preferred_element_type=jnp.float32
    )


def contract_cols(left, right):
    return lax.dot_general(
        left, right, (((1,), (1,)), ((), ())), preferred_element_type=jnp.float32
    )


def rms_norm(values, gain_row):
    factor = lax.rsqrt(jnp.mean(values * values, axis=-1, keepdims=True) + epsilon)
    return values * factor * gain_row


def rotate(values):
    length = values.shape[0]
    half_dim = values.shape[-1] // 2
    position = jnp.arange(length).astype(jnp.float32)
    inverse = rope_base ** (-jnp.arange(half_dim).astype(jnp.float32) * 2.0 / values.shape[-1])
    angle_table = position[:, None] * inverse[None, :]
    cosine = jnp.cos(angle_table)[:, None, :]
    sine_table = jnp.sin(angle_table)[:, None, :]
    lower_half = values[..., :half_dim]
    upper_half = values[..., half_dim:]
    return jnp.concatenate(
        [
            lower_half * cosine - upper_half * sine_table,
            upper_half * cosine + lower_half * sine_table,
        ],
        axis=-1,
    )


def route_slots(routes, experts_total, capacity):
    flat_routes = routes.reshape(-1)
    hit_table = (flat_routes[:, None] == jnp.arange(experts_total)[None, :]).astype(jnp.int32)
    before = jnp.cumsum(hit_table, axis=0) - hit_table
    return flat_routes * capacity + jnp.sum(before * hit_table, axis=1)


def silu_pair(gate_part, up_part):
    return jax.nn.silu(gate_part) * up_part


def shards(
    tokens,
    doc_ids,
    routes,
    gain_attn,
    w_query,
    w_key,
    w_value,
    w_out,
    gain_moe,
    w_router,
    shared_gate,
    shared_up,
    shared_down,
    expert_gate,
    expert_up,
    expert_down,
    cotangent,
):
    length = tokens.shape[0]
    width = tokens.shape[1]
    group_size = HEADS // KV_HEADS
    score_scale = HEAD_DIM ** (-0.5)
    expert_ranks = lax.axis_size("expert")
    local_experts = expert_gate.shape[0]
    experts_total = local_experts * expert_ranks
    capacity = length * TOP * 4 // (3 * experts_total)
    slot_rows = experts_total * capacity
    attn_gain, query_full, key_full, value_full, out_full = (
        lax.all_gather(gain_attn, ("expert", "dp"), axis=0, tiled=True),
        lax.all_gather(w_query, ("expert", "dp"), axis=0, tiled=True),
        lax.all_gather(w_key, ("expert", "dp"), axis=0, tiled=True),
        lax.all_gather(w_value, ("expert", "dp"), axis=0, tiled=True),
        lax.all_gather(w_out, ("expert", "dp"), axis=0, tiled=True),
    )
    moe_gain, router_full, share_gate, share_up, share_down = (
        lax.all_gather(gain_moe, ("expert", "dp"), axis=0, tiled=True),
        lax.all_gather(w_router, ("expert", "dp"), axis=0, tiled=True),
        lax.all_gather(shared_gate, ("expert", "dp"), axis=0, tiled=True),
        lax.all_gather(shared_up, ("expert", "dp"), axis=0, tiled=True),
        lax.all_gather(shared_down, ("expert", "dp"), axis=0, tiled=True),
    )
    routed_gate, routed_up, routed_down = (
        lax.all_gather(expert_gate, "dp", axis=1, tiled=True),
        lax.all_gather(expert_up, "dp", axis=1, tiled=True),
        lax.all_gather(expert_down, "dp", axis=1, tiled=True),
    )
    inputs = tokens.astype(jnp.float32)
    normed, attn_norm_pull = jax.vjp(rms_norm, inputs, attn_gain.astype(jnp.float32))
    normed_low = normed.astype(jnp.bfloat16)
    query_pre = product(normed_low, query_full).reshape(length, HEADS, HEAD_DIM)
    key_pre = product(normed_low, key_full).reshape(length, KV_HEADS, HEAD_DIM)
    value_low = (
        product(normed_low, value_full).astype(jnp.bfloat16).reshape(length, KV_HEADS, HEAD_DIM)
    )
    query_rot, query_pull = jax.vjp(rotate, query_pre)
    key_rot, key_pull = jax.vjp(rotate, key_pre)
    query_low = query_rot.astype(jnp.bfloat16).reshape(length, KV_HEADS, group_size, HEAD_DIM)
    key_low = key_rot.astype(jnp.bfloat16)
    position = jnp.arange(length)
    doc_row = doc_ids[0]
    allowed = (position[None, :] <= position[:, None]) & (doc_row[None, :] == doc_row[:, None])

    def scores_of():
        raw_scores = (
            jnp.einsum("tkgd,skd->kgts", query_low, key_low, preferred_element_type=jnp.float32)
            * score_scale
        )
        return jnp.where(allowed, raw_scores, -1e30)

    scores = scores_of()
    top_score = jnp.max(scores, axis=-1, keepdims=True)
    exp_scores = jnp.exp(scores - top_score)
    exp_total = jnp.sum(exp_scores, axis=-1, keepdims=True)
    log_total = top_score + jnp.log(exp_total)
    attend_low = (exp_scores / exp_total).astype(jnp.bfloat16)
    mixed_rows = jnp.einsum(
        "kgts,skd->tkgd", attend_low, value_low, preferred_element_type=jnp.float32
    )
    mixed_low = mixed_rows.reshape(length, HEADS * HEAD_DIM).astype(jnp.bfloat16)
    hidden = inputs + product(mixed_low, out_full)
    normed_moe, moe_norm_pull = jax.vjp(rms_norm, hidden, moe_gain.astype(jnp.float32))
    moe_low = normed_moe.astype(jnp.bfloat16)
    logits = product(moe_low, router_full)
    chosen = jnp.take_along_axis(logits, routes, axis=1)
    gate_weights = jax.nn.softmax(chosen, axis=-1)
    flat_slot = route_slots(routes, experts_total, capacity)
    token_index = jnp.arange(length * TOP) // TOP
    slot_token = jnp.full((slot_rows,), -1, jnp.int32).at[flat_slot].set(token_index)
    dispatch = (slot_token[:, None] == position[None, :]).astype(jnp.bfloat16)
    outgoing = (
        product(dispatch, moe_low)
        .astype(jnp.bfloat16)
        .reshape(expert_ranks, local_experts, capacity, width)
    )
    arrived = lax.all_to_all(outgoing, "expert", split_axis=0, concat_axis=0, tiled=True)
    gate_rows = jnp.einsum(
        "nlcd,ldf->nlcf", arrived, routed_gate, preferred_element_type=jnp.float32
    )
    up_rows = jnp.einsum("nlcd,ldf->nlcf", arrived, routed_up, preferred_element_type=jnp.float32)
    inner_low, expert_pull = jax.vjp(silu_pair, gate_rows, up_rows)
    inner_low = inner_low.astype(jnp.bfloat16)
    produced = jnp.einsum(
        "nlcf,ldf->nlcd", inner_low, routed_down, preferred_element_type=jnp.float32
    ).astype(jnp.bfloat16)
    returned = lax.all_to_all(produced, "expert", split_axis=0, concat_axis=0, tiled=True).reshape(
        slot_rows, width
    )
    picked = jnp.take(returned, flat_slot, axis=0).reshape(length, TOP, width)
    routed = jnp.sum(gate_weights[:, :, None] * picked, axis=1)
    share_g = product(moe_low, share_gate)
    share_u = product(moe_low, share_up)
    share_low, share_pull = jax.vjp(silu_pair, share_g, share_u)
    share_low = share_low.astype(jnp.bfloat16)
    shared_out = product(share_low, share_down)
    output = (hidden + routed + shared_out).astype(jnp.bfloat16)
    grad_out = cotangent.astype(jnp.float32)
    router_back, gate_back, up_back, down_back = (
        lax.all_gather(w_router, ("expert", "dp"), axis=0, tiled=True),
        lax.all_gather(shared_gate, ("expert", "dp"), axis=0, tiled=True),
        lax.all_gather(shared_up, ("expert", "dp"), axis=0, tiled=True),
        lax.all_gather(shared_down, ("expert", "dp"), axis=0, tiled=True),
    )
    grad_share_down = contract_rows(share_low, cotangent)
    grad_share_inner = contract_cols(cotangent, down_back)
    grad_sg, grad_su = share_pull(grad_share_inner)
    grad_sg_low = grad_sg.astype(jnp.bfloat16)
    grad_su_low = grad_su.astype(jnp.bfloat16)
    grad_share_gate = contract_rows(moe_low, grad_sg_low)
    grad_share_up = contract_rows(moe_low, grad_su_low)
    grad_moe_normed = contract_cols(grad_sg_low, gate_back) + contract_cols(grad_su_low, up_back)
    grad_gates = jnp.sum(picked * grad_out[:, None, :], axis=2)
    slot_gate = jnp.zeros((slot_rows,), jnp.float32).at[flat_slot].set(gate_weights.reshape(-1))
    grad_rows = (slot_gate[:, None] * product(dispatch, cotangent)).astype(jnp.bfloat16)
    grad_arrived = lax.all_to_all(
        grad_rows.reshape(expert_ranks, local_experts, capacity, width),
        "expert",
        split_axis=0,
        concat_axis=0,
        tiled=True,
    )
    grad_routed_down = jnp.einsum(
        "nlcd,nlcf->ldf", grad_arrived, inner_low, preferred_element_type=jnp.float32
    )
    grad_inner = jnp.einsum(
        "nlcd,ldf->nlcf", grad_arrived, routed_down, preferred_element_type=jnp.float32
    )
    grad_gate_rows, grad_up_rows = expert_pull(grad_inner)
    grad_gate_low = grad_gate_rows.astype(jnp.bfloat16)
    grad_up_low = grad_up_rows.astype(jnp.bfloat16)
    grad_routed_gate = jnp.einsum(
        "nlcd,nlcf->ldf", arrived, grad_gate_low, preferred_element_type=jnp.float32
    )
    grad_routed_up = jnp.einsum(
        "nlcd,nlcf->ldf", arrived, grad_up_low, preferred_element_type=jnp.float32
    )
    grad_dispatched = jnp.einsum(
        "nlcf,ldf->nlcd", grad_gate_low, routed_gate, preferred_element_type=jnp.float32
    )
    grad_dispatched = (
        grad_dispatched
        + jnp.einsum("nlcf,ldf->nlcd", grad_up_low, routed_up, preferred_element_type=jnp.float32)
    ).astype(jnp.bfloat16)
    expert_sums = (
        lax.psum_scatter(grad_routed_gate, "dp", scatter_dimension=1, tiled=True),
        lax.psum_scatter(grad_routed_up, "dp", scatter_dimension=1, tiled=True),
        lax.psum_scatter(grad_routed_down, "dp", scatter_dimension=1, tiled=True),
    )
    grad_back = lax.all_to_all(
        grad_dispatched, "expert", split_axis=0, concat_axis=0, tiled=True
    ).reshape(slot_rows, width)
    grad_picked = (
        jnp.take(grad_back, flat_slot, axis=0).reshape(length, TOP, width).astype(jnp.float32)
    )
    grad_moe_normed = grad_moe_normed + jnp.sum(grad_picked, axis=1)
    grad_chosen = gate_weights * (
        grad_gates - jnp.sum(gate_weights * grad_gates, axis=-1, keepdims=True)
    )
    choice_hot = routes[:, :, None] == jnp.arange(experts_total)[None, None, :]
    grad_logits = jnp.sum(jnp.where(choice_hot, grad_chosen[:, :, None], 0.0), axis=1).astype(
        jnp.bfloat16
    )
    grad_router = contract_rows(moe_low, grad_logits)
    grad_moe_normed = grad_moe_normed + contract_cols(grad_logits, router_back)
    grad_hidden_norm, grad_gain_moe = moe_norm_pull(grad_moe_normed)
    grad_hidden = grad_out + grad_hidden_norm
    moe_sums = (
        lax.psum_scatter(grad_gain_moe, ("expert", "dp"), scatter_dimension=0, tiled=True),
        lax.psum_scatter(grad_router, ("expert", "dp"), scatter_dimension=0, tiled=True),
        lax.psum_scatter(grad_share_gate, ("expert", "dp"), scatter_dimension=0, tiled=True),
        lax.psum_scatter(grad_share_up, ("expert", "dp"), scatter_dimension=0, tiled=True),
        lax.psum_scatter(grad_share_down, ("expert", "dp"), scatter_dimension=0, tiled=True),
    )
    query_back, key_back, value_back, out_back = (
        lax.all_gather(w_query, ("expert", "dp"), axis=0, tiled=True),
        lax.all_gather(w_key, ("expert", "dp"), axis=0, tiled=True),
        lax.all_gather(w_value, ("expert", "dp"), axis=0, tiled=True),
        lax.all_gather(w_out, ("expert", "dp"), axis=0, tiled=True),
    )
    grad_hidden_low = grad_hidden.astype(jnp.bfloat16)
    grad_out_proj = contract_rows(mixed_low, grad_hidden_low)
    grad_mixed = (
        contract_cols(grad_hidden_low, out_back)
        .astype(jnp.bfloat16)
        .reshape(length, KV_HEADS, group_size, HEAD_DIM)
    )
    attend = jnp.exp(scores_of() - log_total)
    attend_back = attend.astype(jnp.bfloat16)
    grad_value = jnp.einsum(
        "kgts,tkgd->skd", attend_back, grad_mixed, preferred_element_type=jnp.float32
    )
    grad_attend = jnp.einsum(
        "tkgd,skd->kgts", grad_mixed, value_low, preferred_element_type=jnp.float32
    )
    grad_scores = (
        attend * (grad_attend - jnp.sum(grad_attend * attend, axis=-1, keepdims=True))
    ).astype(jnp.bfloat16)
    grad_query = (
        jnp.einsum("kgts,skd->tkgd", grad_scores, key_low, preferred_element_type=jnp.float32)
        * score_scale
    )
    grad_key = (
        jnp.einsum("kgts,tkgd->skd", grad_scores, query_low, preferred_element_type=jnp.float32)
        * score_scale
    )
    grad_query_low = (
        query_pull(grad_query.reshape(length, HEADS, HEAD_DIM))[0]
        .reshape(length, HEADS * HEAD_DIM)
        .astype(jnp.bfloat16)
    )
    grad_key_low = key_pull(grad_key)[0].reshape(length, KV_HEADS * HEAD_DIM).astype(jnp.bfloat16)
    grad_value_low = grad_value.reshape(length, KV_HEADS * HEAD_DIM).astype(jnp.bfloat16)
    grad_query_proj = contract_rows(normed_low, grad_query_low)
    grad_key_proj = contract_rows(normed_low, grad_key_low)
    grad_value_proj = contract_rows(normed_low, grad_value_low)
    grad_normed = (
        contract_cols(grad_query_low, query_back)
        + contract_cols(grad_key_low, key_back)
        + contract_cols(grad_value_low, value_back)
    )
    grad_inputs_norm, grad_gain_attn = attn_norm_pull(grad_normed)
    grad_tokens = grad_hidden + grad_inputs_norm
    attn_sums = (
        lax.psum_scatter(grad_gain_attn, ("expert", "dp"), scatter_dimension=0, tiled=True),
        lax.psum_scatter(grad_query_proj, ("expert", "dp"), scatter_dimension=0, tiled=True),
        lax.psum_scatter(grad_key_proj, ("expert", "dp"), scatter_dimension=0, tiled=True),
        lax.psum_scatter(grad_value_proj, ("expert", "dp"), scatter_dimension=0, tiled=True),
        lax.psum_scatter(grad_out_proj, ("expert", "dp"), scatter_dimension=0, tiled=True),
    )
    return (
        output,
        grad_tokens,
        attn_sums[0],
        attn_sums[1],
        attn_sums[2],
        attn_sums[3],
        attn_sums[4],
        moe_sums[0],
        moe_sums[1],
        moe_sums[2],
        moe_sums[3],
        moe_sums[4],
        expert_sums[0],
        expert_sums[1],
        expert_sums[2],
    )


def solution(mesh):
    placed = (
        P(("expert", "dp"), None),
        P(("expert", "dp"), None),
        P(("expert", "dp"), None),
        P(("expert", "dp")),
        P(("expert", "dp"), None),
        P(("expert", "dp"), None),
        P(("expert", "dp"), None),
        P(("expert", "dp"), None),
        P(("expert", "dp")),
        P(("expert", "dp"), None),
        P(("expert", "dp"), None),
        P(("expert", "dp"), None),
        P(("expert", "dp"), None),
        P("expert", "dp", None),
        P("expert", "dp", None),
        P("expert", "dp", None),
        P(("expert", "dp"), None),
    )
    return jax.shard_map(
        shards,
        mesh=mesh,
        in_specs=placed,
        out_specs=(
            P(("expert", "dp"), None),
            P(("expert", "dp"), None),
            P(("expert", "dp")),
            P(("expert", "dp"), None),
            P(("expert", "dp"), None),
            P(("expert", "dp"), None),
            P(("expert", "dp"), None),
            P(("expert", "dp")),
            P(("expert", "dp"), None),
            P(("expert", "dp"), None),
            P(("expert", "dp"), None),
            P(("expert", "dp"), None),
            P("expert", "dp", None),
            P("expert", "dp", None),
            P("expert", "dp", None),
        ),
        check_vma=False,
    )
```

profile of v0, /device:TPU:0, one launch (start us, length us, event | category | flops | bytes accessed | tf_op | source)
XLA Modules:
  0.0 3024.6 jit_solution(15064241127850853624)
XLA Ops:
  14.4 42.1 %all-reduce.9 = (bf16[2048]{0:T(1024)(128)(2,1)S(1)}, bf16[2048]{0:T(1024)(128)(2,1)S(1)}) all-reduce(bf16[2048]{0:T(1024)(128)(2,1)S(1)} %dynamic-update-slice, bf16[2048]{0:T(1024)(128)(2,1)S(1)} %dynamic-update-slice.1), channel_id=1, replica_groups=mesh['expert'=8,'dp'=4] {'expert','dp'}, use_global_device_ids=true, to_apply=%add.4 | all-reduce | flops 4096 | bytes 16384
  72.2 56.0 %all-gather.12.cloned.1.call-done = bf16[2048,512]{1,0:T(8,128)(2,1)} async-done(((bf16[64,512]{1,0:T(8,128)(2,1)}), bf16[2048,512]{1,0:T(8,128)(2,1)}) %all-gather.12.cloned.1.call-update) | async-done | bytes 2097168 | tf_op jit(solution)/shard_map/all_gather | solution.py:99
  130.7 76.9 %all-gather.16.cloned.1.call-done = bf16[2048,2048]{1,0:T(8,128)(2,1)} async-done(((bf16[64,2048]{1,0:T(8,128)(2,1)}), bf16[2048,2048]{1,0:T(8,128)(2,1)}) %all-gather.16.cloned.1.call-update) | async-done | bytes 8388624 | tf_op jit(solution)/shard_map/all_gather | solution.py:97
  215.9 70.6 %all-gather.18.cloned.1.call-done = bf16[2048,2048]{1,0:T(8,128)(2,1)} async-done(((bf16[64,2048]{1,0:T(8,128)(2,1)}), bf16[2048,2048]{1,0:T(8,128)(2,1)}) %all-gather.18.cloned.1.call-update) | async-done | bytes 8388624 | tf_op jit(solution)/shard_map/all_gather | solution.py:100
  301.2 61.5 %all-gather.20.cloned.1.call-done = bf16[2,2048,1408]{2,1,0:T(8,128)(2,1)} async-done(((bf16[2,512,1408]{2,1,0:T(8,128)(2,1)}), bf16[2,2048,1408]{2,1,0:T(8,128)(2,1)}) %all-gather.20.cloned.1.call-update) | async-done | bytes 11534352 | tf_op jit(solution)/shard_map/all_gather | solution.py:110
  362.7 32.3 %all-to-all-done = bf16[8,2,64,2048]{3,2,1,0:T(8,128)(2,1)} async-done(((bf16[8,2,64,2048]{3,2,1,0:T(8,128)(2,1)}), bf16[8,2,64,2048]{3,2,1,0:T(8,128)(2,1)}, u32[]{:S(2)}, u32[]{:S(2)}) %all-to-all-start) | async-done | bytes 4194336 | tf_op jit(solution)/shard_map/all_to_all | solution.py:162
  408.3 31.9 %all-gather.22.cloned.1.call-done = bf16[2,2048,1408]{2,1,0:T(8,128)(2,1)} async-done(((bf16[2,512,1408]{2,1,0:T(8,128)(2,1)}), bf16[2,2048,1408]{2,1,0:T(8,128)(2,1)}) %all-gather.22.cloned.1.call-update) | async-done | bytes 11534352 | tf_op jit(solution)/shard_map/all_gather | solution.py:111
  440.3 15.6 fusion.16
  455.9 62.1 %all-gather.24.cloned.1.call-done = bf16[2,2048,1408]{2,1,0:T(8,128)(2,1)} async-done(((bf16[2,512,1408]{2,1,0:T(8,128)(2,1)}), bf16[2,2048,1408]{2,1,0:T(8,128)(2,1)}) %all-gather.24.cloned.1.call-update) | async-done | bytes 11534352 | tf_op jit(solution)/shard_map/all_gather | solution.py:112
  549.6 109.4 %all-gather = bf16[32,64,16]{1,2,0:T(8,128)(2,1)S(1)} all-gather(bf16[1,64,16]{1,2,0:T(8,128)(2,1)S(1)} %bitcast.239), channel_id=1, replica_groups=mesh['expert'=8,'dp'=4] {'expert','dp'}, dimensions={0}, use_global_device_ids=true | all-gather | bytes 67584 | tf_op jit(solution)/shard_map/all_gather | solution.py:104
  693.0 173.1 %all_to_all.20 = bf16[8,2,64,2048]{3,2,1,0:T(8,128)(2,1)S(1)} all-to-all(bf16[8,2,64,2048]{3,2,1,0:T(8,128)(2,1)S(1)} %bitcast.213), channel_id=1, replica_groups=mesh['expert'=8,'dp'=4] {'expert'}, dimensions={0} | all-to-all | bytes 8388608 | tf_op jit(solution)/shard_map/all_to_all | solution.py:201
  866.2 16.8 fusion.14
  950.1 59.8 %all-to-all-done.3 = bf16[8,2,64,2048]{3,2,1,0:T(8,128)(2,1)} async-done(((bf16[8,2,64,2048]{3,2,1,0:T(8,128)(2,1)}), bf16[8,2,64,2048]{3,2,1,0:T(8,128)(2,1)}, u32[]{:S(2)}, u32[]{:S(2)}) %all-to-all-start.3) | async-done | bytes 4194336 | tf_op jit(solution)/shard_map/all_to_all | solution.py:235
  1133.3 13.5 convolution_bitcast_fusion
  1187.3 38.0 %all-reduce.8 = (f32[2048]{0:T(1024)S(1)}, f32[2048]{0:T(1024)S(1)}) all-reduce(f32[2048]{0:T(1024)S(1)} %get-tuple-element.18, f32[2048]{0:T(1024)S(1)} %copy-done.60), channel_id=2, replica_groups=mesh['expert'=8,'dp'=4] {'expert','dp'}, use_global_device_ids=true, to_apply=%region_20.22.clone | all-reduce | flops 4096 | bytes 32768
  1249.6 129.3 %reduce-scatter.16.cloned.1.call-done = f32[64,512]{1,0:T(8,128)} async-done(((f32[2048,512]{1,0:T(8,128)}), f32[64,512]{1,0:T(8,128)}) %reduce-scatter.16.cloned.1.call-update) | async-done | bytes 131088 | tf_op jit(solution)/shard_map/reduce_scatter | solution.py:312
  1378.9 246.0 %reduce-scatter.22.cloned.1.call-done = f32[64,2816]{1,0:T(8,128)} async-done(((f32[2048,2816]{1,0:T(8,128)}), f32[64,2816]{1,0:T(8,128)}) %reduce-scatter.22.cloned.1.call-update) | async-done | bytes 720912 | tf_op jit(solution)/shard_map/reduce_scatter | solution.py:256
  1624.9 252.5 %reduce-scatter.24.cloned.1.call-done = f32[64,2816]{1,0:T(8,128)} async-done(((f32[2048,2816]{1,0:T(8,128)}), f32[64,2816]{1,0:T(8,128)}) %reduce-scatter.24.cloned.1.call-update) | async-done | bytes 720912 | tf_op jit(solution)/shard_map/reduce_scatter | solution.py:257
  1877.4 252.5 %reduce-scatter.26.cloned.1.call-done = f32[88,2048]{1,0:T(8,128)} async-done(((f32[2816,2048]{1,0:T(8,128)}), f32[88,2048]{1,0:T(8,128)}) %reduce-scatter.26.cloned.1.call-update) | async-done | bytes 720912 | tf_op jit(solution)/shard_map/reduce_scatter | solution.py:258
  2129.9 188.2 %reduce-scatter.14.cloned.1.call-done = f32[64,2048]{1,0:T(8,128)} async-done(((f32[2048,2048]{1,0:T(8,128)}), f32[64,2048]{1,0:T(8,128)}) %reduce-scatter.14.cloned.1.call-update) | async-done | bytes 524304 | tf_op jit(solution)/shard_map/reduce_scatter | solution.py:311
  2318.1 187.4 %reduce-scatter.20.cloned.1.call-done = f32[64,2048]{1,0:T(8,128)} async-done(((f32[2048,2048]{1,0:T(8,128)}), f32[64,2048]{1,0:T(8,128)}) %reduce-scatter.20.cloned.1.call-update) | async-done | bytes 524304 | tf_op jit(solution)/shard_map/reduce_scatter | solution.py:314
  2505.6 171.7 %reduce-scatter.32.cloned.1.call-done = f32[2,512,1408]{2,1,0:T(8,128)} async-done(((f32[2,2048,1408]{2,1,0:T(8,128)}), f32[2,512,1408]{2,1,0:T(8,128)}) %reduce-scatter.32.cloned.1.call-update) | async-done | bytes 5767184 | tf_op jit(solution)/shard_map/reduce_scatter | solution.py:233
  2677.2 169.8 %reduce-scatter.28.cloned.1.call-done = f32[2,512,1408]{2,1,0:T(8,128)} async-done(((f32[2,2048,1408]{2,1,0:T(8,128)}), f32[2,512,1408]{2,1,0:T(8,128)}) %reduce-scatter.28.cloned.1.call-update) | async-done | bytes 5767184 | tf_op jit(solution)/shard_map/reduce_scatter | solution.py:231
  2847.0 170.2 %reduce-scatter.30.cloned.1.call-done = f32[2,512,1408]{2,1,0:T(8,128)} async-done(((f32[2,2048,1408]{2,1,0:T(8,128)}), f32[2,512,1408]{2,1,0:T(8,128)}) %reduce-scatter.30.cloned.1.call-update) | async-done | bytes 5767184 | tf_op jit(solution)/shard_map/reduce_scatter | solution.py:232
  (323 shorter events, 381.2 us)
Async XLA Ops:
  7.2 62.8 %all-gather.14.cloned.1.call-start = ((), (), s32[]{:S(2)}) async-start(), calls=%async_computation.16 | async-start | bytes 2162688 | tf_op jit(solution)/shard_map/all_gather | solution.py:98
  8.0 120.3 %all-gather.12.cloned.1.call-start = ((), (), s32[]{:S(2)}) async-start(), calls=%async_computation.15 | async-start | bytes 2162688 | tf_op jit(solution)/shard_map/all_gather | solution.py:99
  8.7 198.9 %all-gather.16.cloned.1.call-start = ((), (), s32[]{:S(2)}) async-start(), calls=%async_computation.17 | async-start | bytes 8650752 | tf_op jit(solution)/shard_map/all_gather | solution.py:97
  9.5 277.0 %all-gather.18.cloned.1.call-start = ((), (), s32[]{:S(2)}) async-start(), calls=%async_computation.18 | async-start | bytes 8650752 | tf_op jit(solution)/shard_map/all_gather | solution.py:100
  10.0 352.7 %all-gather.20.cloned.1.call-start = ((), (), s32[]{:S(2)}) async-start(), calls=%async_computation.19 | async-start | bytes 14417920 | tf_op jit(solution)/shard_map/all_gather | solution.py:110
  10.6 429.7 %all-gather.22.cloned.1.call-start = ((), (), s32[]{:S(2)}) async-start(), calls=%async_computation.20 | async-start | bytes 14417920 | tf_op jit(solution)/shard_map/all_gather | solution.py:111
  11.2 506.9 %all-gather.24.cloned.1.call-start = ((), (), s32[]{:S(2)}) async-start(), calls=%async_computation.21 | async-start | bytes 14417920 | tf_op jit(solution)/shard_map/all_gather | solution.py:112
  11.9 903.0 %all-gather.26.cloned.1.call-start = ((), (), s32[]{:S(2)}) async-start(), calls=%async_computation.22 | async-start | bytes 11894784 | tf_op jit(solution)/shard_map/all_gather | solution.py:105
  12.7 909.7 %all-gather.28.cloned.1.call-start = ((), (), s32[]{:S(2)}) async-start(), calls=%async_computation.23 | async-start | bytes 11894784 | tf_op jit(solution)/shard_map/all_gather | solution.py:106
  295.9 99.1 %all-to-all-start = ((bf16[8,2,64,2048]{3,2,1,0:T(8,128)(2,1)}), bf16[8,2,64,2048]{3,2,1,0:T(8,128)(2,1)}, u32[]{:S(2)}, u32[]{:S(2)}) async-start(bf16[8,2,64,2048]{3,2,1,0:T(8,128)(2,1)} %bitcast.214), calls=%async_computation | async-start | bytes 8388608 | tf_op jit(solution)/shard_map/all_to_all | solution.py:162
  530.8 141.9 %all-to-all-start.1 = ((bf16[8,2,64,2048]{3,2,1,0:T(8,128)(2,1)}), bf16[8,2,64,2048]{3,2,1,0:T(8,128)(2,1)}, u32[]{:S(2)}, u32[]{:S(2)}) async-start(bf16[8,2,64,2048]{3,2,1,0:T(8,128)(2,1)} %copy.177), calls=%async_computation.1 | async-start | bytes 8388608 | tf_op jit(solution)/shard_map/all_to_all | solution.py:172
  536.5 393.0 %all-gather.30.cloned.1.call-start = ((), (), s32[]{:S(2)}) async-start(), calls=%async_computation.24 | async-start | bytes 11894784 | tf_op jit(solution)/shard_map/all_gather | solution.py:107
  909.9 100.0 %all-to-all-start.3 = ((bf16[8,2,64,2048]{3,2,1,0:T(8,128)(2,1)}), bf16[8,2,64,2048]{3,2,1,0:T(8,128)(2,1)}, u32[]{:S(2)}, u32[]{:S(2)}) async-start(bf16[8,2,64,2048]{3,2,1,0:T(8,128)(2,1)} %copy.180), calls=%async_computation.3 | async-start | bytes 8388608 | tf_op jit(solution)/shard_map/all_to_all | solution.py:235
  914.6 262.7 %reduce-scatter.34.cloned.1.call-start = ((), (), s32[]{:S(2)}) async-start(), calls=%async_computation.35 | async-start | bytes 1081344
  949.6 300.1 %reduce-scatter.18.cloned.1.call-start = ((), (), s32[]{:S(2)}) async-start(), calls=%async_computation.27 | async-start | bytes 4325376 | tf_op jit(solution)/shard_map/reduce_scatter | solution.py:313
  1067.3 311.6 %reduce-scatter.16.cloned.1.call-start = ((), (), s32[]{:S(2)}) async-start(), calls=%async_computation.26 | async-start | bytes 4325376 | tf_op jit(solution)/shard_map/reduce_scatter | solution.py:312
  1074.9 550.0 %reduce-scatter.22.cloned.1.call-start = ((), (), s32[]{:S(2)}) async-start(), calls=%async_computation.29 | async-start | bytes 23789568 | tf_op jit(solution)/shard_map/reduce_scatter | solution.py:256
  1084.5 792.9 %reduce-scatter.24.cloned.1.call-start = ((), (), s32[]{:S(2)}) async-start(), calls=%async_computation.30 | async-start | bytes 23789568 | tf_op jit(solution)/shard_map/reduce_scatter | solution.py:257
  1095.0 1034.9 %reduce-scatter.26.cloned.1.call-start = ((), (), s32[]{:S(2)}) async-start(), calls=%async_computation.31 | async-start | bytes 23789568 | tf_op jit(solution)/shard_map/reduce_scatter | solution.py:258
  1105.7 1212.5 %reduce-scatter.14.cloned.1.call-start = ((), (), s32[]{:S(2)}) async-start(), calls=%async_computation.25 | async-start | bytes 17301504 | tf_op jit(solution)/shard_map/reduce_scatter | solution.py:311
  1122.2 1383.3 %reduce-scatter.20.cloned.1.call-start = ((), (), s32[]{:S(2)}) async-start(), calls=%async_computation.28 | async-start | bytes 17301504 | tf_op jit(solution)/shard_map/reduce_scatter | solution.py:314
  1131.5 1545.8 %reduce-scatter.32.cloned.1.call-start = ((), (), s32[]{:S(2)}) async-start(), calls=%async_computation.34 | async-start | bytes 28835840 | tf_op jit(solution)/shard_map/reduce_scatter | solution.py:233
  1146.8 1700.2 %reduce-scatter.28.cloned.1.call-start = ((), (), s32[]{:S(2)}) async-start(), calls=%async_computation.32 | async-start | bytes 28835840 | tf_op jit(solution)/shard_map/reduce_scatter | solution.py:231
  1162.0 1855.2 %reduce-scatter.30.cloned.1.call-start = ((), (), s32[]{:S(2)}) async-start(), calls=%async_computation.33 | async-start | bytes 28835840 | tf_op jit(solution)/shard_map/reduce_scatter | solution.py:232
  (73 other events, 2104.1 us)
Sparse Core Ops, SparseCore 0:
  10.9 59.0 all-gather.13
  72.9 55.2 all-gather.11
  131.1 76.4 all-gather.15
  210.3 76.1 all-gather.17
  287.9 74.7 all-gather.19
  364.1 76.1 all-gather.21
  441.9 76.1 all-gather.23
  520.9 160.6 all-gather.25
  684.4 140.2 all-gather.27
  827.4 94.0 all-gather.29
  949.7 149.0 reduce-scatter.33
  1101.6 137.0 reduce-scatter.17
  1241.6 137.2 reduce-scatter.15
  1381.8 243.1 reduce-scatter.21
  1627.7 249.6 reduce-scatter.23
  1880.2 249.6 reduce-scatter.25
  2132.7 185.3 reduce-scatter.13
  2321.0 184.5 reduce-scatter.19
  2508.9 168.2 reduce-scatter.31
  2680.3 166.7 reduce-scatter.27
  2850.4 166.7 reduce-scatter.29
where the time goes:
time: 3030 us; the launch traced here: 3020 us
  waiting for transfers between devices  2240 us (74%)
  blocking collectives  363 us (12%)
  matrix products  263 us (9%)
  local copies, waits for them, and re-layouts  91.4 us (3%)
  other arithmetic  34.4 us (1%)
    reduce_scatter x1, waiting for transfers between devices, shards(): lax.psum_scatter(grad_share_down, ('expert', 'dp'), scatter_dimension=0,...  252 us
    reduce_scatter x1, waiting for transfers between devices, shards(): lax.psum_scatter(grad_share_up, ('expert', 'dp'), scatter_dimension=0, ti...  252 us
    reduce_scatter x1, waiting for transfers between devices, shards(): lax.psum_scatter(grad_share_gate, ('expert', 'dp'), scatter_dimension=0,...  246 us
    reduce_scatter x1, waiting for transfers between devices, shards(): lax.psum_scatter(grad_query_proj, ('expert', 'dp'), scatter_dimension=0,...  188 us
    reduce_scatter x1, waiting for transfers between devices, shards(): lax.psum_scatter(grad_out_proj, ('expert', 'dp'), scatter_dimension=0, ti...  187 us
    all_to_all x1, blocking collectives, shards(): lax.all_to_all(grad_rows.reshape(expert_ranks, local_experts, capacity, w...  173 us
    reduce_scatter x1, waiting for transfers between devices, shards(): lax.psum_scatter(grad_routed_down, 'dp', scatter_dimension=1, tiled=True)  172 us
    reduce_scatter x1, waiting for transfers between devices, shards(): lax.psum_scatter(grad_routed_up, 'dp', scatter_dimension=1, tiled=True)  170 us
  transfers between devices with their start and end apart: 24, of which 19 were waited for; matrix products, arithmetic and copies ran while one was open for 12% of the time, Pallas kernels for 0%

commit v1 on v0

v1 whole, which is shorter than its diff:
```python
import functools

import jax
import jax.numpy as jnp
from jax import lax
from jax.experimental import pallas as pl
from jax.experimental.pallas import tpu as pltpu
from jax.sharding import Mesh
from jax.sharding import PartitionSpec as P

HEADS = 16
KV_HEADS = 4
HEAD_DIM = 128
TOP = 6
EPS = 1e-06
ROPE_BASE = 10000.0
PLANE = ("a", "b", "l")
ALL = ("a", "b", "l", "s")
F32 = jnp.float32
BF16 = jnp.bfloat16
MESH = pl.DeviceIdType.MESH
VMEM_LIMIT = 60 * 1024 * 1024


def dot(left, right):
    return jnp.dot(left, right, preferred_element_type=F32)


def dot_tn(left, right):
    return lax.dot_general(left, right, (((0,), (0,)), ((), ())), preferred_element_type=F32)


def dot_nt(left, right):
    return lax.dot_general(left, right, (((1,), (1,)), ((), ())), preferred_element_type=F32)


class Grid:
    def __init__(self, sizes):
        self.na, self.nb, self.nl, self.ns = sizes
        self.a, self.b, self.l, self.s = (lax.axis_index(axis) for axis in "abls")

    def at(self, a=None, b=None, l=None, s=None):
        return tuple(
            own if other is None else other
            for own, other in zip((self.a, self.b, self.l, self.s), (a, b, l, s))
        )

    def other(self, axis, step):
        size, own = {"b": (self.nb, self.b), "l": (self.nl, self.l), "s": (self.ns, self.s)}[axis]
        return lax.rem(own + step, size)

    def greet(self, siblings):
        barrier = pltpu.get_barrier_semaphore()

        def hello(device):
            pl.semaphore_signal(barrier, inc=1, device_id=device, device_id_type=MESH)

        @pl.when(self.a > 0)
        def _():
            hello(self.at(a=self.a - 1))

        @pl.when(self.a < self.na - 1)
        def _():
            hello(self.at(a=self.a + 1))

        for step in range(1, self.nb):
            hello(self.at(b=self.other("b", step)))
        for step in range(1, self.nl):
            hello(self.at(l=self.other("l", step)))
        count = self.nb + self.nl - 2
        if siblings:
            for step in range(1, self.ns):
                hello(self.at(s=self.other("s", step)))
            count += self.ns - 1
        above = 1 - (self.a + 1) // self.na
        below = (self.a + self.na - 1) // self.na
        pl.semaphore_wait(barrier, count + above + below)


def remote(src, dst, send, recv, device):
    return pltpu.make_async_remote_copy(
        src_ref=src, dst_ref=dst, send_sem=send, recv_sem=recv, device_id=device, device_id_type=MESH
    )


def gather_kernel(sizes, siblings, x_ref, o_ref, own_sem, a_sem, b_sem, l_sem, bb_sem, ll_sem, s_sem):
    g = Grid(sizes)
    na, nb, nl, ns = sizes
    wide = x_ref.shape[-1]
    half = (wide // 256) * 128
    first, second = pl.ds(0, half), pl.ds(half, wide - half)
    me = g.s if siblings else 0
    g.greet(siblings)

    def slot(a, b, l, s=None):
        return o_ref.at[a, b, l, me if s is None else s]

    own = pltpu.make_async_copy(x_ref, slot(g.a, g.b, g.l), own_sem)
    own.start()
    sends = []

    def up(k):
        src = x_ref if k == 0 else slot(g.a - k, g.b, g.l)
        return remote(src, slot(g.a - k, g.b, g.l), a_sem.at[0, 0, k], a_sem.at[1, 0, k], g.at(a=g.a + 1))

    def down(k):
        src = x_ref if k == 0 else slot(g.a + k, g.b, g.l)
        return remote(src, slot(g.a + k, g.b, g.l), a_sem.at[0, 1, k], a_sem.at[1, 1, k], g.at(a=g.a - 1))

    def came(sem, dst):
        remote(dst, dst, sem, sem, g.at()).wait_recv()

    def sibling_sends(index, own_x=False):
        if siblings:
            a, b, l = index
            for step in range(1, ns):
                remote(
                    x_ref if own_x else slot(a, b, l),
                    slot(a, b, l),
                    s_sem.at[0, step - 1, a, b, l],
                    s_sem.at[1, step - 1, a, b, l],
                    g.at(s=g.other("s", step)),
                ).start()

    def spread(origin, own_x=False):
        src = x_ref if own_x else slot(origin, g.b, g.l)
        dst = slot(origin, g.b, g.l)
        for step in range(1, nb):
            remote(src, dst, b_sem.at[0, step - 1, origin], b_sem.at[1, step - 1, origin], g.at(b=g.other("b", step))).start()
        for step in range(1, nl):
            remote(src, dst, l_sem.at[0, step - 1, origin], l_sem.at[1, step - 1, origin], g.at(l=g.other("l", step))).start()
        sibling_sends((origin, g.b, g.l), own_x)

    def relay(origin):
        for step in range(1, nb):
            b_from = g.other("b", nb - step)
            came(b_sem.at[1, step - 1, origin], slot(origin, b_from, g.l))
            for turn in range(1, nl):
                part = slot(origin, b_from, g.l).at[:, first]
                remote(part, part, ll_sem.at[0, step - 1, turn - 1, origin], ll_sem.at[1, step - 1, turn - 1, origin], g.at(l=g.other("l", turn))).start()
            sibling_sends((origin, b_from, g.l))
        for step in range(1, nl):
            l_from = g.other("l", nl - step)
            came(l_sem.at[1, step - 1, origin], slot(origin, g.b, l_from))
            for turn in range(1, nb):
                part = slot(origin, g.b, l_from).at[:, second]
                remote(part, part, bb_sem.at[0, step - 1, turn - 1, origin], bb_sem.at[1, step - 1, turn - 1, origin], g.at(b=g.other("b", turn))).start()
            sibling_sends((origin, g.b, l_from))

    def finish(origin):
        for step in range(1, nb):
            b_from = g.other("b", nb - step)
            for turn in range(1, nl):
                l_from = g.other("l", nl - turn)
                came(ll_sem.at[1, step - 1, turn - 1, origin], slot(origin, b_from, l_from).at[:, first])
                came(bb_sem.at[1, turn - 1, step - 1, origin], slot(origin, b_from, l_from).at[:, second])
                sibling_sends((origin, b_from, l_from))

    has_up, has_down = g.a < na - 1, g.a > 0

    @pl.when(has_up)
    def _():
        up(0).start()

    @pl.when(has_down)
    def _():
        down(0).start()

    spread(g.a, True)
    for k in range(na - 1):
        @pl.when(g.a - 1 - k >= 0)
        def _():
            came(a_sem.at[1, 0, k], slot(g.a - 1 - k, g.b, g.l))
            if k + 1 < na - 1:
                @pl.when(has_up)
                def _():
                    up(k + 1).start()
            spread(g.a - 1 - k)

        @pl.when(g.a + 1 + k < na)
        def _():
            came(a_sem.at[1, 1, k], slot(g.a + 1 + k, g.b, g.l))
            if k + 1 < na - 1:
                @pl.when(has_down)
                def _():
                    down(k + 1).start()
            spread(g.a + 1 + k)

        if k == 0:
            relay(g.a)
        else:
            @pl.when(g.a - k >= 0)
            def _():
                relay(g.a - k)

            @pl.when(g.a + k < na)
            def _():
                relay(g.a + k)

    last = na - 1

    @pl.when(g.a - last >= 0)
    def _():
        relay(g.a - last)

    @pl.when(g.a + last < na)
    def _():
        relay(g.a + last)

    for origin in range(na):
        finish(origin)
    own.wait()
    for k in range(na - 1):
        @pl.when(has_up & (g.a - k >= 0))
        def _():
            up(k).wait_send()

        @pl.when(has_down & (g.a + k < na))
        def _():
            down(k).wait_send()

    def left(sem, ref):
        remote(ref, ref, sem, sem, g.at()).wait_send()

    for origin in range(na):
        whole = slot(origin, g.b, g.l)
        for step in range(1, nb):
            left(b_sem.at[0, step - 1, origin], whole)
            for turn in range(1, nl):
                left(ll_sem.at[0, step - 1, turn - 1, origin], whole.at[:, first])
        for step in range(1, nl):
            left(l_sem.at[0, step - 1, origin], whole)
            for turn in range(1, nb):
                left(bb_sem.at[0, step - 1, turn - 1, origin], whole.at[:, second])
        if siblings:
            for b in range(nb):
                for l in range(nl):
                    for step in range(1, ns):
                        s_from = g.other("s", ns - step)
                        came(s_sem.at[1, step - 1, origin, b, l], slot(origin, b, l, s_from))
                        left(s_sem.at[0, step - 1, origin, b, l], slot(origin, b, l))


def gather(x, sizes, siblings, collective_id):
    na, nb, nl, ns = sizes
    rows, wide = x.shape
    depth = ns if siblings else 1
    dma = pltpu.SemaphoreType.DMA
    out = pl.pallas_call(
        functools.partial(gather_kernel, sizes, siblings),
        out_shape=jax.ShapeDtypeStruct((na, nb, nl, depth, rows, wide), x.dtype),
        in_specs=[pl.BlockSpec(memory_space=pl.ANY)],
        out_specs=pl.BlockSpec(memory_space=pl.ANY),
        scratch_shapes=[
            dma,
            dma((2, 2, na - 1)),
            dma((2, nb - 1, na)),
            dma((2, nl - 1, na)),
            dma((2, nl - 1, nb - 1, na)),
            dma((2, nb - 1, nl - 1, na)),
            dma((2, max(ns - 1, 1), na, nb, nl)),
        ],
        compiler_params=pltpu.CompilerParams(collective_id=collective_id, has_side_effects=True),
        cost_estimate=pl.CostEstimate(flops=0, bytes_accessed=2 * na * nb * nl * depth * rows * wide * 2, transcendentals=0),
    )(x)
    return out.reshape(-1, wide)


def order(a, k):
    high, odd = a // 2, lax.rem(a, 2)
    return (3 * (1 - high), 2 + high - 2 * odd, 1 + odd, a)[k]


def add_rows(out, *terms):
    rows = out.shape[0]
    step = min(rows, 32)

    @pl.loop(0, rows, step=step)
    def _(r):
        at = pl.ds(pl.multiple_of(r, step), step)
        total = terms[0][at, :].astype(F32)
        for term in terms[1:]:
            total = total + term[at, :].astype(F32)
        out[at, :] = total.astype(out.dtype)


def scatter_kernel(sizes, siblings, p_ref, o_ref, l_one, b_one, b_two, l_two, total, line, s_buf,
                   l_sem, b_sem, bb_sem, ll_sem, a_sem, s_sem):
    g = Grid(sizes)
    na, nb, nl, ns = sizes
    wide = o_ref.shape[-1]
    half = (wide // 256) * 128
    first, second = pl.ds(0, half), pl.ds(half, wide - half)
    g.greet(siblings)

    def part(k, b, l, cols):
        if siblings:
            return s_buf.at[0, k, b, l, :, cols]
        return p_ref.at[order(g.a, k), b, l, 0, :, cols]

    def sibling_copy(k, step):
        to = g.other("s", step)
        return remote(p_ref.at[order(g.a, k), :, :, to], s_buf.at[step - 1, k],
                      s_sem.at[0, step - 1, k], s_sem.at[1, step - 1, k], g.at(s=to))

    def l_first(k, step):
        to = g.other("l", step)
        if siblings:
            src = s_buf.at[0, k, :, to, :, first]
        else:
            src = p_ref.at[order(g.a, k), :, to, 0, :, first]
        return remote(src, l_one.at[step - 1, k], l_sem.at[0, step - 1, k], l_sem.at[1, step - 1, k], g.at(l=to))

    def b_first(k, step):
        to = g.other("b", step)
        if siblings:
            src = s_buf.at[0, k, to, :, :, second]
        else:
            src = p_ref.at[order(g.a, k), to, :, 0, :, second]
        return remote(src, b_one.at[step - 1, k], b_sem.at[0, step - 1, k], b_sem.at[1, step - 1, k], g.at(b=to))

    def b_then(k, step):
        to = g.other("b", step)
        return remote(l_one.at[0, k, to], b_two.at[step - 1, k], bb_sem.at[0, step - 1, k], bb_sem.at[1, step - 1, k], g.at(b=to))

    def l_then(k, step):
        to = g.other("l", step)
        return remote(b_one.at[0, k, to], l_two.at[step - 1, k], ll_sem.at[0, step - 1, k], ll_sem.at[1, step - 1, k], g.at(l=to))

    def line_copy(k, way):
        dest = order(g.a, k)
        return remote(total.at[k], line.at[way, dest], a_sem.at[0, way, dest], a_sem.at[1, way, dest], g.at(a=g.a + 1 - 2 * way))

    def line_came(way, dest):
        remote(line.at[way, dest], line.at[way, dest], a_sem.at[1, way, dest], a_sem.at[1, way, dest], g.at()).wait_recv()

    def start_first(k):
        if siblings:
            for step in range(1, ns):
                sibling_copy(k, step).wait_recv()
            for b in range(nb):
                for l in range(nl):
                    add_rows(s_buf.at[0, k, b, l], p_ref.at[order(g.a, k), b, l, g.s], *[s_buf.at[step, k, b, l] for step in range(ns - 1)])
        for step in range(1, nl):
            l_first(k, step).start()
        for step in range(1, nb):
            b_first(k, step).start()

    def start_second(k):
        for step in range(1, nl):
            l_first(k, step).wait_recv()
        for turn in range(nb):
            b = g.other("b", turn)
            add_rows(l_one.at[0, k, b], part(k, b, g.l, first), *[l_one.at[step, k, b] for step in range(nl - 1)])
            if turn:
                b_then(k, turn).start()
        for step in range(1, nb):
            b_first(k, step).wait_recv()
        for turn in range(nl):
            l = g.other("l", turn)
            add_rows(b_one.at[0, k, l], part(k, g.b, l, second), *[b_one.at[step, k, l] for step in range(nb - 1)])
            if turn:
                l_then(k, turn).start()

    def start_third(k):
        for step in range(1, nb):
            b_then(k, step).wait_recv()
        add_rows(total.at[k, :, first], l_one.at[0, k, g.b], *[b_two.at[step, k] for step in range(nb - 1)])
        for step in range(1, nl):
            l_then(k, step).wait_recv()
        add_rows(total.at[k, :, second], b_one.at[0, k, g.l], *[l_two.at[step, k] for step in range(nl - 1)])
        if k < na - 1:
            dest = order(g.a, k)

            @pl.when((g.a == 0) & (dest > g.a))
            def _():
                line_copy(k, 0).start()

            @pl.when((g.a == na - 1) & (dest < g.a))
            def _():
                line_copy(k, 1).start()

    def pass_on(k):
        dest = order(g.a, k)

        @pl.when((g.a > 0) & (dest > g.a))
        def _():
            line_came(0, dest)
            add_rows(total.at[k], total.at[k], line.at[0, dest])
            line_copy(k, 0).start()

        @pl.when((g.a < na - 1) & (dest < g.a))
        def _():
            line_came(1, dest)
            add_rows(total.at[k], total.at[k], line.at[1, dest])
            line_copy(k, 1).start()

    if siblings:
        for k in range(na):
            for step in range(1, ns):
                sibling_copy(k, step).start()
    start_first(0)
    start_first(1)
    for k in range(na):
        start_second(k)
        if k + 2 < na:
            start_first(k + 2)
        if k >= 1:
            start_third(k - 1)
        if k >= 2:
            pass_on(k - 2)
    start_third(na - 1)
    pass_on(na - 2)

    last = total.at[na - 1]

    @pl.when(g.a == 0)
    def _():
        line_came(1, g.a)
        add_rows(o_ref, last, line.at[1, g.a])

    @pl.when(g.a == na - 1)
    def _():
        line_came(0, g.a)
        add_rows(o_ref, last, line.at[0, g.a])

    @pl.when((g.a > 0) & (g.a < na - 1))
    def _():
        line_came(0, g.a)
        line_came(1, g.a)
        add_rows(o_ref, last, line.at[0, g.a], line.at[1, g.a])

    for k in range(na):
        if siblings:
            for step in range(1, ns):
                sibling_copy(k, step).wait_send()
        for step in range(1, nl):
            l_first(k, step).wait_send()
            l_then(k, step).wait_send()
        for step in range(1, nb):
            b_first(k, step).wait_send()
            b_then(k, step).wait_send()
        if k < na - 1:
            dest = order(g.a, k)

            @pl.when(dest > g.a)
            def _():
                line_copy(k, 0).wait_send()

            @pl.when(dest < g.a)
            def _():
                line_copy(k, 1).wait_send()


def scatter(partial, sizes, siblings, collective_id, dtype=F32):
    na, nb, nl, ns = sizes
    depth = ns if siblings else 1
    places = na * nb * nl * depth
    rows, wide = partial.shape[0] // places, partial.shape[1]
    half = (wide // 256) * 128
    dma = pltpu.SemaphoreType.DMA
    vmem = pl.BlockSpec(memory_space=pltpu.VMEM)
    return pl.pallas_call(
        functools.partial(scatter_kernel, sizes, siblings),
        out_shape=jax.ShapeDtypeStruct((rows, wide), dtype),
        in_specs=[vmem],
        out_specs=vmem,
        scratch_shapes=[
            pltpu.VMEM((nl - 1, na, nb, rows, half), BF16),
            pltpu.VMEM((nb - 1, na, nl, rows, wide - half), BF16),
            pltpu.VMEM((nb - 1, na, rows, half), BF16),
            pltpu.VMEM((nl - 1, na, rows, wide - half), BF16),
            pltpu.VMEM((na, rows, wide), BF16),
            pltpu.VMEM((2, na, rows, wide), BF16),
            pltpu.VMEM((ns - 1, na, nb, nl, rows, wide) if siblings else (16, 128), BF16),
            dma((2, nl - 1, na)),
            dma((2, nb - 1, na)),
            dma((2, nb - 1, na)),
            dma((2, nl - 1, na)),
            dma((2, 2, na)),
            dma((2, max(ns - 1, 1), na)),
        ],
        compiler_params=pltpu.CompilerParams(collective_id=collective_id, has_side_effects=True, vmem_limit_bytes=VMEM_LIMIT),
        cost_estimate=pl.CostEstimate(flops=0, bytes_accessed=4 * partial.size, transcendentals=0),
    )(partial.reshape(na, nb, nl, depth, rows, wide))


def rms_norm(values, gain_row):
    factor = lax.rsqrt(jnp.mean(values * values, axis=-1, keepdims=True) + EPS)
    return values * factor * gain_row


def rotate(values):
    length = values.shape[0]
    half_dim = values.shape[-1] // 2
    position = jnp.arange(length).astype(F32)
    inverse = ROPE_BASE ** (-jnp.arange(half_dim).astype(F32) * 2.0 / values.shape[-1])
    angle_table = position[:, None] * inverse[None, :]
    cosine = jnp.cos(angle_table)[:, None, :]
    sine = jnp.sin(angle_table)[:, None, :]
    lower = values[..., :half_dim]
    upper = values[..., half_dim:]
    return jnp.concatenate(
        [lower * cosine - upper * sine, upper * cosine + lower * sine], axis=-1
    )


def silu_pair(gate_part, up_part):
    return jax.nn.silu(gate_part) * up_part


def ring(axis, step):
    size = lax.axis_size(axis)
    return [(i, (i + step) % size) for i in range(size)]


def pick(parts, index):
    return lax.dynamic_index_in_dim(parts, index, 0, keepdims=False)


def plane_gather(block):
    return lax.all_gather(block, PLANE, axis=0, tiled=True)


def expert_gather(shard):
    ranks, rows, ffe = shard.shape
    sub = lax.axis_size("s")
    l, s = lax.axis_index("l"), lax.axis_index("s")
    whole = jnp.zeros((ranks, sub, rows, ffe), shard.dtype)

    def place(whole, block, at_l, at_s):
        return lax.dynamic_update_slice(whole, block[None, None], (at_l, at_s, 0, 0))

    for turn in range(ranks):
        block = pick(shard, (l + turn) % ranks)
        if turn:
            block = lax.ppermute(block, "l", ring("l", turn))
        from_l = (l - turn) % ranks
        whole = place(whole, block, from_l, s)
        for step in range(1, sub):
            whole = place(whole, lax.ppermute(block, "s", ring("s", step)), from_l, (s - step) % sub)
    return whole.reshape(-1, ffe)


def expert_scatter(partial, ranks):
    depth, ffe = partial.shape
    sub = lax.axis_size("s")
    l, s = lax.axis_index("l"), lax.axis_index("s")
    rows = depth // (ranks * sub)
    parts = partial.astype(BF16).reshape(ranks, sub, rows, ffe).transpose(1, 0, 2, 3)
    total = pick(parts, s).astype(F32)
    for step in range(1, sub):
        total = total + lax.ppermute(pick(parts, (s + step) % sub), "s", ring("s", step)).astype(F32)
    out = jnp.zeros((ranks, rows, ffe), F32)
    for turn in range(ranks):
        block = pick(total, (l + turn) % ranks)
        if turn:
            block = lax.ppermute(block.astype(BF16), "l", ring("l", turn)).astype(F32)
        out = lax.dynamic_update_slice(out, block[None], ((l - turn) % ranks, 0, 0))
    return out


def columns_gather(shard, groups):
    rows, wide = shard.shape
    parts = shard.reshape(rows, groups, wide // groups).transpose(1, 0, 2)
    mine = lax.all_to_all(parts, PLANE, split_axis=0, concat_axis=0, tiled=True)
    both = lax.all_gather(mine, "s", axis=1, tiled=False)
    return both.reshape(-1, wide // groups)


def columns_scatter(partial, groups, sub):
    depth, narrow = partial.shape
    rows = depth // (groups * sub)
    parts = partial.reshape(groups, sub, rows, narrow)
    mine = lax.psum_scatter(parts, "s", scatter_dimension=1, tiled=False)
    back = lax.all_to_all(mine, PLANE, split_axis=0, concat_axis=0, tiled=True)
    return back.transpose(1, 0, 2).reshape(rows, groups * narrow)


def shards(
    tokens,
    doc_ids,
    routes,
    gain_attn,
    w_query,
    w_key,
    w_value,
    w_out,
    gain_moe,
    w_router,
    shared_gate,
    shared_up,
    shared_down,
    expert_gate,
    expert_up,
    expert_down,
    cotangent,
):
    length, width = tokens.shape
    group_size = HEADS // KV_HEADS
    score_scale = HEAD_DIM ** (-0.5)
    local_experts = expert_gate.shape[0]
    sub = lax.axis_size("s")
    groups = lax.axis_size("a") * lax.axis_size("b") * lax.axis_size("l")
    experts_total = groups
    capacity = length * TOP * 4 // (3 * experts_total)
    sizes = tuple(lax.axis_size(axis) for axis in ALL)
    my_expert = lax.axis_index(PLANE)
    kvw = w_key.shape[1]
    qw = w_query.shape[1]

    small = jnp.concatenate(
        [w_router, gain_attn[:, None], gain_moe[:, None]], axis=1
    )
    small = jnp.pad(small, ((0, 0), (0, 128 - small.shape[1])))
    dense = gather(
        jnp.concatenate([w_query, w_key, w_value, w_out, small], axis=1), sizes, True, 1
    )
    query_full = dense[:, :qw]
    key_full = dense[:, qw : qw + kvw]
    value_full = dense[:, qw + kvw : qw + 2 * kvw]
    out_full = dense[:, qw + 2 * kvw : qw + 2 * kvw + width]
    rest = dense[:, qw + 2 * kvw + width :]
    router_full = rest[:, :experts_total]
    attn_gain = rest[:, experts_total].astype(F32)
    moe_gain = rest[:, experts_total + 1].astype(F32)

    dy_all = plane_gather(cotangent)
    routes_all = plane_gather(routes)
    wg, wu, wd = expert_gather(expert_gate), expert_gather(expert_up), expert_gather(expert_down)
    sg_w = columns_gather(shared_gate, groups)
    su_w = columns_gather(shared_up, groups)
    sd_w = lax.all_gather(shared_down, "s", axis=0, tiled=True)

    inputs = tokens.astype(F32)
    normed, attn_norm_pull = jax.vjp(rms_norm, inputs, attn_gain)
    normed_low = normed.astype(BF16)
    query_pre = dot(normed_low, query_full).reshape(length, HEADS, HEAD_DIM)
    key_pre = dot(normed_low, key_full).reshape(length, KV_HEADS, HEAD_DIM)
    value_low = dot(normed_low, value_full).astype(BF16).reshape(length, KV_HEADS, HEAD_DIM)
    query_rot, query_pull = jax.vjp(rotate, query_pre)
    key_rot, key_pull = jax.vjp(rotate, key_pre)
    query_low = query_rot.astype(BF16).reshape(length, KV_HEADS, group_size, HEAD_DIM)
    key_low = key_rot.astype(BF16)
    position = jnp.arange(length)
    doc_row = doc_ids[0]
    allowed = (position[None, :] <= position[:, None]) & (doc_row[None, :] == doc_row[:, None])
    scores = (
        jnp.einsum("tkgd,skd->kgts", query_low, key_low, preferred_element_type=F32) * score_scale
    )
    scores = jnp.where(allowed, scores, -1e30)
    exp_scores = jnp.exp(scores - jnp.max(scores, axis=-1, keepdims=True))
    attend = exp_scores / jnp.sum(exp_scores, axis=-1, keepdims=True)
    attend_low = attend.astype(BF16)
    mixed_low = (
        jnp.einsum("kgts,skd->tkgd", attend_low, value_low, preferred_element_type=F32)
        .reshape(length, HEADS * HEAD_DIM)
        .astype(BF16)
    )
    hidden = inputs + dot(mixed_low, out_full)
    normed_moe, moe_norm_pull = jax.vjp(rms_norm, hidden, moe_gain)
    moe_low = normed_moe.astype(BF16)

    x_all = gather(moe_low, sizes, False, 2)
    seqs = groups
    chosen_hot = jnp.any(
        routes_all[:, :, None] == jnp.arange(experts_total)[None, None, :], axis=1
    )
    logits = dot(x_all, router_full)
    logits = jnp.where(chosen_hot, logits, -1e30)
    gates = jax.nn.softmax(logits, axis=-1)
    mine = jnp.any(routes_all == my_expert, axis=1).reshape(seqs, length)
    my_gate = jnp.sum(
        jnp.where(jnp.arange(experts_total)[None, :] == my_expert, gates, 0.0), axis=1
    ).reshape(seqs, length)
    hits = mine.astype(jnp.int32)
    before = jnp.cumsum(hits, axis=1) - hits
    pick = (jnp.arange(capacity)[None, :, None] == before[:, None, :]) & mine[:, None, :]
    pick_low = pick.astype(BF16)
    slot_gate = jnp.sum(jnp.where(pick, my_gate[:, None, :], 0.0), axis=2)
    x_rows = jnp.einsum(
        "nst,ntd->nsd", pick_low, x_all.reshape(seqs, length, width), preferred_element_type=F32
    )
    x_rows = x_rows.astype(BF16).reshape(-1, width)
    dy_rows = jnp.einsum(
        "nst,ntd->nsd", pick_low, dy_all.reshape(seqs, length, width), preferred_element_type=F32
    ).reshape(-1, width)
    slot_gate = slot_gate.reshape(-1, 1)
    gate_rows = dot(x_rows, wg)
    up_rows = dot(x_rows, wu)
    inner, expert_pull = jax.vjp(silu_pair, gate_rows, up_rows)
    inner_low = inner.astype(BF16)
    produced = dot_nt(inner_low, wd)
    scaled = (slot_gate * produced).astype(BF16).reshape(seqs, capacity, width)
    share_g = dot(x_all, sg_w)
    share_u = dot(x_all, su_w)
    share, share_pull = jax.vjp(silu_pair, share_g, share_u)
    share_low = share.astype(BF16)
    part = (
        jnp.einsum("nst,nsd->ntd", pick_low, scaled, preferred_element_type=F32).reshape(-1, width)
        + dot(share_low, sd_w)
    ).astype(BF16)
    moe_out = scatter(part, sizes, False, 3)
    output = (hidden + moe_out).astype(BF16)

    slot_grad = jnp.sum(dy_rows * produced, axis=1).reshape(seqs, 1, capacity)
    gate_grad = jnp.sum(
        jnp.where(pick.transpose(0, 2, 1), slot_grad, 0.0), axis=2
    )
    gate_grad = lax.all_to_all(gate_grad, PLANE, split_axis=0, concat_axis=0, tiled=True)
    gp = (slot_gate * dy_rows).astype(BF16)
    d_inner = dot(gp, wd)
    dg, du = expert_pull(d_inner)
    dg = dg.astype(BF16)
    du = du.astype(BF16)
    d_share = dot_nt(dy_all, sd_w)
    dsg, dsu = share_pull(d_share)
    dsg = dsg.astype(BF16)
    dsu = dsu.astype(BF16)
    back_rows = (dot_nt(dg, wg) + dot_nt(du, wu)).astype(BF16).reshape(seqs, capacity, width)
    dx_part = (
        jnp.einsum("nst,nsd->ntd", pick_low, back_rows, preferred_element_type=F32).reshape(
            -1, width
        )
        + dot_nt(dsg, sg_w)
        + dot_nt(dsu, su_w)
    ).astype(BF16)
    dx = scatter(dx_part, sizes, False, 4)
    grad_expert_down = expert_scatter(dot_tn(gp, inner_low), local_experts)
    grad_expert_gate = expert_scatter(dot_tn(x_rows, dg), local_experts)
    grad_expert_up = expert_scatter(dot_tn(x_rows, du), local_experts)
    grad_shared_gate = columns_scatter(dot_tn(x_all, dsg), groups, sub)
    grad_shared_up = columns_scatter(dot_tn(x_all, dsu), groups, sub)
    grad_shared_down = lax.psum_scatter(
        dot_tn(share_low, dy_all), "s", scatter_dimension=0, tiled=True
    )

    own_hot = jnp.any(routes[:, :, None] == jnp.arange(experts_total)[None, None, :], axis=1)
    own_logits = jnp.where(own_hot, dot(moe_low, router_full), -1e30)
    own_gates = jax.nn.softmax(own_logits, axis=-1)
    grad_gate = gate_grad.reshape(experts_total, length).T
    grad_logits = own_gates * (
        grad_gate - jnp.sum(own_gates * grad_gate, axis=-1, keepdims=True)
    )
    grad_logits = grad_logits.astype(BF16)
    grad_router = dot_tn(moe_low, grad_logits)
    dx = dx + dot_nt(grad_logits, router_full)
    grad_hidden_norm, grad_gain_moe = moe_norm_pull(dx)
    grad_hidden = cotangent.astype(F32) + grad_hidden_norm

    grad_hidden_low = grad_hidden.astype(BF16)
    grad_out_proj = dot_tn(mixed_low, grad_hidden_low)
    grad_mixed = (
        dot_nt(grad_hidden_low, out_full)
        .astype(BF16)
        .reshape(length, KV_HEADS, group_size, HEAD_DIM)
    )
    grad_value = jnp.einsum("kgts,tkgd->skd", attend_low, grad_mixed, preferred_element_type=F32)
    grad_attend = jnp.einsum("tkgd,skd->kgts", grad_mixed, value_low, preferred_element_type=F32)
    grad_scores = (
        attend * (grad_attend - jnp.sum(grad_attend * attend, axis=-1, keepdims=True))
    ).astype(BF16)
    grad_query = (
        jnp.einsum("kgts,skd->tkgd", grad_scores, key_low, preferred_element_type=F32) * score_scale
    )
    grad_key = (
        jnp.einsum("kgts,tkgd->skd", grad_scores, query_low, preferred_element_type=F32)
        * score_scale
    )
    grad_query_low = (
        query_pull(grad_query.reshape(length, HEADS, HEAD_DIM))[0].reshape(length, -1).astype(BF16)
    )
    grad_key_low = key_pull(grad_key)[0].reshape(length, -1).astype(BF16)
    grad_value_low = grad_value.reshape(length, -1).astype(BF16)
    grad_normed = (
        dot_nt(grad_query_low, query_full)
        + dot_nt(grad_key_low, key_full)
        + dot_nt(grad_value_low, value_full)
    )
    grad_inputs_norm, grad_gain_attn = attn_norm_pull(grad_normed)
    grad_tokens = grad_hidden + grad_inputs_norm
    grad_small = jnp.concatenate(
        [grad_router, grad_gain_attn[:, None], grad_gain_moe[:, None]], axis=1
    )
    grad_small = jnp.pad(grad_small, ((0, 0), (0, 128 - grad_small.shape[1])))
    dense_grads = jnp.concatenate(
        [
            dot_tn(normed_low, grad_query_low).astype(BF16),
            dot_tn(normed_low, grad_key_low).astype(BF16),
            dot_tn(normed_low, grad_value_low).astype(BF16),
            grad_out_proj.astype(BF16),
            grad_small.astype(BF16),
        ],
        axis=1,
    )
    total = scatter(dense_grads, sizes, True, 5)
    dense_sum, small_sum = total[:, :-128], total[:, -128:]
    return (
        output,
        grad_tokens,
        small_sum[:, experts_total],
        dense_sum[:, :qw],
        dense_sum[:, qw : qw + kvw],
        dense_sum[:, qw + kvw : qw + 2 * kvw],
        dense_sum[:, qw + 2 * kvw :],
        small_sum[:, experts_total + 1],
        small_sum[:, :experts_total],
        grad_shared_gate,
        grad_shared_up,
        grad_shared_down,
        grad_expert_gate,
        grad_expert_up,
        grad_expert_down,
    )


def solution(mesh):
    ranks, shards_of = mesh.shape["expert"], mesh.shape["dp"]
    local_experts = 2
    split = Mesh(
        mesh.devices.reshape(4, ranks // 4, local_experts, shards_of // local_experts), ALL
    )
    rows = P(ALL, None)
    flat = P(ALL)
    expert = P(("a", "b"), ("l", "s"), None)
    return jax.shard_map(
        shards,
        mesh=split,
        in_specs=(rows,) * 3
        + (flat,)
        + (rows,) * 4
        + (flat,)
        + (rows,) * 4
        + (expert,) * 3
        + (rows,),
        out_specs=(rows,) * 2
        + (flat,)
        + (rows,) * 4
        + (flat,)
        + (rows,) * 4
        + (expert,) * 3,
        check_vma=False,
    )
```

time: 3030 us -> 1210 us (0.40)
  waiting for transfers between devices: 2240 us -> 74.3 us
  Pallas kernels: 0 us -> 565 us
  blocking collectives: 363 us -> 50.4 us
  local copies, waits for them, and re-layouts: 91.4 us -> 146 us
    reduce_scatter x10 -> x1, waiting for transfers between devices: 1770 us -> 0.01 us  [shards(): lax.psum_scatter(dot_tn(share_low, dy_all), 's', scatter_dimension=0, til...]
    pallas_call x0 -> x5, Pallas kernels: none -> 565 us  [the longest x3 286 us: scatter(): pl.pallas_call(functools.partial(scatter_kernel, sizes, siblings), out_sh...]
    all_gather x10 -> x1, waiting for transfers between devices: 366 us -> 0.01 us  [plane_gather(): return lax.all_gather(block, PLANE, axis=0, tiled=True)]
    all_to_all x1 -> x0, blocking collectives: 173 us -> none  [shards(): lax.all_to_all(grad_rows.reshape(expert_ranks, local_experts, capacity, w...]
    unnamed x2 -> x0, blocking collectives: 80.2 us -> none
    all_gather x1 -> x4, blocking collectives: 109 us -> 50.4 us  [the longest x1 42.6 us: plane_gather(): return lax.all_gather(block, PLANE, axis=0, tiled=True)]
    all_to_all x3 -> x5, waiting for transfers between devices: 99.7 us -> 52.9 us  [the longest x2 49.3 us: columns_scatter(): back = lax.all_to_all(mine, PLANE, split_axis=0, concat_axis=0, tiled=True)]
    dot_general x36 -> x39, matrix products: 258 us -> 262 us  [the longest x11 86.2 us: dot_nt(): lax.dot_general(left, right, (((1,), (1,)), ((), ())), preferred_element_...]
  transfers between devices with their start and end apart: 24 -> 23, of which waited for: 19 -> 4; matrix products, arithmetic and copies ran while one was open for 12% -> 31% of each run, Pallas kernels for 0% -> 47%
where the time goes in v1:
time: 1210 us; the launch traced here: 1200 us
  Pallas kernels  565 us (47%)
  matrix products  270 us (22%)
  local copies, waits for them, and re-layouts  146 us (12%)
  waiting for transfers between devices  74.3 us (6%)
  blocking collectives  50.4 us (4%)
  starting transfers between devices  44.6 us (4%)
  other arithmetic  34.7 us (3%)
  between operations  15.6 us (1%)
    pallas_call x3, Pallas kernels, scatter(): pl.pallas_call(functools.partial(scatter_kernel, sizes, siblings), out_sh...  286 us
    pallas_call x2, Pallas kernels, gather(): pl.pallas_call(functools.partial(gather_kernel, sizes, siblings), out_sha...  278 us
    dot_general x11, matrix products, dot_nt(): lax.dot_general(left, right, (((1,), (1,)), ((), ())), preferred_element_...  86.2 us
    dot_general x12, matrix products, dot(): return jnp.dot(left, right, preferred_element_type=F32)  85.7 us
    dot_general x11, matrix products, dot_tn(): lax.dot_general(left, right, (((0,), (0,)), ((), ())), preferred_element_...  57.1 us
    all_to_all x2, waiting for transfers between devices, columns_scatter(): back = lax.all_to_all(mine, PLANE, split_axis=0, concat_axis=0, tiled=True)  49.3 us
    all_gather x1, blocking collectives, plane_gather(): return lax.all_gather(block, PLANE, axis=0, tiled=True)  42.6 us
    concatenate x1, local copies, waits for them, and re-layouts, shards(): jnp.concatenate([dot_tn(normed_low, grad_query_low).astype(BF16), dot_tn(...  26.4 us
  transfers between devices with their start and end apart: 23, of which 4 were waited for; matrix products, arithmetic and copies ran while one was open for 31% of the time, Pallas kernels for 47%

profile of v1, /device:TPU:0, one launch (start us, length us, event | category | flops | bytes accessed | tf_op | source)
XLA Modules:
  0.0 1200.7 jit_solution(5910371798102218390)
XLA Ops:
  38.4 212.8 %shard_map.280 = bf16[4,2,2,2,64,5248]{5,4,3,2,1,0:T(8,128)(2,1)} custom-call(bf16[64,5248]{1,0:T(8,128)(2,1)} %constant_dynamic-update-slice_fusion.x_ref), custom_call_target="tpu_custom_call" | custom-call | bytes 42991616 | tf_op jit(solution)/shard_map/pallas_call | solution.py:249
  264.1 42.6 %all_gather.21 = s32[2048,6]{0,1:T(8,128)S(1)} all-gather(s32[128,6]{0,1:T(8,128)S(1)} %copy-done.51), channel_id=1, replica_groups=mesh['a'=4,'b'=2,'l'=2,'s'=2] {'a','b','l'}, dimensions={0}, use_global_device_ids=true | all-gather | bytes 52224 | tf_op jit(solution)/shard_map/all_gather | solution.py:522
  332.9 65.7 %shard_map.281 = bf16[4,2,2,1,128,2048]{5,4,3,2,1,0:T(8,128)(2,1)} custom-call(bf16[128,2048]{1,0:T(8,128)(2,1)} %multiply_convert_fusion.7.x_ref), custom_call_target="tpu_custom_call" | custom-call | bytes 16777216 | tf_op jit(solution)/shard_map/pallas_call | solution.py:249
  415.0 12.3 %copy.196 = bf16[2048,2048]{1,0:T(8,128)(2,1)} copy(bf16[2048,2048]{0,1:T(8,128)(2,1)} %bitcast.295) | data formatting | bytes 16777216 | tf_op jit(solution)/shard_map/dot_general | solution.py:30
  505.5 10.9 fusion.140
  516.4 15.6 %fusion.16 = (bf16[1024,1408]{1,0:T(8,128)(2,1)}, bf16[1024,1408]{1,0:T(8,128)(2,1)}, bf16[1024,1408]{1,0:T(8,128)(2,1)}) fusion(f32[1024,1408]{1,0:T(8,128)} %fusion.140, f32[1024,1408]{1,0:T(8,128)} %fusion.139, bf16[1024,2048]{1,0:T(8,128)(2,1)S(1)} %bitcast.326, bf16[2048,1408]{1,0:T(8,128)(2,1)} %bitcast.25), kind=kOutput, calls=%fused_computation.29 | convolution fusion | flops 5928648704 | bytes 30146560 | tf_op jit(solution)/shard_map/dot_general | solution.py:26
  532.0 10.4 fusion.141
  542.4 8.6 convolution_convert_fusion.1
  551.0 11.7 fusion.5
  562.7 8.6 convolution_convert_fusion
  576.5 9.8 convolution_convert_fusion.2
  586.4 14.5 %add_convert_fusion = bf16[1024,2048]{1,0:T(8,128)(2,1)} fusion(f32[1024,2048]{1,0:T(8,128)} %fusion.141, bf16[1024,1408]{1,0:T(8,128)(2,1)S(1)} %copy-done.76, bf16[2048,1408]{1,0:T(8,128)(2,1)} %bitcast.25), kind=kOutput, calls=%fused_computation.13 | convolution fusion | flops 5909774336 | bytes 21233664 | tf_op jit(solution)/shard_map/dot_general | solution.py:34
  619.5 10.5 fusion.85
  629.9 8.5 fusion.89
  638.6 12.3 %fusion.3 = bf16[2048,2048]{1,0:T(8,128)(2,1)} fusion(f32[16,128,2048]{2,1,0:T(8,128)} %fusion.89, bf16[2048,176]{0,1:T(8,128)(2,1)S(1)} %get-tuple-element.108, bf16[176,2048]{1,0:T(8,128)(2,1)S(1)} %copy-done.22), kind=kOutput, calls=%fused_computation.5 | convolution fusion | flops 1484783616 | bytes 26607616 | tf_op jit(solution)/shard_map/dot_general | solution.py:26
  659.0 17.4 %fusion.2 = bf16[2048,2048]{1,0:T(8,128)(2,1)} fusion(f32[2048,2048]{1,0:T(8,128)} %fusion.67, f32[16,128,2048]{2,1,0:T(8,128)} %fusion.85, bf16[2048,176]{0,1:T(8,128)(2,1)S(1)} %get-tuple-element.106, bf16[22,8,16,128]{3,2,1,0:T(8,128)(2,1)S(1)} %bitcast.356), kind=kOutput, calls=%fused_computation.3 | convolution fusion | flops 1488977920 | bytes 43384832 | tf_op jit(solution)/shard_map/dot_general | solution.py:34
  682.6 82.6 %shard_map.282 = f32[128,2048]{1,0:T(8,128)} custom-call(bf16[4,2,2,1,128,2048]{5,4,3,2,1,0:T(8,128)(2,1)} %bitcast.312), custom_call_target="tpu_custom_call" | custom-call | bytes 16777216 | tf_op jit(solution)/shard_map/pallas_call | solution.py:463
  765.3 85.0 %shard_map.283 = f32[128,2048]{1,0:T(8,128)} custom-call(bf16[4,2,2,1,128,2048]{5,4,3,2,1,0:T(8,128)(2,1)} %bitcast.313), custom_call_target="tpu_custom_call" | custom-call | bytes 16777216 | tf_op jit(solution)/shard_map/pallas_call | solution.py:463
  903.2 26.4 %copy.195 = bf16[2048,5248]{1,0:T(8,128)(2,1)} copy(bf16[2048,5248]{0,1:T(8,128)(2,1)} %fusion.81) | data formatting | bytes 42991616 | tf_op jit(solution)/shard_map/concatenate | solution.py:786
  929.7 118.8 %shard_map.284 = f32[64,5248]{1,0:T(8,128)} custom-call(bf16[4,2,2,2,64,5248]{5,4,3,2,1,0:T(8,128)(2,1)} %bitcast.299), custom_call_target="tpu_custom_call" | custom-call | bytes 42991616 | tf_op jit(solution)/shard_map/pallas_call | solution.py:463
  1059.6 11.1 all-to-all-start.4
  1085.7 9.2 all-to-all-done.4
  1120.5 40.0 %all-to-all-done.3 = f32[16,64,176]{2,1,0:T(8,128)} async-done(((f32[16,64,176]{2,1,0:T(8,128)}), f32[16,64,176]{2,1,0:T(8,128)}, u32[]{:S(2)}, u32[]{:S(2)}) %all-to-all-start.3) | async-done | bytes 720928 | tf_op jit(solution)/shard_map/all_to_all | solution.py:576
  1170.0 20.6 %collective-permute-done.10 = bf16[512,1408]{1,0:T(8,128)(2,1)} collective-permute-done((bf16[512,1408]{1,0:T(8,128)(2,1)}, bf16[512,1408]{1,0:T(8,128)(2,1)}, u32[]{:S(2)}, u32[]{:S(2)}) %collective-permute-start.10) | collective-permute-done | bytes 1441824 | tf_op jit(solution)/shard_map/ppermute | solution.py:558
  (394 shorter events, 319.2 us)
Async XLA Ops:
  7.2 493.6 %all-gather.4.cloned.1.call-start = ((), (), s32[]{:S(2)}) async-start(), calls=%async_computation.6 | async-start | bytes 8912896 | tf_op jit(solution)/shard_map/all_gather | solution.py:522
  11.0 425.7 %all-to-all-start = ((bf16[16,64,176]{2,1,0:T(8,128)(2,1)}), bf16[16,64,176]{2,1,0:T(8,128)(2,1)}, u32[]{:S(2)}, u32[]{:S(2)}) async-start(bf16[16,64,176]{2,1,0:T(8,128)(2,1)} %copy.176), calls=%async_computation | async-start | bytes 1048576 | tf_op jit(solution)/shard_map/all_to_all | solution.py:566
  23.2 452.1 %collective-permute-start.1 = (bf16[512,1408]{1,0:T(8,128)(2,1)}, bf16[512,1408]{1,0:T(8,128)(2,1)}, u32[]{:S(2)}, u32[]{:S(2)}) collective-permute-start(bf16[512,1408]{1,0:T(8,128)(2,1)} %get-tuple-element.111), channel_id=1, source_target_pairs={{0,2},{2,0},{1,3},{3,1},{4,6},{6,4},{5,7},{7,5},{8,10},{10,8},{9,1... | collective-permute-start | bytes 4325384 | tf_op jit(solution)/shard_map/ppermute | solution.py:537
  26.9 448.6 %collective-permute-start.4 = (bf16[512,1408]{1,0:T(8,128)(2,1)}, bf16[512,1408]{1,0:T(8,128)(2,1)}, u32[]{:S(2)}, u32[]{:S(2)}) collective-permute-start(bf16[512,1408]{1,0:T(8,128)(2,1)} %get-tuple-element.113), channel_id=1, source_target_pairs={{0,2},{2,0},{1,3},{3,1},{4,6},{6,4},{5,7},{7,5},{8,10},{10,8},{9,1... | collective-permute-start | bytes 4325384 | tf_op jit(solution)/shard_map/ppermute | solution.py:537
  27.1 448.8 %collective-permute-start.3 = (bf16[512,1408]{1,0:T(8,128)(2,1)}, bf16[512,1408]{1,0:T(8,128)(2,1)}, u32[]{:S(2)}, u32[]{:S(2)}) collective-permute-start(bf16[512,1408]{1,0:T(8,128)(2,1)} %get-tuple-element.114), channel_id=1, source_target_pairs={{0,1},{1,0},{2,3},{3,2},{4,5},{5,4},{6,7},{7,6},{8,9},{9,8},{10,11... | collective-permute-start | bytes 4325384 | tf_op jit(solution)/shard_map/ppermute | solution.py:541
  28.9 447.1 %collective-permute-start.7 = (bf16[512,1408]{1,0:T(8,128)(2,1)}, bf16[512,1408]{1,0:T(8,128)(2,1)}, u32[]{:S(2)}, u32[]{:S(2)}) collective-permute-start(bf16[512,1408]{1,0:T(8,128)(2,1)} %get-tuple-element.109), channel_id=1, source_target_pairs={{0,2},{2,0},{1,3},{3,1},{4,6},{6,4},{5,7},{7,5},{8,10},{10,8},{9,1... | collective-permute-start | bytes 4325384 | tf_op jit(solution)/shard_map/ppermute | solution.py:537
  30.8 448.8 %collective-permute-start.6 = (bf16[512,1408]{1,0:T(8,128)(2,1)}, bf16[512,1408]{1,0:T(8,128)(2,1)}, u32[]{:S(2)}, u32[]{:S(2)}) collective-permute-start(bf16[512,1408]{1,0:T(8,128)(2,1)} %get-tuple-element.110), channel_id=1, source_target_pairs={{0,1},{1,0},{2,3},{3,2},{4,5},{5,4},{6,7},{7,6},{8,9},{9,8},{10,11... | collective-permute-start | bytes 4325384 | tf_op jit(solution)/shard_map/ppermute | solution.py:541
  38.4 217.3 %copy-start.55 = (f32[128]{0:T(128)S(1)}, f32[128]{0:T(128)}, u32[]{:S(2)}) copy-start(f32[128]{0:T(128)} %fusion.117) | copy-start | bytes 1540
  436.7 19.0 %all-to-all-start.1 = ((bf16[16,64,176]{2,1,0:T(8,128)(2,1)}), bf16[16,64,176]{2,1,0:T(8,128)(2,1)S(1)}, u32[]{:S(2)}, u32[]{:S(2)}) async-start(bf16[16,64,176]{2,1,0:T(8,128)(2,1)} %copy.179), calls=%async_computation.1 | async-start | bytes 1048576 | tf_op jit(solution)/shard_map/all_to_all | solution.py:566
  475.4 9.3 collective-permute-start
  475.5 14.9 %collective-permute-start.2 = (bf16[512,1408]{1,0:T(8,128)(2,1)}, bf16[512,1408]{1,0:T(8,128)(2,1)S(1)}, u32[]{:S(2)}, u32[]{:S(2)}) collective-permute-start(bf16[512,1408]{1,0:T(8,128)(2,1)} %collective-permute-done.1), channel_id=1, source_target_pairs={{0,1},{1,0},{2,3},{3,2},{4,5},{5,4},{6,7},{7,6},{8,9},{9,8},{10,11... | collective-permute-start | bytes 4325384 | tf_op jit(solution)/shard_map/ppermute | solution.py:541
  475.9 12.9 %collective-permute-start.5 = (bf16[512,1408]{1,0:T(8,128)(2,1)}, bf16[512,1408]{1,0:T(8,128)(2,1)S(1)}, u32[]{:S(2)}, u32[]{:S(2)}) collective-permute-start(bf16[512,1408]{1,0:T(8,128)(2,1)} %collective-permute-done.4), channel_id=1, source_target_pairs={{0,1},{1,0},{2,3},{3,2},{4,5},{5,4},{6,7},{7,6},{8,9},{9,8},{10,11... | collective-permute-start | bytes 4325384 | tf_op jit(solution)/shard_map/ppermute | solution.py:541
  476.0 13.0 %collective-permute-start.8 = (bf16[512,1408]{1,0:T(8,128)(2,1)}, bf16[512,1408]{1,0:T(8,128)(2,1)S(1)}, u32[]{:S(2)}, u32[]{:S(2)}) collective-permute-start(bf16[512,1408]{1,0:T(8,128)(2,1)} %collective-permute-done.7), channel_id=1, source_target_pairs={{0,1},{1,0},{2,3},{3,2},{4,5},{5,4},{6,7},{7,6},{8,9},{9,8},{10,11... | collective-permute-start | bytes 4325384 | tf_op jit(solution)/shard_map/ppermute | solution.py:541
  572.2 278.1 %all-to-all-start.2 = ((f32[16,1,128]{2,1,0:T(1,128)}), f32[16,1,128]{2,1,0:T(1,128)S(1)}, u32[]{:S(2)}, u32[]{:S(2)}) async-start(f32[16,1,128]{2,1,0:T(1,128)} %bitcast.52), calls=%async_computation.2 | async-start | bytes 16384 | tf_op jit(solution)/shard_map/all_to_all | solution.py:710
  576.4 480.3 %all-reduce.11.cloned.1.call-start = ((), (), s32[]{:S(2)}) async-start(), calls=%async_computation.8 | async-start | bytes 8388608
  606.5 464.3 %collective-permute-start.13 = (bf16[2,512,1408]{2,1,0:T(8,128)(2,1)}, bf16[2,512,1408]{2,1,0:T(8,128)(2,1)}, u32[]{:S(2)}, u32[]{:S(2)}) collective-permute-start(bf16[2,512,1408]{2,1,0:T(8,128)(2,1)} %dynamic-slice_bitcast_fusion), channel_id=1, source_target_pairs={{0,1},{1,0},{2,3},{3,2},{4,5},{5,4},{6,7},{7,6},{8,9},{9,8},{10,11... | collective-permute-start | bytes 8650760 | tf_op jit(solution)/shard_map/ppermute | solution.py:553
  606.5 471.0 %collective-permute-start.11 = (bf16[2,512,1408]{2,1,0:T(8,128)(2,1)}, bf16[2,512,1408]{2,1,0:T(8,128)(2,1)}, u32[]{:S(2)}, u32[]{:S(2)}) collective-permute-start(bf16[2,512,1408]{2,1,0:T(8,128)(2,1)} %dynamic-slice_bitcast_fusion.1), channel_id=1, source_target_pairs={{0,1},{1,0},{2,3},{3,2},{4,5},{5,4},{6,7},{7,6},{8,9},{9,8},{10,11... | collective-permute-start | bytes 8650760 | tf_op jit(solution)/shard_map/ppermute | solution.py:553
  607.0 494.4 %collective-permute-start.9 = (bf16[2,512,1408]{2,1,0:T(8,128)(2,1)}, bf16[2,512,1408]{2,1,0:T(8,128)(2,1)}, u32[]{:S(2)}, u32[]{:S(2)}) collective-permute-start(bf16[2,512,1408]{2,1,0:T(8,128)(2,1)} %dynamic-slice_bitcast_fusion.2), channel_id=1, source_target_pairs={{0,1},{1,0},{2,3},{3,2},{4,5},{5,4},{6,7},{7,6},{8,9},{9,8},{10,11... | collective-permute-start | bytes 8650760 | tf_op jit(solution)/shard_map/ppermute | solution.py:553
  638.5 555.2 %reduce-scatter.4.cloned.1.call-start = ((), (), s32[]{:S(2)}) async-start(), calls=%async_computation.7 | async-start | bytes 2162688 | tf_op jit(solution)/shard_map/reduce_scatter | solution.py:734
  1059.6 35.3 %all-to-all-start.4 = ((f32[16,64,176]{2,1,0:T(8,128)}), f32[16,64,176]{2,1,0:T(8,128)S(1)}, u32[]{:S(2)}, u32[]{:S(2)}) async-start(f32[16,64,176]{2,1,0:T(8,128)} %dynamic-slice_bitcast_fusion.9), calls=%async_computation.4 | async-start | bytes 2097152 | tf_op jit(solution)/shard_map/all_to_all | solution.py:576
  1075.6 88.2 %collective-permute-start.14 = (bf16[512,1408]{1,0:T(8,128)(2,1)}, bf16[512,1408]{1,0:T(8,128)(2,1)}, u32[]{:S(2)}, u32[]{:S(2)}) collective-permute-start(bf16[512,1408]{1,0:T(8,128)(2,1)} %fusion.38), channel_id=1, source_target_pairs={{0,2},{2,0},{1,3},{3,1},{4,6},{6,4},{5,7},{7,5},{8,10},{10,8},{9,1... | collective-permute-start | bytes 4325384 | tf_op jit(solution)/shard_map/ppermute | solution.py:558
  1082.9 84.0 %collective-permute-start.12 = (bf16[512,1408]{1,0:T(8,128)(2,1)}, bf16[512,1408]{1,0:T(8,128)(2,1)}, u32[]{:S(2)}, u32[]{:S(2)}) collective-permute-start(bf16[512,1408]{1,0:T(8,128)(2,1)} %fusion.37), channel_id=1, source_target_pairs={{0,2},{2,0},{1,3},{3,1},{4,6},{6,4},{5,7},{7,5},{8,10},{10,8},{9,1... | collective-permute-start | bytes 4325384 | tf_op jit(solution)/shard_map/ppermute | solution.py:558
  1094.9 65.5 %all-to-all-start.3 = ((f32[16,64,176]{2,1,0:T(8,128)}), f32[16,64,176]{2,1,0:T(8,128)}, u32[]{:S(2)}, u32[]{:S(2)}) async-start(f32[16,64,176]{2,1,0:T(8,128)} %dynamic-slice_bitcast_fusion.10), calls=%async_computation.3 | async-start | bytes 2097152 | tf_op jit(solution)/shard_map/all_to_all | solution.py:576
  1106.1 84.5 %collective-permute-start.10 = (bf16[512,1408]{1,0:T(8,128)(2,1)}, bf16[512,1408]{1,0:T(8,128)(2,1)}, u32[]{:S(2)}, u32[]{:S(2)}) collective-permute-start(bf16[512,1408]{1,0:T(8,128)(2,1)} %fusion.36), channel_id=1, source_target_pairs={{0,2},{2,0},{1,3},{3,1},{4,6},{6,4},{5,7},{7,5},{8,10},{10,8},{9,1... | collective-permute-start | bytes 4325384 | tf_op jit(solution)/shard_map/ppermute | solution.py:558
  (94 other events, 1680.7 us)
Sparse Core Ops, SparseCore 0:
  10.7 164.2 all-gather.3
  638.6 29.8 all-reduce.10
  850.4 11.7 reduce-scatter.3

commit v2 on v1

v2 whole, which is shorter than its diff:
```python
import functools

import jax
import jax.numpy as jnp
from jax import lax
from jax.experimental import pallas as pl
from jax.experimental.pallas import tpu as pltpu
from jax.sharding import Mesh
from jax.sharding import PartitionSpec as P

HEADS = 16
KV_HEADS = 4
HEAD_DIM = 128
TOP = 6
EPS = 1e-06
ROPE_BASE = 10000.0
PLANE = ("a", "b", "l")
ALL = ("a", "b", "l", "s")
F32 = jnp.float32
BF16 = jnp.bfloat16
MESH = pl.DeviceIdType.MESH
VMEM_LIMIT = 60 * 1024 * 1024
DMA = pltpu.SemaphoreType.DMA
ANY = pl.BlockSpec(memory_space=pl.ANY)
VMEM = pl.BlockSpec(memory_space=pltpu.VMEM)


def dot(left, right):
    return jnp.dot(left, right, preferred_element_type=F32)


def dot_tn(left, right):
    return lax.dot_general(left, right, (((0,), (0,)), ((), ())), preferred_element_type=F32)


def dot_nt(left, right):
    return lax.dot_general(left, right, (((1,), (1,)), ((), ())), preferred_element_type=F32)


class Grid:
    def __init__(self, sizes):
        self.na, self.nb, self.nl, self.ns = self.sizes = sizes
        self.a, self.b, self.l, self.s = (lax.axis_index(axis) for axis in "abls")
        self.is_up = self.a < self.na - 1
        self.is_down = self.a > 0

    def at(self, a=None, b=None, l=None, s=None):
        return tuple(
            own if other is None else other
            for own, other in zip((self.a, self.b, self.l, self.s), (a, b, l, s))
        )

    def other(self, axis, step):
        size, own = {"b": (self.nb, self.b), "l": (self.nl, self.l), "s": (self.ns, self.s)}[axis]
        return lax.rem(own + step, size)

    def to(self, axis, step):
        return self.at(**{axis: self.other(axis, step)})

    def hello(self, device):
        pl.semaphore_signal(
            pltpu.get_barrier_semaphore(), inc=1, device_id=device, device_id_type=MESH
        )

    def greet_neighbours(self, siblings):
        @pl.when(self.is_down)
        def _():
            self.hello(self.at(a=self.a - 1))

        @pl.when(self.is_up)
        def _():
            self.hello(self.at(a=self.a + 1))

        count = 0
        for axis, size in (("b", self.nb), ("l", self.nl), ("s", self.ns if siblings else 1)):
            for step in range(1, size):
                self.hello(self.to(axis, step))
                count += 1
        above = 1 - (self.a + 1) // self.na
        below = (self.a + self.na - 1) // self.na
        pl.semaphore_wait(pltpu.get_barrier_semaphore(), count + above + below)

    def greet_plane(self, siblings):
        count = 0
        for index in self.plane_steps():
            self.hello(self.plane_at(index))
            count += 1
        for step in range(1, self.ns if siblings else 1):
            self.hello(self.to("s", step))
            count += 1
        pl.semaphore_wait(pltpu.get_barrier_semaphore(), count)

    def plane_steps(self):
        return [
            (i, j, k)
            for i in range(self.na)
            for j in range(self.nb)
            for k in range(self.nl)
            if i + j + k
        ]

    def plane_at(self, steps, sign=1):
        return self.at(
            a=lax.rem(self.a + sign * steps[0] + self.na, self.na),
            b=lax.rem(self.b + sign * steps[1] + self.nb, self.nb),
            l=lax.rem(self.l + sign * steps[2] + self.nl, self.nl),
        )


def remote(src, dst, sems, device):
    return pltpu.make_async_remote_copy(
        src_ref=src, dst_ref=dst, send_sem=sems[0], recv_sem=sems[1], device_id=device, device_id_type=MESH
    )


def came(g, sem, dst):
    remote(dst, dst, (sem, sem), g.at()).wait_recv()


def left(g, sem, src):
    remote(src, src, (sem, sem), g.at()).wait_send()


def split_of(wide):
    return (wide * 5 // 7) // 128 * 128


def gather_sems(sizes, siblings):
    na, nb, nl, ns = sizes
    return [
        DMA((2, 2, na)),
        DMA((2, 2, na)),
        DMA((2, nb - 1, na)),
        DMA((2, nl - 1, na)),
        DMA((2, nl - 1, nb - 1, na)),
        DMA((2, nb - 1, nl - 1)),
        DMA((2, ns, na)) if siblings else DMA((2, 1, 1)),
        DMA((1,)),
    ]


def gathering(g, siblings, x_ref, o_ref, sems):
    la_sem, lb_sem, b_sem, l_sem, lb2_sem, bl2_sem, s_sem, own_sem = sems
    na, nb, nl, ns = g.sizes
    wide = x_ref.shape[-1]
    cut = split_of(wide)
    head, tail = pl.ds(0, cut), pl.ds(cut, wide - cut)
    me = g.s if siblings else 0

    def slot(a, b, l):
        return o_ref.at[a, b, l, me]

    def square(a):
        return o_ref.at[a, :, :, me]

    def pair(sem, *index):
        return sem.at[(0, *index)], sem.at[(1, *index)]

    def cols(origin):
        return (slice(None), head)

    def line_head(way, origin, first=False):
        src = x_ref.at[:, head] if first else slot(origin, g.b, g.l).at[:, head]
        return remote(src, slot(origin, g.b, g.l).at[:, head], pair(la_sem, way, origin), g.at(a=g.a + 1 - 2 * way))

    def line_tail(way, origin):
        block = o_ref.at[origin, :, :, me, :, tail]
        return remote(block, block, pair(lb_sem, way, origin), g.at(a=g.a + 1 - 2 * way))

    def spread(origin, first=False):
        for step in range(1, nl):
            if first:
                remote(x_ref, slot(origin, g.b, g.l), pair(l_sem, step - 1, origin), g.to("l", step)).start()
            else:
                part = slot(origin, g.b, g.l).at[:, head]
                remote(part, part, pair(l_sem, step - 1, origin), g.to("l", step)).start()
        for step in range(1, nb):
            if first:
                remote(x_ref, slot(origin, g.b, g.l), pair(b_sem, step - 1, origin), g.to("b", step)).start()
            else:
                part = slot(origin, g.b, g.l).at[:, head]
                remote(part, part, pair(b_sem, step - 1, origin), g.to("b", step)).start()

    def l_came(step, origin, first=False):
        l_from = g.other("l", nl - step)
        ref = slot(origin, g.b, l_from)
        came(g, l_sem.at[1, step - 1, origin], ref if first else ref.at[:, head])
        return l_from

    def b_came(step, origin, first=False):
        b_from = g.other("b", nb - step)
        ref = slot(origin, b_from, g.l)
        came(g, b_sem.at[1, step - 1, origin], ref if first else ref.at[:, head])
        return b_from

    def relay_head(origin, first=False):
        for step in range(1, nl):
            l_from = l_came(step, origin, first)
            part = slot(origin, g.b, l_from).at[:, head]
            for turn in range(1, nb):
                remote(part, part, pair(lb2_sem, step - 1, turn - 1, origin), g.to("b", turn)).start()

    def relay_tail():
        for step in range(1, nb):
            b_from = b_came(step, g.a, True)
            part = slot(g.a, b_from, g.l).at[:, tail]
            for turn in range(1, nl):
                remote(part, part, pair(bl2_sem, step - 1, turn - 1), g.to("l", turn)).start()

    def diagonal_head(origin):
        for step in range(1, nl):
            for turn in range(1, nb):
                ref = slot(origin, g.other("b", nb - turn), g.other("l", nl - step))
                came(g, lb2_sem.at[1, step - 1, turn - 1, origin], ref.at[:, head])

    def diagonal_tail():
        for step in range(1, nb):
            for turn in range(1, nl):
                ref = slot(g.a, g.other("b", nb - step), g.other("l", nl - turn))
                came(g, bl2_sem.at[1, step - 1, turn - 1], ref.at[:, tail])

    def siblings_send(origin):
        if siblings:
            for step in range(1, ns):
                remote(square(origin), square(origin), pair(s_sem, step - 1, origin), g.to("s", step)).start()

    def when_up_origin(k, act):
        @pl.when(g.a - k >= 0)
        def _():
            act(0, g.a - k)

    def when_down_origin(k, act):
        @pl.when(g.a + k < na)
        def _():
            act(1, g.a + k)

    def both(k, act):
        when_up_origin(k, act)
        when_down_origin(k, act)

    def onward(way, copy):
        @pl.when(g.is_up if way == 0 else g.is_down)
        def _():
            copy.start()

    def head_arrives(way, origin):
        came(g, la_sem.at[1, way, origin], slot(origin, g.b, g.l).at[:, head])
        onward(way, line_head(way, origin))
        spread(origin)

    def tail_arrives(way, origin):
        came(g, lb_sem.at[1, way, origin], o_ref.at[origin, :, :, me, :, tail])
        onward(way, line_tail(way, origin))

    own = pltpu.make_async_copy(x_ref, slot(g.a, g.b, g.l), own_sem.at[0])
    own.start()
    onward(0, line_head(0, g.a, True))
    onward(1, line_head(1, g.a, True))
    spread(g.a, True)
    yield
    relay_head(g.a, True)
    relay_tail()
    yield
    both(1, head_arrives)
    diagonal_tail()
    own.wait()
    onward(0, line_tail(0, g.a))
    onward(1, line_tail(1, g.a))
    yield
    for k in range(1, na):
        both(k, lambda way, origin: relay_head(origin))
        if k + 1 < na:
            both(k + 1, head_arrives)
        both(k, tail_arrives)
        if k == 1:
            diagonal_head(g.a)
            siblings_send(g.a)
        yield

    def complete(way, origin):
        for step in range(1, nb):
            b_came(step, origin)
        diagonal_head(origin)
        siblings_send(origin)

    for k in range(1, na):
        both(k, complete)
    yield

    def sent_line(way, origin):
        @pl.when(g.is_up if way == 0 else g.is_down)
        def _():
            line_head(way, origin).wait_send()
            line_tail(way, origin).wait_send()

    when_up_origin(0, sent_line)
    when_down_origin(0, sent_line)
    for k in range(1, na):
        both(k, sent_line)

    def sent(way, origin, first=False):
        whole = slot(origin, g.b, g.l)
        for step in range(1, nl):
            left(g, l_sem.at[0, step - 1, origin], whole if first else whole.at[:, head])
            for turn in range(1, nb):
                left(g, lb2_sem.at[0, step - 1, turn - 1, origin], whole.at[:, head])
        for step in range(1, nb):
            left(g, b_sem.at[0, step - 1, origin], whole if first else whole.at[:, head])
        if siblings:
            for step in range(1, ns):
                left(g, s_sem.at[0, step - 1, origin], square(origin))
                came(g, s_sem.at[1, step - 1, origin], o_ref.at[origin, :, :, g.other("s", ns - step)])

    sent(0, g.a, True)
    for step in range(1, nb):
        for turn in range(1, nl):
            left(g, bl2_sem.at[0, step - 1, turn - 1], slot(g.a, g.b, g.l).at[:, tail])
    for k in range(1, na):
        both(k, sent)


def run_steps(*programs):
    alive = list(programs)
    while alive:
        for program in list(alive):
            try:
                next(program)
            except StopIteration:
                alive.remove(program)


def gather_kernel(sizes, x_ref, o_ref, *sems):
    g = Grid(sizes)
    g.greet_neighbours(False)
    run_steps(gathering(g, False, x_ref, o_ref, sems))


def gather(x, sizes, collective_id):
    na, nb, nl, ns = sizes
    rows, wide = x.shape
    out = pl.pallas_call(
        functools.partial(gather_kernel, sizes),
        out_shape=jax.ShapeDtypeStruct((na, nb, nl, 1, rows, wide), x.dtype),
        in_specs=[ANY],
        out_specs=ANY,
        scratch_shapes=gather_sems(sizes, False),
        compiler_params=pltpu.CompilerParams(collective_id=collective_id, has_side_effects=True),
    )(x)
    return out.reshape(-1, wide)


def expert_steps(g, shards, wholes, shared, columns, down, downs, sems):
    e_sem, es_sem, c_sem, cs_sem, d_sem, own_sem = sems
    na, nb, nl, ns = g.sizes

    def across(i, step):
        l_to = g.other("l", step)
        return remote(shards[i].at[l_to], wholes[i].at[g.l, g.s], (e_sem.at[0, i, step - 1], e_sem.at[1, i, step - 1]), g.at(l=l_to))

    def aside(i, turn, step):
        l_from = g.other("l", nl - turn) if turn else g.l
        src = wholes[i].at[l_from, g.s] if turn else shards[i].at[g.l]
        return remote(src, wholes[i].at[l_from, g.s], (es_sem.at[0, i, turn, step - 1], es_sem.at[1, i, turn, step - 1]), g.to("s", step))

    def aside_came(i, turn, step):
        l_from = g.other("l", nl - turn) if turn else g.l
        came(g, es_sem.at[1, i, turn, step - 1], wholes[i].at[l_from, g.other("s", ns - step)])

    def block(n, steps):
        a, b, l, _ = g.plane_at(steps)
        return remote(shared.at[a, b, l], columns.at[:, g.a, g.b, g.l, g.s], (c_sem.at[0, n], c_sem.at[1, n]), g.plane_at(steps))

    def downward(step):
        return remote(down, downs.at[g.s], (d_sem.at[0, step - 1], d_sem.at[1, step - 1]), g.to("s", step))

    def columns_aside(step):
        part = columns.at[:, :, :, :, g.s]
        return remote(part, part, (cs_sem.at[0, step - 1], cs_sem.at[1, step - 1]), g.to("s", step))

    count = len(shards)
    owns = [pltpu.make_async_copy(shards[i].at[g.l], wholes[i].at[g.l, g.s], own_sem.at[i]) for i in range(count)]
    owns.append(pltpu.make_async_copy(shared.at[g.a, g.b, g.l], columns.at[:, g.a, g.b, g.l, g.s], own_sem.at[count]))
    owns.append(pltpu.make_async_copy(down, downs.at[g.s], own_sem.at[count + 1]))
    steps = g.plane_steps()
    yield
    for step in range(1, nl):
        across(0, step).start()
    for copy in owns:
        copy.start()
    for step in range(1, ns):
        downward(step).start()
        for i in range(count):
            aside(i, 0, step).start()
    for n, at in enumerate(steps):
        block(n, at).start()
    yield
    for i in range(1, count):
        for step in range(1, nl):
            across(i, step).start()
        yield
    for copy in owns:
        copy.wait()
    for n, at in enumerate(steps):
        a, b, l, _ = g.plane_at(at, -1)
        came(g, c_sem.at[1, n], columns.at[:, a, b, l, g.s])
    for step in range(1, ns):
        columns_aside(step).start()
    for i in range(count):
        for turn in range(1, nl):
            came(g, e_sem.at[1, i, turn - 1], wholes[i].at[g.other("l", nl - turn), g.s])
            for step in range(1, ns):
                aside(i, turn, step).start()
    yield
    for n, at in enumerate(steps):
        block(n, at).wait_send()
    for step in range(1, ns):
        downward(step).wait_send()
        came(g, d_sem.at[1, step - 1], downs.at[g.other("s", ns - step)])
        columns_aside(step).wait_send()
        came(g, cs_sem.at[1, step - 1], columns.at[:, :, :, :, g.other("s", ns - step)])
    for i in range(count):
        for step in range(1, nl):
            across(i, step).wait_send()
        for turn in range(nl):
            for step in range(1, ns):
                aside(i, turn, step).wait_send()
                aside_came(i, turn, step)


def inputs_kernel(sizes, dense, wide_dy, gate, up, down, shared, sh_down, dense_o, dy_o, gate_o, up_o, down_o, columns_o, downs_o, *sems):
    g = Grid(sizes)
    g.greet_plane(True)
    run_steps(
        gathering(g, True, dense, dense_o, sems[:8]),
        gathering(g, False, wide_dy, dy_o, sems[8:16]),
        expert_steps(g, (gate, up, down), (gate_o, up_o, down_o), shared, columns_o, sh_down, downs_o, sems[16:]),
    )


def inputs_gather(dense, wide_dy, experts, shared, sh_down, sizes, collective_id):
    na, nb, nl, ns = sizes
    ranks, rows, ffe = experts[0].shape
    two, sh_rows, narrow = shared.shape[3:]
    shape = jax.ShapeDtypeStruct
    places = len(Grid.plane_steps(type("S", (), {"na": na, "nb": nb, "nl": nl})))
    dense_o, dy_o, *wholes, columns, downs = pl.pallas_call(
        functools.partial(inputs_kernel, sizes),
        out_shape=[
            shape((na, nb, nl, ns, *dense.shape), BF16),
            shape((na, nb, nl, 1, *wide_dy.shape), BF16),
            *[shape((ranks, ns, rows, ffe), BF16)] * 3,
            shape((two, na, nb, nl, ns, sh_rows, narrow), BF16),
            shape((ns, *sh_down.shape), BF16),
        ],
        in_specs=[ANY] * 7,
        out_specs=[ANY] * 7,
        scratch_shapes=gather_sems(sizes, True)
        + gather_sems(sizes, False)
        + [
            DMA((2, 3, nl - 1)),
            DMA((2, 3, nl, ns - 1)),
            DMA((2, places)),
            DMA((2, ns - 1)),
            DMA((2, ns - 1)),
            DMA((5,)),
        ],
        compiler_params=pltpu.CompilerParams(collective_id=collective_id, has_side_effects=True),
    )(dense, wide_dy, *experts, shared, sh_down)
    return (
        dense_o.reshape(-1, dense.shape[1]),
        dy_o.reshape(-1, wide_dy.shape[1]),
        [whole.reshape(-1, ffe) for whole in wholes],
        columns.reshape(two, -1, narrow),
        downs,
    )


def order(a, k):
    high, odd = a // 2, lax.rem(a, 2)
    return (3 * (1 - high), 2 + high - 2 * odd, 1 + odd, a)[k]


def add_rows(out, *terms):
    rows = out.shape[0]
    step = min(rows, 32)

    @pl.loop(0, rows, step=step)
    def _(r):
        at = pl.ds(pl.multiple_of(r, step), step)
        total = terms[0][at, :].astype(F32)
        for term in terms[1:]:
            total = total + term[at, :].astype(F32)
        out[at, :] = total.astype(out.dtype)


def scatter_scratch(sizes, siblings, rows, wide):
    na, nb, nl, ns = sizes
    head = split_of(wide)
    tail = wide - head
    shapes = [
        (nb - 1, na, nl, rows, head),
        (nl - 1, na, rows, head),
        (na, rows, head),
        (na + 1, rows, head),
        (na + 1, nb, nl, rows, tail),
        (nb, nl, rows, tail),
        (nl - 1, nb, rows, tail),
        (nb - 1, rows, tail),
        (ns - 1, na, nb, nl, rows, wide) if siblings else (16, 128),
    ]
    sems = [(2, nb - 1, na), (2, nl - 1, na), (2, 2, na), (2, 2, na), (2, nl - 1), (2, nb - 1), (2, ns - 1, na)]
    return [pltpu.VMEM(s, BF16) for s in shapes] + [DMA(s) for s in sems]


def scattering(g, siblings, p_ref, o_ref, scratch):
    one, two, total, line_a, line_b, tail_sum, tail_two, tail_three, s_buf = scratch[:9]
    b_sem, l_sem, la_sem, lb_sem, l2_sem, b2_sem, s_sem = scratch[9:]
    na, nb, nl, ns = g.sizes
    wide = o_ref.shape[-1]
    cut = split_of(wide)
    head, tail = pl.ds(0, cut), pl.ds(cut, wide - cut)

    def pair(sem, *index):
        return sem.at[(0, *index)], sem.at[(1, *index)]

    def block(k):
        return s_buf.at[0, k] if siblings else p_ref.at[order(g.a, k), :, :, 0]

    def sibling_copy(k, step):
        to = g.other("s", step)
        return remote(p_ref.at[order(g.a, k), :, :, to], s_buf.at[step - 1, k], pair(s_sem, step - 1, k), g.at(s=to))

    def b_copy(k, step):
        to = g.other("b", step)
        return remote(block(k).at[to, :, :, head], one.at[step - 1, k], pair(b_sem, step - 1, k), g.at(b=to))

    def l_copy(k, step):
        to = g.other("l", step)
        return remote(one.at[0, k, to], two.at[step - 1, k], pair(l_sem, step - 1, k), g.at(l=to))

    def place(way, dest, at):
        if way == 0:
            return dest
        far = (at - dest + na - 1) // na
        return dest * far + na * (1 - far)

    def head_copy(way, k):
        dest, to = order(g.a, k), g.a + 1 - 2 * way
        return remote(total.at[k], line_a.at[place(way, dest, to)], pair(la_sem, way, dest), g.at(a=to))

    def tail_copy(way, k, first):
        dest, to = order(g.a, k), g.a + 1 - 2 * way
        src = block(k).at[:, :, :, tail] if first else line_b.at[dest]
        return remote(src, line_b.at[place(way, dest, to)], pair(lb_sem, way, dest), g.at(a=to))

    def starts(k, act):
        if k == na - 1:
            return
        dest = order(g.a, k)

        @pl.when((g.a == 0) & (dest > g.a))
        def _():
            act(0)

        @pl.when((g.a == na - 1) & (dest < g.a))
        def _():
            act(1)

    def passes(k, act):
        if k == na - 1:
            return
        dest = order(g.a, k)

        @pl.when((g.a > 0) & (dest > g.a))
        def _():
            act(0)

        @pl.when((g.a < na - 1) & (dest < g.a))
        def _():
            act(1)

    def arrivals(act):
        mine = place(0, g.a, g.a)

        @pl.when(g.a == 0)
        def _():
            act((1,), (na,))

        @pl.when(g.a == na - 1)
        def _():
            act((0,), (mine,))

        @pl.when((g.a > 0) & (g.a < na - 1))
        def _():
            act((0, 1), (mine, na))

    def begin(k):
        if k >= na:
            return
        if siblings:
            for step in range(1, ns):
                came(g, s_sem.at[1, step - 1, k], s_buf.at[step - 1, k])
            for b in range(nb):
                for l in range(nl):
                    add_rows(s_buf.at[0, k, b, l], p_ref.at[order(g.a, k), b, l, g.s], *[s_buf.at[step, k, b, l] for step in range(ns - 1)])
        for step in range(1, nb):
            b_copy(k, step).start()
        starts(k, lambda way: tail_copy(way, k, True).start())

    def second(k):
        for step in range(1, nb):
            came(g, b_sem.at[1, step - 1, k], one.at[step - 1, k])
        for turn in range(nl):
            l = g.other("l", turn)
            add_rows(one.at[0, k, l], block(k).at[g.b, l, :, head], *[one.at[step, k, l] for step in range(nb - 1)])
            if turn:
                l_copy(k, turn).start()

    def third(k):
        for step in range(1, nl):
            came(g, l_sem.at[1, step - 1, k], two.at[step - 1, k])
        add_rows(total.at[k], one.at[0, k, g.l], *[two.at[step, k] for step in range(nl - 1)])
        starts(k, lambda way: head_copy(way, k).start())

    def pass_head(k):
        def act(way):
            dest = order(g.a, k)
            came(g, la_sem.at[1, way, dest], line_a.at[dest])
            add_rows(total.at[k], total.at[k], line_a.at[dest])
            head_copy(way, k).start()

        passes(k, act)

    def pass_tail(k):
        def act(way):
            dest = order(g.a, k)
            came(g, lb_sem.at[1, way, dest], line_b.at[dest])
            for b in range(nb):
                for l in range(nl):
                    add_rows(line_b.at[dest, b, l], line_b.at[dest, b, l], block(k).at[b, l, :, tail])
            tail_copy(way, k, False).start()

        passes(k, act)

    def tail_here():
        def act(ways, slots):
            for way, slot in zip(ways, slots):
                came(g, lb_sem.at[1, way, g.a], line_b.at[slot])
            for b in range(nb):
                for l in range(nl):
                    add_rows(tail_sum.at[b, l], block(na - 1).at[b, l, :, tail], *[line_b.at[slot, b, l] for slot in slots])

        arrivals(act)
        for step in range(1, nl):
            tail_l(step).start()

    def tail_l(step):
        to = g.other("l", step)
        return remote(tail_sum.at[:, to], tail_two.at[step - 1], pair(l2_sem, step - 1), g.at(l=to))

    def tail_b(step):
        to = g.other("b", step)
        return remote(tail_two.at[0, to], tail_three.at[step - 1], pair(b2_sem, step - 1), g.at(b=to))

    if siblings:
        for k in range(na):
            for step in range(1, ns):
                sibling_copy(k, step).start()
    begin(0)
    begin(1)
    yield
    for k in range(na):
        second(k)
        begin(k + 2)
        if k >= 1:
            third(k - 1)
            pass_tail(k - 1)
        if k >= 2:
            pass_head(k - 2)
        yield
    third(na - 1)
    pass_head(na - 2)
    tail_here()
    yield

    def head_here(ways, slots):
        for way, slot in zip(ways, slots):
            came(g, la_sem.at[1, way, g.a], line_a.at[slot])
        add_rows(o_ref.at[:, head], total.at[na - 1], *[line_a.at[slot] for slot in slots])

    for step in range(1, nl):
        came(g, l2_sem.at[1, step - 1], tail_two.at[step - 1])
    for b in range(nb):
        add_rows(tail_two.at[0, b], tail_sum.at[b, g.l], *[tail_two.at[step, b] for step in range(nl - 1)])
    for step in range(1, nb):
        tail_b(step).start()
    arrivals(head_here)
    yield
    for step in range(1, nb):
        came(g, b2_sem.at[1, step - 1], tail_three.at[step - 1])
    add_rows(o_ref.at[:, tail], tail_two.at[0, g.b], *[tail_three.at[step] for step in range(nb - 1)])

    for k in range(na):
        if siblings:
            for step in range(1, ns):
                sibling_copy(k, step).wait_send()
        for step in range(1, nb):
            b_copy(k, step).wait_send()
        for step in range(1, nl):
            l_copy(k, step).wait_send()

        def sent(way, first):
            tail_copy(way, k, first).wait_send()
            head_copy(way, k).wait_send()

        starts(k, lambda way: sent(way, True))
        passes(k, lambda way: sent(way, False))
    for step in range(1, nl):
        tail_l(step).wait_send()
    for step in range(1, nb):
        tail_b(step).wait_send()


def scatters_kernel(sizes, count, *refs):
    g = Grid(sizes)
    g.greet_neighbours(False)
    ins, outs, scratch = refs[:count], refs[count : 2 * count], refs[2 * count :]
    each = len(scratch) // count
    run_steps(
        *[
            scattering(g, False, ins[i], outs[i], scratch[i * each : (i + 1) * each])
            for i in range(count)
        ]
    )


def scatter(partials, sizes, collective_id):
    na, nb, nl, ns = sizes
    count = len(partials)
    rows, wide = partials[0].shape[0] // (na * nb * nl), partials[0].shape[1]
    return pl.pallas_call(
        functools.partial(scatters_kernel, sizes, count),
        out_shape=[jax.ShapeDtypeStruct((rows, wide), F32)] * count,
        in_specs=[VMEM] * count,
        out_specs=[VMEM] * count,
        scratch_shapes=scatter_scratch(sizes, False, rows, wide) * count,
        compiler_params=pltpu.CompilerParams(collective_id=collective_id, has_side_effects=True, vmem_limit_bytes=VMEM_LIMIT),
    )(*[partial.reshape(na, nb, nl, 1, rows, wide) for partial in partials])


def scatter_pair(p, q, sizes, first_id, second_id):
    if p.size <= 2048 * 2048:
        return scatter([p, q], sizes, first_id)
    return scatter([p], sizes, first_id) + scatter([q], sizes, second_id)


def shared_steps(g, part, blocks, own, other, sems):
    s_sem, c_sem, own_sem = sems
    na, nb, nl, ns = g.sizes
    steps = g.plane_steps()

    def aside(step):
        to = g.other("s", step)
        return remote(part.at[:, :, :, to], other.at[step - 1], (s_sem.at[0, step - 1], s_sem.at[1, step - 1]), g.at(s=to))

    def send(n, at):
        a, b, l, _ = g.plane_at(at)
        return remote(other.at[0, a, b, l], blocks.at[g.a, g.b, g.l], (c_sem.at[0, n], c_sem.at[1, n]), g.plane_at(at))

    mine = pltpu.make_async_copy(part.at[:, :, :, g.s], own, own_sem.at[0])
    mine.start()
    for step in range(1, ns):
        aside(step).start()
    yield
    mine.wait()
    for step in range(1, ns):
        came(g, s_sem.at[1, step - 1], other.at[step - 1])
    for a in range(na):
        for b in range(nb):
            for l in range(nl):
                add_rows(other.at[0, a, b, l], own.at[a, b, l], *[other.at[step, a, b, l] for step in range(ns - 1)])
    for n, at in enumerate(steps):
        send(n, at).start()
    here = pltpu.make_async_copy(other.at[0, g.a, g.b, g.l], blocks.at[g.a, g.b, g.l], own_sem.at[1])
    here.start()
    yield
    yield
    yield
    yield
    here.wait()
    for n, at in enumerate(steps):
        a, b, l, _ = g.plane_at(at, -1)
        came(g, c_sem.at[1, n], blocks.at[a, b, l])
        send(n, at).wait_send()
    for step in range(1, ns):
        aside(step).wait_send()


def across_steps(g, blocks, outs, sem):
    def send(i, step):
        return remote(blocks.at[i, step - 1], outs.at[i, step - 1], (sem.at[0, i, step - 1], sem.at[1, i, step - 1]), g.to("l", step))

    count = blocks.shape[0]
    for i in range(count):
        for step in range(1, g.nl):
            send(i, step).start()
        yield
        yield
    for i in range(count):
        for step in range(1, g.nl):
            send(i, step).wait()


def outputs_kernel(sizes, p_ref, shared_ref, cross_ref, o_ref, blocks_ref, cross_o, own, other, *scratch):
    g = Grid(sizes)
    g.greet_plane(True)
    run_steps(
        scattering(g, True, p_ref, o_ref, scratch[4:]),
        shared_steps(g, shared_ref, blocks_ref, own, other, scratch[:3]),
        across_steps(g, cross_ref, cross_o, scratch[3]),
    )


def outputs_scatter(partial, shared, cross, sizes, collective_id):
    na, nb, nl, ns = sizes
    rows, wide = partial.shape[0] // (na * nb * nl * ns), partial.shape[1]
    shared = shared.reshape(na, nb, nl, ns, -1, shared.shape[1])
    shape = jax.ShapeDtypeStruct
    return pl.pallas_call(
        functools.partial(outputs_kernel, sizes),
        out_shape=[
            shape((rows, wide), F32),
            shape((na, nb, nl, *shared.shape[4:]), BF16),
            shape(cross.shape, BF16),
        ],
        in_specs=[VMEM] + [ANY] * 2,
        out_specs=[VMEM] + [ANY] * 2,
        scratch_shapes=[
            pltpu.VMEM((na, nb, nl, *shared.shape[4:]), BF16),
            pltpu.VMEM((ns - 1, na, nb, nl, *shared.shape[4:]), BF16),
            DMA((2, ns - 1)),
            DMA((2, na * nb * nl - 1)),
            DMA((2,)),
            DMA((2, 3, nl - 1)),
        ]
        + scatter_scratch(sizes, True, rows, wide),
        compiler_params=pltpu.CompilerParams(collective_id=collective_id, has_side_effects=True, vmem_limit_bytes=VMEM_LIMIT),
    )(partial.reshape(na, nb, nl, ns, rows, wide), shared, cross)


def weights_kernel(sizes, gp, inner, xr, dg, du, own_o, cross_o, send, recv, own_buf, cross_buf, s_sem, c_sem):
    g = Grid(sizes)
    na, nb, nl, ns = sizes
    for step in range(1, ns):
        g.hello(g.to("s", step))
    pl.semaphore_wait(pltpu.get_barrier_semaphore(), ns - 1)
    rows, ffe = own_buf.shape[1:]
    jobs = ((xr, dg), (xr, du), (gp, inner))

    def product(i, l, s, out):
        left, right = jobs[i]
        at = (l * ns + s) * rows
        step = 256 if rows % 256 == 0 else rows

        @pl.loop(0, rows, step=step)
        def _(r):
            cols = pl.ds(pl.multiple_of(at + r, step), step)
            for to, tile in column_tiles(ffe, 256):
                value = dot_tn(left[:, cols], right[:, pl.ds(to, tile)])
                out[pl.ds(pl.multiple_of(r, step), step), pl.ds(to, tile)] = value.astype(out.dtype)

    def aside(i, turn, step):
        return remote(send.at[i % 2, turn, step - 1], recv.at[i, turn, step - 1], (s_sem.at[0, i, turn, step - 1], s_sem.at[1, i, turn, step - 1]), g.to("s", step))

    def keep(i):
        return [pltpu.make_async_copy(own_buf.at[i % 2], own_o.at[i], c_sem.at[i, 0])] + [
            pltpu.make_async_copy(cross_buf.at[i % 2, turn - 1], cross_o.at[i, turn - 1], c_sem.at[i, turn])
            for turn in range(1, nl)
        ]

    def sums(i):
        for turn in range(nl):
            out = cross_buf.at[i % 2, turn - 1] if turn else own_buf.at[i % 2]
            for step in range(1, ns):
                came(g, s_sem.at[1, i, turn, step - 1], recv.at[i, turn, step - 1])
            add_rows(out, out, *[recv.at[i, turn, step] for step in range(ns - 1)])
        for copy in keep(i):
            copy.start()

    for i in range(3):
        for turn in range(nl):
            for step in range(1, ns):
                if i >= 2:
                    aside(i - 2, turn, step).wait_send()
                product(i, g.other("l", turn), g.other("s", step), send.at[i % 2, turn, step - 1])
                aside(i, turn, step).start()
        if i >= 1:
            sums(i - 1)
        if i >= 2:
            for copy in keep(i - 2):
                copy.wait()
        for turn in range(nl):
            product(i, g.other("l", turn), g.s, cross_buf.at[i % 2, turn - 1] if turn else own_buf.at[i % 2])
    sums(2)
    for i in range(1, 3):
        for copy in keep(i):
            copy.wait()
        for turn in range(nl):
            for step in range(1, ns):
                aside(i, turn, step).wait_send()


def expert_weights(gp, inner, xr, dg, du, sizes, collective_id):
    na, nb, nl, ns = sizes
    rows, ffe = gp.shape[1] // (nl * ns), inner.shape[1]
    return pl.pallas_call(
        functools.partial(weights_kernel, sizes),
        out_shape=[
            jax.ShapeDtypeStruct((3, rows, ffe), F32),
            jax.ShapeDtypeStruct((3, nl - 1, rows, ffe), BF16),
        ],
        in_specs=[VMEM] * 5,
        out_specs=[ANY] * 2,
        scratch_shapes=[
            pltpu.VMEM((2, nl, ns - 1, rows, ffe), BF16),
            pltpu.VMEM((3, nl, ns - 1, rows, ffe), BF16),
            pltpu.VMEM((2, rows, ffe), F32),
            pltpu.VMEM((2, nl - 1, rows, ffe), BF16),
            DMA((2, 3, nl, ns - 1)),
            DMA((3, nl)),
        ],
        compiler_params=pltpu.CompilerParams(collective_id=collective_id, has_side_effects=True, vmem_limit_bytes=VMEM_LIMIT),
    )(gp, inner, xr, dg, du)


def rms_norm(values, gain_row):
    factor = lax.rsqrt(jnp.mean(values * values, axis=-1, keepdims=True) + EPS)
    return values * factor * gain_row


def rotate(values):
    length = values.shape[0]
    half_dim = values.shape[-1] // 2
    position = jnp.arange(length).astype(F32)
    inverse = ROPE_BASE ** (-jnp.arange(half_dim).astype(F32) * 2.0 / values.shape[-1])
    angle_table = position[:, None] * inverse[None, :]
    cosine = jnp.cos(angle_table)[:, None, :]
    sine = jnp.sin(angle_table)[:, None, :]
    lower = values[..., :half_dim]
    upper = values[..., half_dim:]
    return jnp.concatenate(
        [lower * cosine - upper * sine, upper * cosine + lower * sine], axis=-1
    )


def lane_pad(block):
    return jnp.pad(block, ((0, 0), (0, -block.shape[1] % 128)))


def silu_pair(gate_part, up_part):
    return jax.nn.silu(gate_part) * up_part


def silu_parts(v):
    sig = 1.0 / (1.0 + jnp.exp(-v))
    return sig, v * sig


def exact(left, right, dims):
    return lax.dot_general(
        left, right, (dims, ((), ())), preferred_element_type=F32, precision=lax.Precision.HIGHEST
    )


def column_tiles(wide, tile):
    return [(at, min(tile, wide - at)) for at in range(0, wide, tile)]


def moe_kernel(seqs, experts, x_ref, dy_ref, pick_ref, back_ref, router_ref, wg_ref, wu_ref, wd_ref, sgu_ref, sd_ref,
               xr_ref, gp_ref, inner_ref, dg_ref, du_ref, share_ref, dsgu_ref, out_ref, dx_ref, gg_ref,
               g_buf, u_buf, dyr_buf, gate_buf, sum_buf, mm_buf):
    length = x_ref.shape[0] // seqs
    cap = xr_ref.shape[0] // seqs
    width = x_ref.shape[1]
    ffe = wg_ref.shape[1]
    narrow = sd_ref.shape[0]
    lane = lax.broadcasted_iota(jnp.int32, (length, 128), 1)
    mine = (lax.axis_index(PLANE) == lane).astype(F32)

    for n in range(seqs):
        toks, slots = pl.ds(n * length, length), pl.ds(n * cap, cap)
        x = x_ref[toks, :]
        dy = dy_ref[toks, pl.ds(0, width)]
        xr_ref[slots, :] = dot(pick_ref[n], x).astype(BF16)
        dyr_buf[slots, :] = dot(pick_ref[n], dy).astype(BF16)
        hot = dy_ref[toks, pl.ds(width, 128)].astype(F32)
        logits = jnp.where(hot > 0, dot(x, router_ref[...]), -1e30)
        top = jnp.max(logits, axis=1, keepdims=True)
        raised = jnp.exp(logits - top)
        gate = jnp.sum(raised * mine, axis=1, keepdims=True) / jnp.sum(raised, axis=1, keepdims=True)
        gate = jnp.broadcast_to(gate, (length, 128))
        gate_buf[slots, :] = exact(pick_ref[n].astype(F32), gate, ((1,), (0,)))

    for at, tile in column_tiles(ffe, 256):
        cols = pl.ds(at, tile)
        g = dot(xr_ref[...], wg_ref[:, cols])
        u = dot(xr_ref[...], wu_ref[:, cols])
        g_buf[:, cols] = g
        u_buf[:, cols] = u
        inner_ref[:, cols] = (silu_parts(g)[1] * u).astype(BF16)
    share_gu = dot(x_ref[...], sgu_ref[...])
    d_share = dot_nt(dy_ref[:, pl.ds(0, width)], sd_ref[...])
    sg, su = share_gu[:, :narrow], share_gu[:, narrow:]
    sig, act = silu_parts(sg)
    share_ref[...] = (act * su).astype(BF16)
    dsgu_ref[:, :narrow] = (d_share * su * sig * (1.0 + sg * (1.0 - sig))).astype(BF16)
    dsgu_ref[:, narrow:] = (d_share * act).astype(BF16)
    sum_buf[...] = jnp.zeros_like(sum_buf)
    for at, tile in column_tiles(width, 256):
        cols = pl.ds(at, tile)
        produced = dot_nt(inner_ref[...], wd_ref[cols, :])
        dyr = dyr_buf[:, cols].astype(F32)
        gate = gate_buf[:, pl.ds(0, 1)]
        sum_buf[...] += jnp.broadcast_to(jnp.sum(produced * dyr, axis=1, keepdims=True), sum_buf.shape)
        gp_ref[:, cols] = (gate * dyr).astype(BF16)
        mm_buf[...] = (gate * produced).astype(BF16)
        for n in range(seqs):
            toks, slots = pl.ds(n * length, length), pl.ds(n * cap, cap)
            out_ref[toks, cols] = (dot(back_ref[n], mm_buf[slots, :]) + dot(share_ref[toks, :], sd_ref[:, cols])).astype(BF16)
    for n in range(seqs):
        slots = pl.ds(n * cap, cap)
        gg_ref[n] = exact(sum_buf[slots, :], pick_ref[n].astype(F32), ((0,), (0,)))[:8]

    for at, tile in column_tiles(ffe, 256):
        cols = pl.ds(at, tile)
        d_inner = dot(gp_ref[...], wd_ref[:, cols])
        g, u = g_buf[:, cols], u_buf[:, cols]
        sig, act = silu_parts(g)
        dg_ref[:, cols] = (d_inner * u * sig * (1.0 + g * (1.0 - sig))).astype(BF16)
        du_ref[:, cols] = (d_inner * act).astype(BF16)
    for at, tile in column_tiles(width, 256):
        cols = pl.ds(at, tile)
        rows = dot_nt(dg_ref[...], wg_ref[cols, :]) + dot_nt(du_ref[...], wu_ref[cols, :])
        mm_buf[...] = rows.astype(BF16)
        for n in range(seqs):
            toks, slots = pl.ds(n * length, length), pl.ds(n * cap, cap)
            dx_ref[toks, cols] = (dot(back_ref[n], mm_buf[slots, :]) + dot_nt(dsgu_ref[toks, :], sgu_ref[cols, :])).astype(BF16)


def moe(x_all, wide_dy, pick, router, wg, wu, wd, sgu, sd, experts, length, cap, steps):
    total = x_all.shape[0] // length
    seqs = total // steps
    width, ffe, narrow = x_all.shape[1], wg.shape[1], sd.shape[0]
    toks, slots = seqs * length, seqs * cap
    shape = jax.ShapeDtypeStruct

    def rows(count, wide):
        return pl.BlockSpec((count, wide), lambda i: (i, 0))

    def whole(array):
        return pl.BlockSpec(array.shape, lambda i: (0, 0), pipeline_mode=pl.Buffered(1))

    def out(count, wide):
        return shape((steps * count, wide), BF16)

    return pl.pallas_call(
        functools.partial(moe_kernel, seqs, experts),
        grid=(steps,),
        in_specs=[
            rows(toks, width),
            rows(toks, wide_dy.shape[1]),
            pl.BlockSpec((seqs, cap, length), lambda i: (i, 0, 0)),
            pl.BlockSpec((seqs, length, cap), lambda i: (i, 0, 0)),
            *[whole(w) for w in (router, wg, wu, wd, sgu, sd)],
        ],
        out_specs=[
            rows(slots, width),
            rows(slots, width),
            rows(slots, ffe),
            rows(slots, ffe),
            rows(slots, ffe),
            rows(toks, narrow),
            rows(toks, 2 * narrow),
            rows(toks, width),
            rows(toks, width),
            pl.BlockSpec((seqs, 8, length), lambda i: (i, 0, 0)),
        ],
        out_shape=[
            out(slots, width),
            out(slots, width),
            out(slots, ffe),
            out(slots, ffe),
            out(slots, ffe),
            out(toks, narrow),
            out(toks, 2 * narrow),
            out(toks, width),
            out(toks, width),
            shape((total, 8, length), F32),
        ],
        scratch_shapes=[
            pltpu.VMEM((slots, ffe), F32),
            pltpu.VMEM((slots, ffe), F32),
            pltpu.VMEM((slots, width), BF16),
            pltpu.VMEM((slots, 128), F32),
            pltpu.VMEM((slots, 128), F32),
            pltpu.VMEM((slots, 256), BF16),
        ],
        compiler_params=pltpu.CompilerParams(vmem_limit_bytes=VMEM_LIMIT),
        cost_estimate=pl.CostEstimate(flops=6 * 10**10, bytes_accessed=10**8, transcendentals=0),
    )(x_all, wide_dy, pick, pick.transpose(0, 2, 1), router, wg, wu, wd, sgu, sd)


def shards(
    tokens,
    doc_ids,
    routes,
    gain_attn,
    w_query,
    w_key,
    w_value,
    w_out,
    gain_moe,
    w_router,
    shared_gate,
    shared_up,
    shared_down,
    expert_gate,
    expert_up,
    expert_down,
    cotangent,
):
    length, width = tokens.shape
    group_size = HEADS // KV_HEADS
    score_scale = HEAD_DIM ** (-0.5)
    local_experts = expert_gate.shape[0]
    sub = lax.axis_size("s")
    groups = lax.axis_size("a") * lax.axis_size("b") * lax.axis_size("l")
    experts_total = groups
    capacity = length * TOP * 4 // (3 * experts_total)
    sizes = tuple(lax.axis_size(axis) for axis in ALL)
    my_expert = lax.axis_index(PLANE)
    kvw = w_key.shape[1]
    qw = w_query.shape[1]

    small = jnp.concatenate(
        [w_router, gain_attn[:, None], gain_moe[:, None]], axis=1
    )
    small = lane_pad(small)
    hot = jnp.any(routes[:, :, None] == jnp.arange(experts_total)[None, None, :], axis=1)
    wide_dy = jnp.concatenate([cotangent, lane_pad(hot.astype(BF16))], axis=1)
    shared = jnp.stack([shared_gate, shared_up]).reshape(2, shared_gate.shape[0], *sizes[:3], -1)
    sh_rows = shared_down.shape[0]
    sh_pad = -sh_rows % 16
    dense, dy_all, (wg, wu, wd), columns, downs = inputs_gather(
        jnp.concatenate([w_query, w_key, w_value, w_out, small], axis=1),
        wide_dy,
        (expert_gate, expert_up, expert_down),
        shared.transpose(2, 3, 4, 0, 1, 5),
        jnp.pad(shared_down, ((0, sh_pad), (0, 0))),
        sizes,
        1,
    )
    sgu = jnp.concatenate([lane_pad(columns[0]), lane_pad(columns[1])], axis=1)
    narrow = columns.shape[2]
    sd_w = downs[:, :sh_rows].reshape(-1, width)
    sd_w = jnp.pad(sd_w, ((0, -narrow % 128), (0, 0)))
    hot_all = dy_all[:, width : width + experts_total] > 0
    query_full = dense[:, :qw]
    key_full = dense[:, qw : qw + kvw]
    value_full = dense[:, qw + kvw : qw + 2 * kvw]
    out_full = dense[:, qw + 2 * kvw : qw + 2 * kvw + width]
    rest = dense[:, qw + 2 * kvw + width :]
    router_full = rest[:, :experts_total]
    attn_gain = rest[:, experts_total].astype(F32)
    moe_gain = rest[:, experts_total + 1].astype(F32)

    inputs = tokens.astype(F32)
    normed, attn_norm_pull = jax.vjp(rms_norm, inputs, attn_gain)
    normed_low = normed.astype(BF16)
    query_pre = dot(normed_low, query_full).reshape(length, HEADS, HEAD_DIM)
    key_pre = dot(normed_low, key_full).reshape(length, KV_HEADS, HEAD_DIM)
    value_low = dot(normed_low, value_full).astype(BF16).reshape(length, KV_HEADS, HEAD_DIM)
    query_rot, query_pull = jax.vjp(rotate, query_pre)
    key_rot, key_pull = jax.vjp(rotate, key_pre)
    query_low = query_rot.astype(BF16).reshape(length, KV_HEADS, group_size, HEAD_DIM)
    key_low = key_rot.astype(BF16)
    position = jnp.arange(length)
    doc_row = doc_ids[0]
    allowed = (position[None, :] <= position[:, None]) & (doc_row[None, :] == doc_row[:, None])
    scores = (
        jnp.einsum("tkgd,skd->kgts", query_low, key_low, preferred_element_type=F32) * score_scale
    )
    scores = jnp.where(allowed, scores, -1e30)
    exp_scores = jnp.exp(scores - jnp.max(scores, axis=-1, keepdims=True))
    attend = exp_scores / jnp.sum(exp_scores, axis=-1, keepdims=True)
    attend_low = attend.astype(BF16)
    mixed_low = (
        jnp.einsum("kgts,skd->tkgd", attend_low, value_low, preferred_element_type=F32)
        .reshape(length, HEADS * HEAD_DIM)
        .astype(BF16)
    )
    hidden = inputs + dot(mixed_low, out_full)
    normed_moe, moe_norm_pull = jax.vjp(rms_norm, hidden, moe_gain)
    moe_low = normed_moe.astype(BF16)

    x_all = gather(moe_low, sizes, 2)
    seqs = groups
    mine = jnp.any(hot_all & (jnp.arange(experts_total)[None, :] == my_expert), axis=1)
    mine = mine.reshape(seqs, length)
    hits = mine.astype(jnp.int32)
    before = jnp.cumsum(hits, axis=1) - hits
    slot_hot = (jnp.arange(capacity)[None, :, None] == before[:, None, :]) & mine[:, None, :]
    x_rows, gp, inner_low, dg, du, share_low, dsgu, part, dx_part, gate_grad = moe(
        x_all, dy_all, slot_hot.astype(BF16), lane_pad(router_full), wg, wu, wd, sgu, sd_w,
        experts_total, length, capacity, max(seqs // 4, 1),
    )
    gate_grad = lax.all_to_all(gate_grad[:, 0], PLANE, split_axis=0, concat_axis=0, tiled=True)
    dy_all = dy_all[:, :width]
    moe_out, dx = scatter_pair(part, dx_part, sizes, 3, 6)
    output = (hidden + moe_out).astype(BF16)
    own_experts, cross_experts = expert_weights(gp, inner_low, x_rows, dg, du, sizes, 4)
    shared_grads = dot_tn(x_all, dsgu).astype(BF16)
    grad_shared_down = lax.psum_scatter(
        dot_tn(share_low[:, :narrow], dy_all), "s", scatter_dimension=0, tiled=True
    )

    own_logits = jnp.where(hot, dot(moe_low, router_full), -1e30)
    own_gates = jax.nn.softmax(own_logits, axis=-1)
    grad_gate = gate_grad.reshape(experts_total, length).T
    grad_logits = own_gates * (
        grad_gate - jnp.sum(own_gates * grad_gate, axis=-1, keepdims=True)
    )
    grad_logits = grad_logits.astype(BF16)
    grad_router = dot_tn(moe_low, grad_logits)
    dx = dx + dot_nt(grad_logits, router_full)
    grad_hidden_norm, grad_gain_moe = moe_norm_pull(dx)
    grad_hidden = cotangent.astype(F32) + grad_hidden_norm

    grad_hidden_low = grad_hidden.astype(BF16)
    grad_out_proj = dot_tn(mixed_low, grad_hidden_low)
    grad_mixed = (
        dot_nt(grad_hidden_low, out_full)
        .astype(BF16)
        .reshape(length, KV_HEADS, group_size, HEAD_DIM)
    )
    grad_value = jnp.einsum("kgts,tkgd->skd", attend_low, grad_mixed, preferred_element_type=F32)
    grad_attend = jnp.einsum("tkgd,skd->kgts", grad_mixed, value_low, preferred_element_type=F32)
    grad_scores = (
        attend * (grad_attend - jnp.sum(grad_attend * attend, axis=-1, keepdims=True))
    ).astype(BF16)
    grad_query = (
        jnp.einsum("kgts,skd->tkgd", grad_scores, key_low, preferred_element_type=F32) * score_scale
    )
    grad_key = (
        jnp.einsum("kgts,tkgd->skd", grad_scores, query_low, preferred_element_type=F32)
        * score_scale
    )
    grad_query_low = (
        query_pull(grad_query.reshape(length, HEADS, HEAD_DIM))[0].reshape(length, -1).astype(BF16)
    )
    grad_key_low = key_pull(grad_key)[0].reshape(length, -1).astype(BF16)
    grad_value_low = grad_value.reshape(length, -1).astype(BF16)
    grad_normed = (
        dot_nt(grad_query_low, query_full)
        + dot_nt(grad_key_low, key_full)
        + dot_nt(grad_value_low, value_full)
    )
    grad_inputs_norm, grad_gain_attn = attn_norm_pull(grad_normed)
    grad_tokens = grad_hidden + grad_inputs_norm
    grad_small = jnp.concatenate(
        [grad_router, grad_gain_attn[:, None], grad_gain_moe[:, None]], axis=1
    )
    grad_small = lane_pad(grad_small)
    dense_grads = jnp.concatenate(
        [
            dot_tn(normed_low, grad_query_low).astype(BF16),
            dot_tn(normed_low, grad_key_low).astype(BF16),
            dot_tn(normed_low, grad_value_low).astype(BF16),
            grad_out_proj.astype(BF16),
            grad_small.astype(BF16),
        ],
        axis=1,
    )
    total, blocks, cross = outputs_scatter(dense_grads, shared_grads, cross_experts, sizes, 5)
    dense_sum, small_sum = total[:, :-128], total[:, -128:]
    blocks = blocks.reshape(groups, *blocks.shape[3:]).transpose(1, 0, 2).astype(F32)
    half = blocks.shape[2] // 2
    grad_shared_gate = blocks[:, :, :narrow].reshape(blocks.shape[0], -1)
    grad_shared_up = blocks[:, :, half : half + narrow].reshape(blocks.shape[0], -1)
    my_l = lax.axis_index("l")
    expert_grads = []
    for i in range(3):
        here = jnp.arange(local_experts)[:, None, None]
        grad = own_experts[i][None]
        for step in range(1, local_experts):
            from_l = (my_l - step) % local_experts
            grad = jnp.where(here == from_l, cross[i, step - 1].astype(F32)[None], grad)
        expert_grads.append(grad)
    return (
        output,
        grad_tokens,
        small_sum[:, experts_total],
        dense_sum[:, :qw],
        dense_sum[:, qw : qw + kvw],
        dense_sum[:, qw + kvw : qw + 2 * kvw],
        dense_sum[:, qw + 2 * kvw :],
        small_sum[:, experts_total + 1],
        small_sum[:, :experts_total],
        grad_shared_gate,
        grad_shared_up,
        grad_shared_down,
        *expert_grads,
    )


def solution(mesh):
    ranks, shards_of = mesh.shape["expert"], mesh.shape["dp"]
    local_experts = 2
    split = Mesh(
        mesh.devices.reshape(4, ranks // 4, local_experts, shards_of // local_experts), ALL
    )
    rows = P(ALL, None)
    flat = P(ALL)
    expert = P(("a", "b"), ("l", "s"), None)
    return jax.shard_map(
        shards,
        mesh=split,
        in_specs=(rows,) * 3
        + (flat,)
        + (rows,) * 4
        + (flat,)
        + (rows,) * 4
        + (expert,) * 3
        + (rows,),
        out_specs=(rows,) * 2
        + (flat,)
        + (rows,) * 4
        + (flat,)
        + (rows,) * 4
        + (expert,) * 3,
        check_vma=False,
    )
```

time: 1210 us -> 1030 us (0.85)
  Pallas kernels: 565 us -> 798 us
  matrix products: 270 us -> 82.2 us
  waiting for transfers between devices: 74.3 us -> 0.02 us
  local copies, waits for them, and re-layouts: 146 us -> 79.1 us
  blocking collectives: 50.4 us -> 0 us
  starting transfers between devices: 44.6 us -> 4.73 us
    pallas_call x5 -> x6, Pallas kernels: 565 us -> 798 us  [the longest x1 217 us: inputs_gather(): pl.pallas_call(functools.partial(inputs_kernel, sizes), out_shape=[shape(...]
    dot_general x12 -> x5, matrix products: 85.7 us -> 16.2 us  [dot(): return jnp.dot(left, right, preferred_element_type=F32)]
    dot_general x11 -> x5, matrix products: 86.2 us -> 23.4 us  [dot_nt(): lax.dot_general(left, right, (((1,), (1,)), ((), ())), preferred_element_...]
    all_to_all x5 -> x1, waiting for transfers between devices: 52.9 us -> 0.01 us  [shards(): lax.all_to_all(gate_grad[:, 0], PLANE, split_axis=0, concat_axis=0, tiled...]
    all_gather x4 -> x0, blocking collectives: 50.4 us -> none  [the longest x1 42.6 us: plane_gather(): return lax.all_gather(block, PLANE, axis=0, tiled=True)]
    dot_general x4 -> x0, matrix products: 30.3 us -> none  [the longest x1 10.5 us: shards(): jnp.einsum('nst,nsd->ntd', pick_low, back_rows, preferred_element_type=F32)]
    all_to_all x5 -> x1, starting transfers between devices: 33.7 us -> 4.69 us  [shards(): lax.all_to_all(gate_grad[:, 0], PLANE, split_axis=0, concat_axis=0, tiled...]
    dot_general x11 -> x7, matrix products: 57.1 us -> 32.6 us  [dot_tn(): lax.dot_general(left, right, (((0,), (0,)), ((), ())), preferred_element_...]
  transfers between devices with their start and end apart: 23 -> 2, of which waited for: 4 -> 0; matrix products, arithmetic and copies ran while one was open for 31% -> 15% of each run, Pallas kernels for 47% -> 38%
where the time goes in v2:
time: 1030 us; the launch traced here: 1020 us
  Pallas kernels  798 us (77%)
  matrix products  82.2 us (8%)
  local copies, waits for them, and re-layouts  79.1 us (8%)
  other arithmetic  44.2 us (4%)
  between operations  15 us (1%)
    pallas_call x1, Pallas kernels, inputs_gather(): pl.pallas_call(functools.partial(inputs_kernel, sizes), out_shape=[shape(...  217 us
    pallas_call x1, Pallas kernels, outputs_scatter(): pl.pallas_call(functools.partial(outputs_kernel, sizes), out_shape=[shape...  186 us
    pallas_call x1, Pallas kernels, scatter(): pl.pallas_call(functools.partial(scatters_kernel, sizes, count), out_shap...  165 us
    pallas_call x1, Pallas kernels, moe(): pl.pallas_call(functools.partial(moe_kernel, seqs, experts), grid=(steps,...  119 us
    pallas_call x1, Pallas kernels, gather(): pl.pallas_call(functools.partial(gather_kernel, sizes), out_shape=jax.Sha...  76.8 us
    pallas_call x1, Pallas kernels, expert_weights(): pl.pallas_call(functools.partial(weights_kernel, sizes), out_shape=[jax.S...  35.7 us
    dot_general x7, matrix products, dot_tn(): lax.dot_general(left, right, (((0,), (0,)), ((), ())), preferred_element_...  32.6 us
    concatenate x1, local copies, waits for them, and re-layouts, shards(): jnp.concatenate([dot_tn(normed_low, grad_query_low).astype(BF16), dot_tn(...  26.2 us
  transfers between devices with their start and end apart: 2, of which 0 were waited for; matrix products, arithmetic and copies ran while one was open for 15% of the time, Pallas kernels for 38%

profile of v2, /device:TPU:0, one launch (start us, length us, event | category | flops | bytes accessed | tf_op | source)
XLA Modules:
  0.0 1023.5 jit_solution(3859517303368592727)
XLA Ops:
  21.5 216.7 %shard_map.280 = (bf16[4,2,2,2,64,5248]{5,4,3,2,1,0:T(8,128)(2,1)}, bf16[4,2,2,1,128,2176]{5,4,3,2,1,0:T(8,128)(2,1)}, bf16[2,2,512,1408]{3,2,1,0:T(8,128)(2,1)}...) custom-call(bf16[64,5248]{1,0:T(8,128)(2,1)} %copy-done.14, ...), custom_call_target="tpu_custom_call" | custom-call | tf_op jit(solution)/shard_map/pallas_call | solution.py:446
  242.5 4.7 fusion.29
  258.8 4.9 multiply_reduce_fusion.3
  265.8 76.8 %shard_map.281 = bf16[4,2,2,1,128,2048]{5,4,3,2,1,0:T(8,128)(2,1)} custom-call(bf16[128,2048]{1,0:T(8,128)(2,1)} %multiply_convert_fusion.1.x_ref), custom_call_target="tpu_custom_call" | custom-call | tf_op jit(solution)/shard_map/pallas_call | solution.py:341
  347.6 118.6 %shard_map.282 = (bf16[1024,2048]{1,0:T(8,128)(2,1)}, bf16[1024,2048]{1,0:T(8,128)(2,1)}, bf16[1024,1408]{1,0:T(8,128)(2,1)}, bf16[1024,1408]{1,0:T(8,128)(2,1)}...) custom-call(bf16[2048,2048]{1,0:T(8,128)(2,1)} %bitcast.142, ...), custom_call_target="tpu_custom_call" | custom-call | flops 60000002048 | bytes 100000000 | tf_op jit(solution)/shard_map/pallas_call | solution.py:1066
  467.6 4.7 all-to-all-start
  472.4 6.7 fusion.1
  481.5 9.4 convolution_convert_fusion.2
  490.9 35.7 %shard_map.284 = (f32[3,512,1408]{2,1,0:T(8,128)}, bf16[3,1,512,1408]{3,2,1,0:T(8,128)(2,1)}) custom-call(bf16[1024,2048]{1,0:T(8,128)(2,1)} %get-tuple-element.52.gp, bf16[1024,1408]{1,0:T(8,128)(2,1)} %get-tuple-element.53.inner, bf16[1024,2048]{1,0:T(8,128)(2,1)} %get-tuple-element.54.xr, bf16[1024,1408]{1,0:T(8,128)(2,1)} %get-tuple-element.55.dg, ...), custom_call_target="tpu_custom_call" | custom-call | tf_op jit(solution)/shard_map/pallas_call | solution.py:916
  526.7 6.6 slice_bitcast_fusion
  534.5 164.9 %shard_map.283 = (f32[128,2048]{1,0:T(8,128)}, f32[128,2048]{1,0:T(8,128)}) custom-call(bf16[4,2,2,1,128,2048]{5,4,3,2,1,0:T(8,128)(2,1)} %bitcast.140, bf16[4,2,2,1,128,2048]{5,4,3,2,1,0:T(8,128)(2,1)} %bitcast.141), custom_call_target="tpu_custom_call" | custom-call | tf_op jit(solution)/shard_map/pallas_call | solution.py:741
  700.9 2.9 multiply_reduce_fusion
  704.5 2.9 fusion.45
  708.4 7.1 fusion.18
  723.4 3.0 fusion.42
  735.6 7.2 fusion.7
  742.9 5.7 convert_dynamic-update-slice_fusion.1
  756.5 3.5 fusion.44
  762.1 5.6 convert_dynamic-update-slice_fusion
  768.6 26.2 %copy.136 = bf16[2048,5248]{1,0:T(8,128)(2,1)} copy(bf16[2048,5248]{0,1:T(8,128)(2,1)} %fusion.57) | data formatting | bytes 42991616 | tf_op jit(solution)/shard_map/concatenate | solution.py:1274
  794.9 185.5 %shard_map.285 = (f32[64,5248]{1,0:T(8,128)}, bf16[4,2,2,64,512]{4,3,2,1,0:T(8,128)(2,1)}, bf16[3,1,512,1408]{3,2,1,0:T(8,128)(2,1)}) custom-call(bf16[4,2,2,2,64,5248]{5,4,3,2,1,0:T(8,128)(2,1)} %bitcast.138, bf16[4,2,2,2,64,512]{5,4,3,2,1,0:T(8,128)(2,1)} %bitcast.168, bf16[3,1,512,1408]{3,2,1,0:T(8,128)(2,1)} %get-tuple-element.57.cross_ref), custom_call_target="tpu_custom_call" | custom-call | tf_op jit(solution)/shard_map/pallas_call | solution.py:829
  991.0 2.8 copy.138
  1002.5 5.4 bitcast_convert_fusion
  1007.9 8.5 broadcast_select_fusion
  (182 shorter events, 92.3 us)
Async XLA Ops:
  7.2 13.6 %copy-start.22 = (bf16[88,2048]{1,0:T(8,128)(2,1)S(1)}, bf16[88,2048]{1,0:T(8,128)(2,1)}, u32[]{:S(2)}) copy-start(bf16[88,2048]{1,0:T(8,128)(2,1)} %param.29) | copy-start | bytes 1081348
  21.5 218.7 %copy-start = (bf16[128,2048]{1,0:T(8,128)(2,1)S(1)}, bf16[128,2048]{1,0:T(8,128)(2,1)}, u32[]{:S(2)}) copy-start(bf16[128,2048]{1,0:T(8,128)(2,1)} %param.17) | copy-start | bytes 1572868
  240.4 6.8 copy-start.39
  240.4 6.8 copy-start.34
  247.2 7.2 copy-start.38
  255.9 7.9 copy-start.11
  256.3 7.5 copy-start.17
  256.3 7.5 copy-start.19
  257.9 5.9 copy-start.32
  263.8 79.7 %copy-start.37 = (f32[128]{0:T(128)}, f32[128]{0:T(128)S(1)}, u32[]{:S(2)}) copy-start(f32[128]{0:T(128)S(1)} %fusion.75) | copy-start | bytes 1540
  264.8 78.7 %copy-start.13 = (bf16[2,4,2,2,2,64,176]{6,5,4,3,2,1,0:T(8,128)(2,1)S(1)}, bf16[2,4,2,2,2,64,176]{6,5,4,3,2,1,0:T(8,128)(2,1)}, u32[]{:S(2)}) copy-start(bf16[2,4,2,2,2,64,176]{6,5,4,3,2,1,0:T(8,128)(2,1)} %get-tuple-element.44) | copy-start | bytes 4325380
  467.6 231.8 %all-to-all-start = ((f32[16,1,128]{2,1,0:T(1,128)}), f32[16,1,128]{2,1,0:T(1,128)}, u32[]{:S(2)}, u32[]{:S(2)}) async-start(f32[16,1,128]{2,1,0:T(1,128)} %slice.129), calls=%async_computation | async-start | bytes 16384 | tf_op jit(solution)/shard_map/all_to_all | solution.py:1217
  472.3 544.2 %reduce-scatter.2.cloned.1.call-start = ((), (), s32[]{:S(2)}) async-start(), calls=%async_computation.2 | async-start | bytes 2162688 | tf_op jit(solution)/shard_map/reduce_scatter | solution.py:1223
  472.3 6.7 copy-start.6
  472.4 6.7 copy-start.29
  472.4 9.2 copy-start.43
  526.7 6.7 copy-start.24
  526.7 6.6 copy-start.36
  708.4 9.1 copy-start.33
  735.6 7.3 copy-start.35
  742.9 6.5 copy-start.8
  754.1 8.0 copy-start.4
  754.1 8.0 copy-start.16
  794.9 188.5 %copy-start.40 = (f32[128]{0:T(128)S(1)}, f32[128]{0:T(128)}, u32[]{:S(2)}) copy-start(f32[128]{0:T(128)} %copy-done.39) | copy-start | bytes 1540
  (22 other events, 85.9 us)
Sparse Core Ops, SparseCore 0:
  479.2 10.1 reduce-scatter.1

commit v3 on v2

--- a/solution.py
+++ b/solution.py
@@ -121,11 +121,27 @@
     remote(src, src, (sem, sem), g.at()).wait_send()
 
 
+class Bounce:
+    def __init__(self, src, via, dst, sems):
+        self.there = pltpu.make_async_copy(src, via, sems.at[0])
+        self.back = pltpu.make_async_copy(via, dst, sems.at[1])
+
+    def start(self):
+        self.there.start()
+
+    def turn(self):
+        self.there.wait()
+        self.back.start()
+
+    def wait(self):
+        self.back.wait()
+
+
 def split_of(wide):
     return (wide * 5 // 7) // 128 * 128
 
 
-def gather_sems(sizes, siblings):
+def gather_scratch(sizes, siblings, x):
     na, nb, nl, ns = sizes
     return [
         DMA((2, 2, na)),
@@ -135,12 +151,13 @@
         DMA((2, nl - 1, nb - 1, na)),
         DMA((2, nb - 1, nl - 1)),
         DMA((2, ns, na)) if siblings else DMA((2, 1, 1)),
-        DMA((1,)),
+        DMA((2,)),
+        pltpu.VMEM(x.shape, x.dtype),
     ]
 
 
 def gathering(g, siblings, x_ref, o_ref, sems):
-    la_sem, lb_sem, b_sem, l_sem, lb2_sem, bl2_sem, s_sem, own_sem = sems
+    la_sem, lb_sem, b_sem, l_sem, lb2_sem, bl2_sem, s_sem, own_sem, own_buf = sems
     na, nb, nl, ns = g.sizes
     wide = x_ref.shape[-1]
     cut = split_of(wide)
@@ -252,12 +269,13 @@
         came(g, lb_sem.at[1, way, origin], o_ref.at[origin, :, :, me, :, tail])
         onward(way, line_tail(way, origin))
 
-    own = pltpu.make_async_copy(x_ref, slot(g.a, g.b, g.l), own_sem.at[0])
+    own = Bounce(x_ref, own_buf, slot(g.a, g.b, g.l), own_sem)
     own.start()
     onward(0, line_head(0, g.a, True))
     onward(1, line_head(1, g.a, True))
     spread(g.a, True)
     yield
+    own.turn()
     relay_head(g.a, True)
     relay_tail()
     yield
@@ -319,6 +337,12 @@
         both(k, sent)
 
 
+def after(count, program):
+    for _ in range(count):
+        yield
+    yield from program
+
+
 def run_steps(*programs):
     alive = list(programs)
     while alive:
@@ -329,46 +353,109 @@
                 alive.remove(program)
 
 
-def gather_kernel(sizes, x_ref, o_ref, *sems):
+def gather_kernel(sizes, x_ref, shard, o_ref, whole, *sems):
     g = Grid(sizes)
-    g.greet_neighbours(False)
-    run_steps(gathering(g, False, x_ref, o_ref, sems))
-
-
-def gather(x, sizes, collective_id):
+    g.greet_neighbours(True)
+    run_steps(
+        gathering(g, False, x_ref, o_ref, sems[:9]),
+        matrix_steps(g, (shard,), (whole,), sems[9:], (0, 0, 0, 2, 2)),
+    )
+
+
+def gather(x, shard, sizes, collective_id):
     na, nb, nl, ns = sizes
     rows, wide = x.shape
-    out = pl.pallas_call(
+    out, whole = pl.pallas_call(
         functools.partial(gather_kernel, sizes),
-        out_shape=jax.ShapeDtypeStruct((na, nb, nl, 1, rows, wide), x.dtype),
-        in_specs=[ANY],
-        out_specs=ANY,
-        scratch_shapes=gather_sems(sizes, False),
-        compiler_params=pltpu.CompilerParams(collective_id=collective_id, has_side_effects=True),
-    )(x)
-    return out.reshape(-1, wide)
-
-
-def expert_steps(g, shards, wholes, shared, columns, down, downs, sems):
-    e_sem, es_sem, c_sem, cs_sem, d_sem, own_sem = sems
+        out_shape=[jax.ShapeDtypeStruct((na, nb, nl, 1, rows, wide), x.dtype), matrix_shape(shard, sizes)],
+        in_specs=[ANY] * 2,
+        out_specs=[ANY] * 2,
+        scratch_shapes=gather_scratch(sizes, False, x) + matrix_scratch(sizes, shard),
+        compiler_params=pltpu.CompilerParams(collective_id=collective_id, has_side_effects=True, vmem_limit_bytes=VMEM_LIMIT),
+    )(x, shard)
+    return out.reshape(-1, wide), whole.reshape(-1, shard.shape[2])
+
+
+CHUNKS = 4
+
+
+def matrix_scratch(sizes, *shards):
+    na, nb, nl, ns = sizes
+    count = len(shards)
+    return [
+        DMA((2, count, nl - 1, CHUNKS)),
+        DMA((2, count, nl, ns - 1, CHUNKS)),
+        DMA((count, 2)),
+        pltpu.VMEM((count, *shards[0].shape[1:]), BF16),
+    ]
+
+
+def matrix_steps(g, shards, wholes, sems, paces):
+    e_sem, es_sem, own_sem, own_buf = sems
     na, nb, nl, ns = g.sizes
-
-    def across(i, step):
-        l_to = g.other("l", step)
-        return remote(shards[i].at[l_to], wholes[i].at[g.l, g.s], (e_sem.at[0, i, step - 1], e_sem.at[1, i, step - 1]), g.at(l=l_to))
-
-    def aside(i, turn, step):
+    count = len(shards)
+    rows = shards[0].shape[1] // CHUNKS
+    chunks = [(i, pl.ds(c * rows, rows), c) for i in range(count) for c in range(CHUNKS)]
+
+    def across(i, at, c, step):
+        to = g.other("l", step)
+        return remote(shards[i].at[to, at], wholes[i].at[g.l, g.s, at], (e_sem.at[0, i, step - 1, c], e_sem.at[1, i, step - 1, c]), g.at(l=to))
+
+    def aside(i, at, c, turn, step):
         l_from = g.other("l", nl - turn) if turn else g.l
-        src = wholes[i].at[l_from, g.s] if turn else shards[i].at[g.l]
-        return remote(src, wholes[i].at[l_from, g.s], (es_sem.at[0, i, turn, step - 1], es_sem.at[1, i, turn, step - 1]), g.to("s", step))
-
-    def aside_came(i, turn, step):
+        src = wholes[i].at[l_from, g.s, at] if turn else shards[i].at[g.l, at]
+        return remote(src, wholes[i].at[l_from, g.s, at], (es_sem.at[0, i, turn, step - 1, c], es_sem.at[1, i, turn, step - 1, c]), g.to("s", step))
+
+    def aside_came(i, at, c, turn, step):
         l_from = g.other("l", nl - turn) if turn else g.l
-        came(g, es_sem.at[1, i, turn, step - 1], wholes[i].at[l_from, g.other("s", ns - step)])
-
-    def block(n, steps):
-        a, b, l, _ = g.plane_at(steps)
-        return remote(shared.at[a, b, l], columns.at[:, g.a, g.b, g.l, g.s], (c_sem.at[0, n], c_sem.at[1, n]), g.plane_at(steps))
+        came(g, es_sem.at[1, i, turn, step - 1, c], wholes[i].at[l_from, g.other("s", ns - step), at])
+
+    owns = [Bounce(shards[i].at[g.l], own_buf.at[i], wholes[i].at[g.l, g.s], own_sem.at[i]) for i in range(count)]
+    for copy in owns:
+        copy.start()
+    rest = list(chunks)
+    for j, pace in enumerate(paces):
+        for chunk in rest[:pace]:
+            for step in range(1, nl):
+                across(*chunk, step).start()
+            for step in range(1, ns):
+                aside(*chunk, 0, step).start()
+        rest = rest[pace:]
+        if j == 2:
+            for copy in owns:
+                copy.turn()
+        yield
+    for chunk in chunks:
+        i, at, c = chunk
+        for turn in range(1, nl):
+            came(g, e_sem.at[1, i, turn - 1, c], wholes[i].at[g.other("l", nl - turn), g.s, at])
+            for step in range(1, ns):
+                aside(*chunk, turn, step).start()
+    yield
+    for copy in owns:
+        copy.wait()
+    for chunk in chunks:
+        for step in range(1, nl):
+            across(*chunk, step).wait_send()
+        for turn in range(nl):
+            for step in range(1, ns):
+                aside(*chunk, turn, step).wait_send()
+                aside_came(*chunk, turn, step)
+
+
+def matrix_shape(shard, sizes):
+    ranks, rows, ffe = shard.shape
+    return jax.ShapeDtypeStruct((ranks, sizes[3], rows, ffe), BF16)
+
+
+def column_steps(g, shared, columns, down, downs, sems):
+    c_sem, cs_sem, d_sem, own_sem, own_buf, down_buf = sems
+    ns = g.ns
+    steps = g.plane_steps()
+
+    def block(n, at):
+        a, b, l, _ = g.plane_at(at)
+        return remote(shared.at[a, b, l], columns.at[:, g.a, g.b, g.l, g.s], (c_sem.at[0, n], c_sem.at[1, n]), g.plane_at(at))
 
     def downward(step):
         return remote(down, downs.at[g.s], (d_sem.at[0, step - 1], d_sem.at[1, step - 1]), g.to("s", step))
@@ -377,39 +464,29 @@
         part = columns.at[:, :, :, :, g.s]
         return remote(part, part, (cs_sem.at[0, step - 1], cs_sem.at[1, step - 1]), g.to("s", step))
 
-    count = len(shards)
-    owns = [pltpu.make_async_copy(shards[i].at[g.l], wholes[i].at[g.l, g.s], own_sem.at[i]) for i in range(count)]
-    owns.append(pltpu.make_async_copy(shared.at[g.a, g.b, g.l], columns.at[:, g.a, g.b, g.l, g.s], own_sem.at[count]))
-    owns.append(pltpu.make_async_copy(down, downs.at[g.s], own_sem.at[count + 1]))
-    steps = g.plane_steps()
-    yield
-    for step in range(1, nl):
-        across(0, step).start()
+    owns = [
+        Bounce(shared.at[g.a, g.b, g.l], own_buf, columns.at[:, g.a, g.b, g.l, g.s], own_sem.at[0]),
+        Bounce(down, down_buf, downs.at[g.s], own_sem.at[1]),
+    ]
+    yield
     for copy in owns:
         copy.start()
     for step in range(1, ns):
         downward(step).start()
-        for i in range(count):
-            aside(i, 0, step).start()
+    yield
     for n, at in enumerate(steps):
         block(n, at).start()
-    yield
-    for i in range(1, count):
-        for step in range(1, nl):
-            across(i, step).start()
-        yield
+    for copy in owns:
+        copy.turn()
+    yield
     for copy in owns:
         copy.wait()
+    yield
     for n, at in enumerate(steps):
         a, b, l, _ = g.plane_at(at, -1)
         came(g, c_sem.at[1, n], columns.at[:, a, b, l, g.s])
     for step in range(1, ns):
         columns_aside(step).start()
-    for i in range(count):
-        for turn in range(1, nl):
-            came(g, e_sem.at[1, i, turn - 1], wholes[i].at[g.other("l", nl - turn), g.s])
-            for step in range(1, ns):
-                aside(i, turn, step).start()
     yield
     for n, at in enumerate(steps):
         block(n, at).wait_send()
@@ -418,58 +495,53 @@
         came(g, d_sem.at[1, step - 1], downs.at[g.other("s", ns - step)])
         columns_aside(step).wait_send()
         came(g, cs_sem.at[1, step - 1], columns.at[:, :, :, :, g.other("s", ns - step)])
-    for i in range(count):
-        for step in range(1, nl):
-            across(i, step).wait_send()
-        for turn in range(nl):
-            for step in range(1, ns):
-                aside(i, turn, step).wait_send()
-                aside_came(i, turn, step)
-
-
-def inputs_kernel(sizes, dense, wide_dy, gate, up, down, shared, sh_down, dense_o, dy_o, gate_o, up_o, down_o, columns_o, downs_o, *sems):
+
+
+def inputs_kernel(sizes, dense, wide_dy, gate, up, shared, sh_down, dense_o, dy_o, gate_o, up_o, columns_o, downs_o, *sems):
     g = Grid(sizes)
     g.greet_plane(True)
     run_steps(
-        gathering(g, True, dense, dense_o, sems[:8]),
-        gathering(g, False, wide_dy, dy_o, sems[8:16]),
-        expert_steps(g, (gate, up, down), (gate_o, up_o, down_o), shared, columns_o, sh_down, downs_o, sems[16:]),
-    )
-
-
-def inputs_gather(dense, wide_dy, experts, shared, sh_down, sizes, collective_id):
+        gathering(g, True, dense, dense_o, sems[:9]),
+        after(2, gathering(g, False, wide_dy, dy_o, sems[9:18])),
+        matrix_steps(g, (gate, up), (gate_o, up_o), sems[18:22], (0, 0, 0, 2, 2, 2, 2)),
+        after(2, column_steps(g, shared, columns_o, sh_down, downs_o, sems[22:])),
+    )
+
+
+def inputs_gather(dense, wide_dy, gate, up, shared, sh_down, sizes, collective_id):
     na, nb, nl, ns = sizes
-    ranks, rows, ffe = experts[0].shape
     two, sh_rows, narrow = shared.shape[3:]
     shape = jax.ShapeDtypeStruct
-    places = len(Grid.plane_steps(type("S", (), {"na": na, "nb": nb, "nl": nl})))
-    dense_o, dy_o, *wholes, columns, downs = pl.pallas_call(
+    dense_o, dy_o, gate_o, up_o, columns, downs = pl.pallas_call(
         functools.partial(inputs_kernel, sizes),
         out_shape=[
             shape((na, nb, nl, ns, *dense.shape), BF16),
             shape((na, nb, nl, 1, *wide_dy.shape), BF16),
-            *[shape((ranks, ns, rows, ffe), BF16)] * 3,
+            matrix_shape(gate, sizes),
+            matrix_shape(up, sizes),
             shape((two, na, nb, nl, ns, sh_rows, narrow), BF16),
             shape((ns, *sh_down.shape), BF16),
         ],
-        in_specs=[ANY] * 7,
-        out_specs=[ANY] * 7,
-        scratch_shapes=gather_sems(sizes, True)
-        + gather_sems(sizes, False)
+        in_specs=[ANY] * 6,
+        out_specs=[ANY] * 6,
+        scratch_shapes=gather_scratch(sizes, True, dense)
+        + gather_scratch(sizes, False, wide_dy)
+        + matrix_scratch(sizes, gate, up)
         + [
-            DMA((2, 3, nl - 1)),
-            DMA((2, 3, nl, ns - 1)),
-            DMA((2, places)),
+            DMA((2, na * nb * nl - 1)),
             DMA((2, ns - 1)),
             DMA((2, ns - 1)),
-            DMA((5,)),
+            DMA((2, 2)),
+            pltpu.VMEM((two, sh_rows, narrow), BF16),
+            pltpu.VMEM(sh_down.shape, BF16),
         ],
-        compiler_params=pltpu.CompilerParams(collective_id=collective_id, has_side_effects=True),
-    )(dense, wide_dy, *experts, shared, sh_down)
+        compiler_params=pltpu.CompilerParams(collective_id=collective_id, has_side_effects=True, vmem_limit_bytes=VMEM_LIMIT),
+    )(dense, wide_dy, gate, up, shared, sh_down)
     return (
         dense_o.reshape(-1, dense.shape[1]),
         dy_o.reshape(-1, wide_dy.shape[1]),
-        [whole.reshape(-1, ffe) for whole in wholes],
+        gate_o.reshape(-1, gate.shape[2]),
+        up_o.reshape(-1, up.shape[2]),
         columns.reshape(two, -1, narrow),
         downs,
     )
@@ -512,7 +584,7 @@
     return [pltpu.VMEM(s, BF16) for s in shapes] + [DMA(s) for s in sems]
 
 
-def scattering(g, siblings, p_ref, o_ref, scratch):
+def scattering(g, siblings, p_ref, o_ref, scratch, prepare=None):
     one, two, total, line_a, line_b, tail_sum, tail_two, tail_three, s_buf = scratch[:9]
     b_sem, l_sem, la_sem, lb_sem, l2_sem, b2_sem, s_sem = scratch[9:]
     na, nb, nl, ns = g.sizes
@@ -662,14 +734,20 @@
         to = g.other("b", step)
         return remote(tail_two.at[0, to], tail_three.at[step - 1], pair(b2_sem, step - 1), g.at(b=to))
 
-    if siblings:
-        for k in range(na):
+    def ahead(k):
+        if siblings and k < na:
+            prepare(order(g.a, k))
             for step in range(1, ns):
                 sibling_copy(k, step).start()
+
+    ahead(0)
+    ahead(1)
     begin(0)
+    ahead(2)
     begin(1)
     yield
     for k in range(na):
+        ahead(k + 3)
         second(k)
         begin(k + 2)
         if k >= 1:
@@ -721,37 +799,110 @@
         tail_b(step).wait_send()
 
 
-def scatters_kernel(sizes, count, *refs):
+def scatter_kernel(sizes, p_ref, o_ref, *scratch):
     g = Grid(sizes)
     g.greet_neighbours(False)
-    ins, outs, scratch = refs[:count], refs[count : 2 * count], refs[2 * count :]
-    each = len(scratch) // count
-    run_steps(
-        *[
-            scattering(g, False, ins[i], outs[i], scratch[i * each : (i + 1) * each])
-            for i in range(count)
-        ]
-    )
-
-
-def scatter(partials, sizes, collective_id):
+    run_steps(scattering(g, False, p_ref, o_ref, scratch))
+
+
+def scatter_shapes(partial, sizes):
     na, nb, nl, ns = sizes
-    count = len(partials)
-    rows, wide = partials[0].shape[0] // (na * nb * nl), partials[0].shape[1]
+    rows, wide = partial.shape[0] // (na * nb * nl), partial.shape[1]
+    return partial.reshape(na, nb, nl, 1, rows, wide), jax.ShapeDtypeStruct((rows, wide), F32)
+
+
+def scatter(partial, sizes, collective_id):
+    split, out = scatter_shapes(partial, sizes)
     return pl.pallas_call(
-        functools.partial(scatters_kernel, sizes, count),
-        out_shape=[jax.ShapeDtypeStruct((rows, wide), F32)] * count,
-        in_specs=[VMEM] * count,
-        out_specs=[VMEM] * count,
-        scratch_shapes=scatter_scratch(sizes, False, rows, wide) * count,
+        functools.partial(scatter_kernel, sizes),
+        out_shape=out,
+        in_specs=[VMEM],
+        out_specs=VMEM,
+        scratch_shapes=scatter_scratch(sizes, False, *out.shape),
         compiler_params=pltpu.CompilerParams(collective_id=collective_id, has_side_effects=True, vmem_limit_bytes=VMEM_LIMIT),
-    )(*[partial.reshape(na, nb, nl, 1, rows, wide) for partial in partials])
-
-
-def scatter_pair(p, q, sizes, first_id, second_id):
-    if p.size <= 2048 * 2048:
-        return scatter([p, q], sizes, first_id)
-    return scatter([p], sizes, first_id) + scatter([q], sizes, second_id)
+    )(split)
+
+
+def fits(partial):
+    return partial.size <= 2048 * 2048
+
+
+def each_tile(wide, tile, body):
+    @pl.loop(0, wide // tile)
+    def _(i):
+        body(pl.ds(pl.multiple_of(i * tile, tile), tile))
+
+
+def back_steps(dg, du, wg, wu, sgu, dsgu, back_ref, dx_o, scratch):
+    *bufs, row_buf, stage, load_sem, out_sem = scratch
+    dg_v, du_v, wg_v, wu_v, sgu_v, dsgu_v = bufs
+    steps, toks, slots = back_ref.shape
+    width = wg.shape[0]
+    loads = [
+        pltpu.make_async_copy(src, dst, load_sem.at[i])
+        for i, (src, dst) in enumerate(zip((dg, du, wg, wu, sgu, dsgu), bufs))
+    ]
+    for load in loads:
+        load.start()
+    yield
+    for load in loads:
+        load.wait()
+
+    def out_copy(t):
+        return pltpu.make_async_copy(stage.at[t % 2], dx_o.at[pl.ds(t * toks, toks)], out_sem.at[t % 2])
+
+    for t in range(steps):
+        mine, theirs = pl.ds(t * slots, slots), pl.ds(t * toks, toks)
+
+        @functools.partial(each_tile, width, 512)
+        def _(cols):
+            rows = dot_nt(dg_v[mine, :], wg_v[cols, :]) + dot_nt(du_v[mine, :], wu_v[cols, :])
+            row_buf[:, cols] = rows.astype(BF16)
+
+        yield
+        if t >= 2:
+            out_copy(t - 2).wait()
+
+        @functools.partial(each_tile, width, 512)
+        def _(cols):
+            total = dot(back_ref[t], row_buf[:, cols]) + dot_nt(dsgu_v[theirs, :], sgu_v[cols, :])
+            stage[t % 2, :, cols] = total.astype(BF16)
+
+        out_copy(t).start()
+        yield
+    for t in range(max(steps - 2, 0), steps):
+        out_copy(t).wait()
+
+
+def back_kernel(sizes, scattered, *refs):
+    ins, refs = refs[: 7 + scattered], refs[7 + scattered :]
+    outs, scratch = refs[: 1 + scattered], refs[1 + scattered :]
+    programs = [back_steps(*ins[:7], outs[0], scratch[:10])]
+    if scattered:
+        g = Grid(sizes)
+        g.greet_neighbours(False)
+        programs.insert(0, scattering(g, False, ins[7], outs[1], scratch[10:]))
+    run_steps(*programs)
+
+
+def back_rows(dg, du, wg, wu, sgu, dsgu, back, partial, sizes, first_id):
+    steps, toks, slots = back.shape
+    width, ffe = wg.shape
+    together = fits(partial)
+    split, total = scatter_shapes(partial, sizes)
+    params = {"collective_id": first_id, "has_side_effects": True} if together else {}
+    sources = (dg, du, wg, wu, sgu, dsgu)
+    out = pl.pallas_call(
+        functools.partial(back_kernel, sizes, int(together)),
+        out_shape=[jax.ShapeDtypeStruct((steps * toks, width), BF16)] + [total] * together,
+        in_specs=[ANY] * 6 + [VMEM] + [VMEM] * together,
+        out_specs=[ANY] + [VMEM] * together,
+        scratch_shapes=[pltpu.VMEM(source.shape, BF16) for source in sources]
+        + [pltpu.VMEM((slots, width), BF16), pltpu.VMEM((2, toks, width), BF16), DMA((6,)), DMA((2,))]
+        + (scatter_scratch(sizes, False, *total.shape) if together else []),
+        compiler_params=pltpu.CompilerParams(vmem_limit_bytes=VMEM_LIMIT, **params),
+    )(*sources, back, *([split] if together else []))
+    return out if together else (out[0], scatter(partial, sizes, first_id))
 
 
 def shared_steps(g, part, blocks, own, other, sems):
@@ -797,33 +948,52 @@
 
 
 def across_steps(g, blocks, outs, sem):
-    def send(i, step):
-        return remote(blocks.at[i, step - 1], outs.at[i, step - 1], (sem.at[0, i, step - 1], sem.at[1, i, step - 1]), g.to("l", step))
-
-    count = blocks.shape[0]
-    for i in range(count):
-        for step in range(1, g.nl):
-            send(i, step).start()
-        yield
-        yield
-    for i in range(count):
-        for step in range(1, g.nl):
-            send(i, step).wait()
-
-
-def outputs_kernel(sizes, p_ref, shared_ref, cross_ref, o_ref, blocks_ref, cross_o, own, other, *scratch):
+    def send(step):
+        return remote(blocks.at[step - 1], outs.at[step - 1], (sem.at[0, step - 1], sem.at[1, step - 1]), g.to("l", step))
+
+    for step in range(1, g.nl):
+        send(step).start()
+    yield
+    for step in range(1, g.nl):
+        send(step).wait()
+
+
+def outputs_kernel(sizes, normed, grads, mixed, gh, small, shared_ref, cross_ref, o_ref, blocks_ref, cross_o, p_buf, own, other, *scratch):
     g = Grid(sizes)
+    na, nb, nl, ns = sizes
     g.greet_plane(True)
+    rows = p_buf.shape[4]
+    chunk = nb * nl * ns * rows
+    left = grads.shape[1]
+
+    def prepare(a):
+        at = pl.ds(pl.multiple_of(a * chunk, chunk), chunk)
+
+        def store(value, cols):
+            value = value.astype(BF16)
+            for n in range(nb * nl * ns):
+                b, l, s = n // (nl * ns), n // ns % nl, n % ns
+                p_buf[a, b, l, s, :, cols] = value[n * rows : (n + 1) * rows]
+
+        for base, one, two in ((0, normed, grads), (left, mixed, gh)):
+            tile = 512
+            @pl.loop(0, two.shape[1], step=tile)
+            def _(c):
+                c = pl.multiple_of(c, tile)
+                store(dot_tn(one[:, at], two[:, pl.ds(c, tile)]), pl.ds(pl.multiple_of(base + c, 128), tile))
+        store(small[at, :], pl.ds(left + gh.shape[1], small.shape[1]))
+
     run_steps(
-        scattering(g, True, p_ref, o_ref, scratch[4:]),
+        scattering(g, True, p_buf, o_ref, scratch[4:], prepare),
         shared_steps(g, shared_ref, blocks_ref, own, other, scratch[:3]),
         across_steps(g, cross_ref, cross_o, scratch[3]),
     )
 
 
-def outputs_scatter(partial, shared, cross, sizes, collective_id):
+def outputs_scatter(normed, grads, mixed, gh, small, shared, cross, sizes, collective_id):
     na, nb, nl, ns = sizes
-    rows, wide = partial.shape[0] // (na * nb * nl * ns), partial.shape[1]
+    rows = normed.shape[1] // (na * nb * nl * ns)
+    wide = grads.shape[1] + gh.shape[1] + small.shape[1]
     shared = shared.reshape(na, nb, nl, ns, -1, shared.shape[1])
     shape = jax.ShapeDtypeStruct
     return pl.pallas_call(
@@ -833,104 +1003,152 @@
             shape((na, nb, nl, *shared.shape[4:]), BF16),
             shape(cross.shape, BF16),
         ],
-        in_specs=[VMEM] + [ANY] * 2,
+        in_specs=[VMEM] * 5 + [ANY] * 2,
         out_specs=[VMEM] + [ANY] * 2,
         scratch_shapes=[
+            pltpu.VMEM((na, nb, nl, ns, rows, wide), BF16),
             pltpu.VMEM((na, nb, nl, *shared.shape[4:]), BF16),
             pltpu.VMEM((ns - 1, na, nb, nl, *shared.shape[4:]), BF16),
             DMA((2, ns - 1)),
             DMA((2, na * nb * nl - 1)),
             DMA((2,)),
-            DMA((2, 3, nl - 1)),
+            DMA((2, nl - 1)),
         ]
         + scatter_scratch(sizes, True, rows, wide),
         compiler_params=pltpu.CompilerParams(collective_id=collective_id, has_side_effects=True, vmem_limit_bytes=VMEM_LIMIT),
-    )(partial.reshape(na, nb, nl, ns, rows, wide), shared, cross)
-
-
-def weights_kernel(sizes, gp, inner, xr, dg, du, own_o, cross_o, send, recv, own_buf, cross_buf, s_sem, c_sem):
-    g = Grid(sizes)
-    na, nb, nl, ns = sizes
-    for step in range(1, ns):
-        g.hello(g.to("s", step))
-    pl.semaphore_wait(pltpu.get_barrier_semaphore(), ns - 1)
-    rows, ffe = own_buf.shape[1:]
-    jobs = ((xr, dg), (xr, du), (gp, inner))
+    )(normed, grads, mixed, gh, small, shared, cross)
+
+
+def weight_steps(g, gp, inner, xr, dg, du, own_os, cross_os, crossed_o, scratch):
+    left_buf, right_buf, send, recv, own_buf, cross_buf, load_sem, s_sem, c_sem, l_sem = scratch
+    na, nb, nl, ns = g.sizes
+    rows, ffe = own_buf.shape
+    lefts, rights = (xr, xr, gp), (dg, du, inner)
+
+    def load_left(i):
+        return pltpu.make_async_copy(lefts[i], left_buf, load_sem.at[0])
+
+    def load_right(i):
+        return pltpu.make_async_copy(rights[i], right_buf.at[i % 2], load_sem.at[1 + i % 2])
 
     def product(i, l, s, out):
-        left, right = jobs[i]
         at = (l * ns + s) * rows
-        step = 256 if rows % 256 == 0 else rows
+        step = 256
 
         @pl.loop(0, rows, step=step)
         def _(r):
             cols = pl.ds(pl.multiple_of(at + r, step), step)
-            for to, tile in column_tiles(ffe, 256):
-                value = dot_tn(left[:, cols], right[:, pl.ds(to, tile)])
+            for to, tile in column_tiles(ffe, 512):
+                value = dot_tn(left_buf[:, cols], right_buf[i % 2, :, pl.ds(to, tile)])
                 out[pl.ds(pl.multiple_of(r, step), step), pl.ds(to, tile)] = value.astype(out.dtype)
 
     def aside(i, turn, step):
-        return remote(send.at[i % 2, turn, step - 1], recv.at[i, turn, step - 1], (s_sem.at[0, i, turn, step - 1], s_sem.at[1, i, turn, step - 1]), g.to("s", step))
+        return remote(send.at[turn, step - 1], recv.at[i, turn, step - 1], (s_sem.at[0, i, turn, step - 1], s_sem.at[1, i, turn, step - 1]), g.to("s", step))
 
     def keep(i):
-        return [pltpu.make_async_copy(own_buf.at[i % 2], own_o.at[i], c_sem.at[i, 0])] + [
-            pltpu.make_async_copy(cross_buf.at[i % 2, turn - 1], cross_o.at[i, turn - 1], c_sem.at[i, turn])
+        return [pltpu.make_async_copy(own_buf, own_os[i], c_sem.at[i, 0])] + [
+            pltpu.make_async_copy(cross_buf.at[turn - 1], cross_os[i].at[turn - 1], c_sem.at[i, turn])
             for turn in range(1, nl)
         ]
 
+    def over(step):
+        return remote(cross_os[0].at[step - 1], crossed_o.at[step - 1], (l_sem.at[0, step - 1], l_sem.at[1, step - 1]), g.to("l", step))
+
     def sums(i):
         for turn in range(nl):
-            out = cross_buf.at[i % 2, turn - 1] if turn else own_buf.at[i % 2]
+            out = cross_buf.at[turn - 1] if turn else own_buf
             for step in range(1, ns):
                 came(g, s_sem.at[1, i, turn, step - 1], recv.at[i, turn, step - 1])
             add_rows(out, out, *[recv.at[i, turn, step] for step in range(ns - 1)])
         for copy in keep(i):
             copy.start()
 
+    def kept(i):
+        for copy in keep(i):
+            copy.wait()
+        if i == 0:
+            for step in range(1, nl):
+                over(step).start()
+
+    load_left(0).start()
+    load_right(0).start()
+    load_right(1).start()
+    yield
+    load_left(0).wait()
     for i in range(3):
+        load_right(i).wait()
+        if i == 2:
+            load_left(2).wait()
         for turn in range(nl):
             for step in range(1, ns):
-                if i >= 2:
-                    aside(i - 2, turn, step).wait_send()
-                product(i, g.other("l", turn), g.other("s", step), send.at[i % 2, turn, step - 1])
+                if i >= 1:
+                    aside(i - 1, turn, step).wait_send()
+                product(i, g.other("l", turn), g.other("s", step), send.at[turn, step - 1])
                 aside(i, turn, step).start()
+        yield
         if i >= 1:
             sums(i - 1)
-        if i >= 2:
-            for copy in keep(i - 2):
-                copy.wait()
+            kept(i - 1)
         for turn in range(nl):
-            product(i, g.other("l", turn), g.s, cross_buf.at[i % 2, turn - 1] if turn else own_buf.at[i % 2])
+            product(i, g.other("l", turn), g.s, cross_buf.at[turn - 1] if turn else own_buf)
+        if i == 0:
+            load_right(2).start()
+        if i == 1:
+            load_left(2).start()
+        yield
     sums(2)
-    for i in range(1, 3):
-        for copy in keep(i):
-            copy.wait()
-        for turn in range(nl):
-            for step in range(1, ns):
-                aside(i, turn, step).wait_send()
-
-
-def expert_weights(gp, inner, xr, dg, du, sizes, collective_id):
+    kept(2)
+    yield
+    for step in range(1, nl):
+        over(step).wait()
+    for turn in range(nl):
+        for step in range(1, ns):
+            aside(2, turn, step).wait_send()
+
+
+def weights_kernel(sizes, scattered, *refs):
+    g = Grid(sizes)
+    g.greet_neighbours(True)
+    ins, refs = refs[: 5 + scattered], refs[5 + scattered :]
+    outs, scratch = refs[: 7 + scattered], refs[7 + scattered :]
+    programs = [weight_steps(g, *ins[:5], outs[:3], outs[3:6], outs[6], scratch[:10])]
+    if scattered:
+        programs.insert(0, scattering(g, False, ins[5], outs[7], scratch[10:]))
+    run_steps(*programs)
+
+
+def expert_weights(gp, inner, xr, dg, du, partial, sizes, first_id, second_id):
     na, nb, nl, ns = sizes
     rows, ffe = gp.shape[1] // (nl * ns), inner.shape[1]
-    return pl.pallas_call(
-        functools.partial(weights_kernel, sizes),
+    together = fits(partial)
+    split, total = scatter_shapes(partial, sizes)
+    shape = jax.ShapeDtypeStruct
+    out = pl.pallas_call(
+        functools.partial(weights_kernel, sizes, int(together)),
         out_shape=[
-            jax.ShapeDtypeStruct((3, rows, ffe), F32),
-            jax.ShapeDtypeStruct((3, nl - 1, rows, ffe), BF16),
-        ],
-        in_specs=[VMEM] * 5,
-        out_specs=[ANY] * 2,
+            *[shape((rows, ffe), F32)] * 3,
+            *[shape((nl - 1, rows, ffe), BF16)] * 4,
+        ]
+        + [total] * together,
+        in_specs=[ANY] * 5 + [VMEM] * together,
+        out_specs=[ANY] * 7 + [VMEM] * together,
         scratch_shapes=[
-            pltpu.VMEM((2, nl, ns - 1, rows, ffe), BF16),
+            pltpu.VMEM(gp.shape, BF16),
+            pltpu.VMEM((2, *inner.shape), BF16),
+            pltpu.VMEM((nl, ns - 1, rows, ffe), BF16),
             pltpu.VMEM((3, nl, ns - 1, rows, ffe), BF16),
-            pltpu.VMEM((2, rows, ffe), F32),
-            pltpu.VMEM((2, nl - 1, rows, ffe), BF16),
+            pltpu.VMEM((rows, ffe), F32),
+            pltpu.VMEM((nl - 1, rows, ffe), BF16),
+            DMA((3,)),
             DMA((2, 3, nl, ns - 1)),
             DMA((3, nl)),
-        ],
-        compiler_params=pltpu.CompilerParams(collective_id=collective_id, has_side_effects=True, vmem_limit_bytes=VMEM_LIMIT),
-    )(gp, inner, xr, dg, du)
+            DMA((2, nl - 1)),
+        ]
+        + (scatter_scratch(sizes, False, *total.shape) if together else []),
+        compiler_params=pltpu.CompilerParams(collective_id=first_id, has_side_effects=True, vmem_limit_bytes=VMEM_LIMIT),
+    )(gp, inner, xr, dg, du, *([split] if together else []))
+    own, (_, second, third, crossed) = out[:3], out[3:7]
+    return own, crossed, second, third, out[7] if together else scatter(partial, sizes, second_id)
 
 
 def rms_norm(values, gain_row):
@@ -976,30 +1194,26 @@
     return [(at, min(tile, wide - at)) for at in range(0, wide, tile)]
 
 
-def moe_kernel(seqs, experts, x_ref, dy_ref, pick_ref, back_ref, router_ref, wg_ref, wu_ref, wd_ref, sgu_ref, sd_ref,
-               xr_ref, gp_ref, inner_ref, dg_ref, du_ref, share_ref, dsgu_ref, out_ref, dx_ref, gg_ref,
+def moe_kernel(x_ref, dy_ref, pick_ref, back_ref, router_ref, wg_ref, wu_ref, wd_ref, sgu_ref, sd_ref,
+               xr_ref, gp_ref, inner_ref, dg_ref, du_ref, share_ref, dsgu_ref, out_ref, gg_ref,
                g_buf, u_buf, dyr_buf, gate_buf, sum_buf, mm_buf):
-    length = x_ref.shape[0] // seqs
-    cap = xr_ref.shape[0] // seqs
-    width = x_ref.shape[1]
+    toks, width = x_ref.shape
     ffe = wg_ref.shape[1]
     narrow = sd_ref.shape[0]
-    lane = lax.broadcasted_iota(jnp.int32, (length, 128), 1)
+    lane = lax.broadcasted_iota(jnp.int32, (toks, 128), 1)
     mine = (lax.axis_index(PLANE) == lane).astype(F32)
 
-    for n in range(seqs):
-        toks, slots = pl.ds(n * length, length), pl.ds(n * cap, cap)
-        x = x_ref[toks, :]
-        dy = dy_ref[toks, pl.ds(0, width)]
-        xr_ref[slots, :] = dot(pick_ref[n], x).astype(BF16)
-        dyr_buf[slots, :] = dot(pick_ref[n], dy).astype(BF16)
-        hot = dy_ref[toks, pl.ds(width, 128)].astype(F32)
-        logits = jnp.where(hot > 0, dot(x, router_ref[...]), -1e30)
-        top = jnp.max(logits, axis=1, keepdims=True)
-        raised = jnp.exp(logits - top)
-        gate = jnp.sum(raised * mine, axis=1, keepdims=True) / jnp.sum(raised, axis=1, keepdims=True)
-        gate = jnp.broadcast_to(gate, (length, 128))
-        gate_buf[slots, :] = exact(pick_ref[n].astype(F32), gate, ((1,), (0,)))
+    hot = dy_ref[:, pl.ds(width, 128)].astype(F32)
+    logits = jnp.where(hot > 0, dot(x_ref[...], router_ref[...]), -1e30)
+    top = jnp.max(logits, axis=1, keepdims=True)
+    raised = jnp.exp(logits - top)
+    gate = jnp.sum(raised * mine, axis=1, keepdims=True) / jnp.sum(raised, axis=1, keepdims=True)
+    gate = jnp.broadcast_to(gate, (toks, 128))
+    gate_buf[...] = exact(pick_ref[...].astype(F32), gate, ((1,), (0,)))
+    for at, tile in column_tiles(width, 512):
+        cols = pl.ds(at, tile)
+        xr_ref[:, cols] = dot(pick_ref[...], x_ref[:, cols]).astype(BF16)
+        dyr_buf[:, cols] = dot(pick_ref[...], dy_ref[:, cols]).astype(BF16)
 
     for at, tile in column_tiles(ffe, 256):
         cols = pl.ds(at, tile)
@@ -1021,15 +1235,15 @@
         produced = dot_nt(inner_ref[...], wd_ref[cols, :])
         dyr = dyr_buf[:, cols].astype(F32)
         gate = gate_buf[:, pl.ds(0, 1)]
-        sum_buf[...] += jnp.broadcast_to(jnp.sum(produced * dyr, axis=1, keepdims=True), sum_buf.shape)
+        for half in range(0, tile, 128):
+            sum_buf[...] += produced[:, half : half + 128] * dyr[:, half : half + 128]
         gp_ref[:, cols] = (gate * dyr).astype(BF16)
-        mm_buf[...] = (gate * produced).astype(BF16)
-        for n in range(seqs):
-            toks, slots = pl.ds(n * length, length), pl.ds(n * cap, cap)
-            out_ref[toks, cols] = (dot(back_ref[n], mm_buf[slots, :]) + dot(share_ref[toks, :], sd_ref[:, cols])).astype(BF16)
-    for n in range(seqs):
-        slots = pl.ds(n * cap, cap)
-        gg_ref[n] = exact(sum_buf[slots, :], pick_ref[n].astype(F32), ((0,), (0,)))[:8]
+        mm_buf[:, cols] = (gate * produced).astype(BF16)
+    for at, tile in column_tiles(width, 256):
+        cols = pl.ds(at, tile)
+        out_ref[:, cols] = (dot(back_ref[...], mm_buf[:, cols]) + dot(share_ref[...], sd_ref[:, cols])).astype(BF16)
+    total = jnp.broadcast_to(jnp.sum(sum_buf[...], axis=1, keepdims=True), sum_buf.shape)
+    gg_ref[0] = exact(total, pick_ref[...].astype(F32), ((0,), (0,)))[:8]
 
     for at, tile in column_tiles(ffe, 256):
         cols = pl.ds(at, tile)
@@ -1038,20 +1252,11 @@
         sig, act = silu_parts(g)
         dg_ref[:, cols] = (d_inner * u * sig * (1.0 + g * (1.0 - sig))).astype(BF16)
         du_ref[:, cols] = (d_inner * act).astype(BF16)
-    for at, tile in column_tiles(width, 256):
-        cols = pl.ds(at, tile)
-        rows = dot_nt(dg_ref[...], wg_ref[cols, :]) + dot_nt(du_ref[...], wu_ref[cols, :])
-        mm_buf[...] = rows.astype(BF16)
-        for n in range(seqs):
-            toks, slots = pl.ds(n * length, length), pl.ds(n * cap, cap)
-            dx_ref[toks, cols] = (dot(back_ref[n], mm_buf[slots, :]) + dot_nt(dsgu_ref[toks, :], sgu_ref[cols, :])).astype(BF16)
-
-
-def moe(x_all, wide_dy, pick, router, wg, wu, wd, sgu, sd, experts, length, cap, steps):
-    total = x_all.shape[0] // length
-    seqs = total // steps
+
+
+def moe(x_all, wide_dy, pick, back, router, wg, wu, wd, sgu, sd):
+    steps, slots, toks = pick.shape
     width, ffe, narrow = x_all.shape[1], wg.shape[1], sd.shape[0]
-    toks, slots = seqs * length, seqs * cap
     shape = jax.ShapeDtypeStruct
 
     def rows(count, wide):
@@ -1064,13 +1269,13 @@
         return shape((steps * count, wide), BF16)
 
     return pl.pallas_call(
-        functools.partial(moe_kernel, seqs, experts),
+        moe_kernel,
         grid=(steps,),
         in_specs=[
             rows(toks, width),
             rows(toks, wide_dy.shape[1]),
-            pl.BlockSpec((seqs, cap, length), lambda i: (i, 0, 0)),
-            pl.BlockSpec((seqs, length, cap), lambda i: (i, 0, 0)),
+            pl.BlockSpec((None, slots, toks), lambda i: (i, 0, 0)),
+            pl.BlockSpec((None, toks, slots), lambda i: (i, 0, 0)),
             *[whole(w) for w in (router, wg, wu, wd, sgu, sd)],
         ],
         out_specs=[
@@ -1082,8 +1287,7 @@
             rows(toks, narrow),
             rows(toks, 2 * narrow),
             rows(toks, width),
-            rows(toks, width),
-            pl.BlockSpec((seqs, 8, length), lambda i: (i, 0, 0)),
+            pl.BlockSpec((1, 8, toks), lambda i: (i, 0, 0)),
         ],
         out_shape=[
             out(slots, width),
@@ -1094,8 +1298,7 @@
             out(toks, narrow),
             out(toks, 2 * narrow),
             out(toks, width),
-            out(toks, width),
-            shape((total, 8, length), F32),
+            shape((steps, 8, toks), F32),
         ],
         scratch_shapes=[
             pltpu.VMEM((slots, ffe), F32),
@@ -1103,11 +1306,11 @@
             pltpu.VMEM((slots, width), BF16),
             pltpu.VMEM((slots, 128), F32),
             pltpu.VMEM((slots, 128), F32),
-            pltpu.VMEM((slots, 256), BF16),
+            pltpu.VMEM((slots, width), BF16),
         ],
         compiler_params=pltpu.CompilerParams(vmem_limit_bytes=VMEM_LIMIT),
         cost_estimate=pl.CostEstimate(flops=6 * 10**10, bytes_accessed=10**8, transcendentals=0),
-    )(x_all, wide_dy, pick, pick.transpose(0, 2, 1), router, wg, wu, wd, sgu, sd)
+    )(x_all, wide_dy, pick, back, router, wg, wu, wd, sgu, sd)
 
 
 def shards(
@@ -1151,10 +1354,11 @@
     shared = jnp.stack([shared_gate, shared_up]).reshape(2, shared_gate.shape[0], *sizes[:3], -1)
     sh_rows = shared_down.shape[0]
     sh_pad = -sh_rows % 16
-    dense, dy_all, (wg, wu, wd), columns, downs = inputs_gather(
+    dense, dy_all, wg, wu, columns, downs = inputs_gather(
         jnp.concatenate([w_query, w_key, w_value, w_out, small], axis=1),
         wide_dy,
-        (expert_gate, expert_up, expert_down),
+        expert_gate,
+        expert_up,
         shared.transpose(2, 3, 4, 0, 1, 5),
         jnp.pad(shared_down, ((0, sh_pad), (0, 0))),
         sizes,
@@ -1203,22 +1407,34 @@
     normed_moe, moe_norm_pull = jax.vjp(rms_norm, hidden, moe_gain)
     moe_low = normed_moe.astype(BF16)
 
-    x_all = gather(moe_low, sizes, 2)
+    x_all, wd = gather(moe_low, expert_down, sizes, 2)
     seqs = groups
     mine = jnp.any(hot_all & (jnp.arange(experts_total)[None, :] == my_expert), axis=1)
     mine = mine.reshape(seqs, length)
     hits = mine.astype(jnp.int32)
     before = jnp.cumsum(hits, axis=1) - hits
     slot_hot = (jnp.arange(capacity)[None, :, None] == before[:, None, :]) & mine[:, None, :]
-    x_rows, gp, inner_low, dg, du, share_low, dsgu, part, dx_part, gate_grad = moe(
-        x_all, dy_all, slot_hot.astype(BF16), lane_pad(router_full), wg, wu, wd, sgu, sd_w,
-        experts_total, length, capacity, max(seqs // 4, 1),
-    )
-    gate_grad = lax.all_to_all(gate_grad[:, 0], PLANE, split_axis=0, concat_axis=0, tiled=True)
+    together = min(seqs, 4)
+    slot_hot = slot_hot.reshape(-1, together, capacity, 1, length)
+    slot_hot = slot_hot & jnp.eye(together, dtype=bool)[None, :, None, :, None]
+    slot_hot = slot_hot.reshape(-1, together * capacity, together * length).astype(BF16)
+    token_hot = slot_hot.transpose(0, 2, 1)
+    x_rows, gp, inner_low, dg, du, share_low, dsgu, part, gate_grad = moe(
+        x_all, dy_all, slot_hot, token_hot, lane_pad(router_full), wg, wu, wd, sgu, sd_w
+    )
+    gate_grad = gate_grad[:, 0].reshape(seqs, length)
+    gate_grad = lax.all_to_all(gate_grad, PLANE, split_axis=0, concat_axis=0, tiled=True)
     dy_all = dy_all[:, :width]
-    moe_out, dx = scatter_pair(part, dx_part, sizes, 3, 6)
+    dx_part, moe_out = back_rows(dg, du, wg, wu, sgu, dsgu, token_hot, part, sizes, 3)
+    own_experts, cross_gate, cross_up, cross_down, dx = expert_weights(
+        gp, inner_low, x_rows, dg, du, dx_part, sizes, 4, 6
+    )
+    ranks = sizes[2]
+    cross_up = [
+        lax.ppermute(cross_up[step - 1], "l", [(i, (i + step) % ranks) for i in range(ranks)])
+        for step in range(1, ranks)
+    ]
     output = (hidden + moe_out).astype(BF16)
-    own_experts, cross_experts = expert_weights(gp, inner_low, x_rows, dg, du, sizes, 4)
     shared_grads = dot_tn(x_all, dsgu).astype(BF16)
     grad_shared_down = lax.psum_scatter(
         dot_tn(share_low[:, :narrow], dy_all), "s", scatter_dimension=0, tiled=True
@@ -1237,7 +1453,6 @@
     grad_hidden = cotangent.astype(F32) + grad_hidden_norm
 
     grad_hidden_low = grad_hidden.astype(BF16)
-    grad_out_proj = dot_tn(mixed_low, grad_hidden_low)
     grad_mixed = (
         dot_nt(grad_hidden_low, out_full)
         .astype(BF16)
@@ -1271,17 +1486,18 @@
         [grad_router, grad_gain_attn[:, None], grad_gain_moe[:, None]], axis=1
     )
     grad_small = lane_pad(grad_small)
-    dense_grads = jnp.concatenate(
-        [
-            dot_tn(normed_low, grad_query_low).astype(BF16),
-            dot_tn(normed_low, grad_key_low).astype(BF16),
-            dot_tn(normed_low, grad_value_low).astype(BF16),
-            grad_out_proj.astype(BF16),
-            grad_small.astype(BF16),
-        ],
-        axis=1,
-    )
-    total, blocks, cross = outputs_scatter(dense_grads, shared_grads, cross_experts, sizes, 5)
+    grad_small, cross_up = lax.optimization_barrier((grad_small, cross_up))
+    total, blocks, cross_down = outputs_scatter(
+        normed_low,
+        jnp.concatenate([grad_query_low, grad_key_low, grad_value_low], axis=1),
+        mixed_low,
+        grad_hidden_low,
+        grad_small,
+        shared_grads,
+        cross_down,
+        sizes,
+        5,
+    )
     dense_sum, small_sum = total[:, :-128], total[:, -128:]
     blocks = blocks.reshape(groups, *blocks.shape[3:]).transpose(1, 0, 2).astype(F32)
     half = blocks.shape[2] // 2
@@ -1289,12 +1505,12 @@
     grad_shared_up = blocks[:, :, half : half + narrow].reshape(blocks.shape[0], -1)
     my_l = lax.axis_index("l")
     expert_grads = []
-    for i in range(3):
+    for grad, cross in zip(own_experts, (cross_gate, cross_up, cross_down)):
         here = jnp.arange(local_experts)[:, None, None]
-        grad = own_experts[i][None]
+        grad = grad[None]
         for step in range(1, local_experts):
             from_l = (my_l - step) % local_experts
-            grad = jnp.where(here == from_l, cross[i, step - 1].astype(F32)[None], grad)
+            grad = jnp.where(here == from_l, cross[step - 1].astype(F32)[None], grad)
         expert_grads.append(grad)
     return (
         output,

time: 1030 us -> 899 us (0.87)
  Pallas kernels: 798 us -> 702 us
  local copies, waits for them, and re-layouts: 79.1 us -> 58.2 us
  matrix products: 82.2 us -> 65 us
    pallas_call x1, Pallas kernels: 186 us -> 145 us  [outputs_scatter(): pl.pallas_call(functools.partial(outputs_kernel, sizes), out_shape=[shape...]
    pallas_call x1, Pallas kernels: 217 us -> 186 us  [inputs_gather(): pl.pallas_call(functools.partial(inputs_kernel, sizes), out_shape=[shape(...]
    pallas_call x4, Pallas kernels: 396 us -> 371 us  [the longest x1 127 us: expert_weights(): pl.pallas_call(functools.partial(weights_kernel, sizes, int(together)), o...]
    concatenate x1, local copies, waits for them, and re-layouts: 26.2 us -> 2.25 us  [shards(): jnp.concatenate([grad_router, grad_gain_attn[:, None], grad_gain_moe[:, N...]
    dot_general x7 -> x3, matrix products: 32.6 us -> 17 us  [dot_tn(): lax.dot_general(left, right, (((0,), (0,)), ((), ())), preferred_element_...]
  transfers between devices with their start and end apart: 2 -> 3, of which waited for: 0 -> 0; matrix products, arithmetic and copies ran while one was open for 15% -> 12% of each run, Pallas kernels for 38% -> 42%
where the time goes in v3:
time: 899 us; the launch traced here: 888 us
  Pallas kernels  702 us (78%)
  matrix products  65 us (7%)
  local copies, waits for them, and re-layouts  58.2 us (6%)
  other arithmetic  42.6 us (5%)
  between operations  15.1 us (2%)
    pallas_call x1, Pallas kernels, inputs_gather(): pl.pallas_call(functools.partial(inputs_kernel, sizes), out_shape=[shape(...  186 us
    pallas_call x1, Pallas kernels, outputs_scatter(): pl.pallas_call(functools.partial(outputs_kernel, sizes), out_shape=[shape...  145 us
    pallas_call x1, Pallas kernels, expert_weights(): pl.pallas_call(functools.partial(weights_kernel, sizes, int(together)), o...  127 us
    pallas_call x1, Pallas kernels, back_rows(): pl.pallas_call(functools.partial(back_kernel, sizes, int(together)), out_...  99.1 us
    pallas_call x1, Pallas kernels, gather(): pl.pallas_call(functools.partial(gather_kernel, sizes), out_shape=[jax.Sh...  80.4 us
    pallas_call x1, Pallas kernels, moe(): pl.pallas_call(moe_kernel, grid=(steps,), in_specs=[rows(toks, width), ro...  64.2 us
    dot_general x5, matrix products, dot_nt(): lax.dot_general(left, right, (((1,), (1,)), ((), ())), preferred_element_...  23.8 us
  transfers between devices with their start and end apart: 3, of which 0 were waited for; matrix products, arithmetic and copies ran while one was open for 12% of the time, Pallas kernels for 42%

profile of v3, /device:TPU:0, one launch (start us, length us, event | category | flops | bytes accessed | tf_op | source)
XLA Modules:
  0.0 887.8 jit_solution(460943976893966292)
XLA Ops:
  19.5 186.1 %shard_map.280 = (bf16[4,2,2,2,64,5248]{5,4,3,2,1,0:T(8,128)(2,1)}, bf16[4,2,2,1,128,2176]{5,4,3,2,1,0:T(8,128)(2,1)}, bf16[2,2,512,1408]{3,2,1,0:T(8,128)(2,1)}...) custom-call(bf16[64,5248]{1,0:T(8,128)(2,1)} %copy-done.14, ...), custom_call_target="tpu_custom_call" | custom-call | tf_op jit(solution)/shard_map/pallas_call | solution.py:515
  210.3 4.6 fusion.27
  225.5 4.9 multiply_reduce_fusion.3
  242.6 2.7 fusion.72
  247.4 80.4 %shard_map.281 = (bf16[4,2,2,1,128,2048]{5,4,3,2,1,0:T(8,128)(2,1)}, bf16[2,2,512,1408]{3,2,1,0:T(8,128)(2,1)}) custom-call(bf16[128,2048]{1,0:T(8,128)(2,1)} %multiply_convert_fusion.1.x_ref, bf16[2,512,1408]{2,1,0:T(8,128)(2,1)} %shard.1), custom_call_target="tpu_custom_call" | custom-call | tf_op jit(solution)/shard_map/pallas_call | solution.py:368
  327.7 3.0 fusion.19.sgu_ref.refs_4_
  330.7 64.2 %shard_map.282 = (bf16[1024,2048]{1,0:T(8,128)(2,1)}, bf16[1024,2048]{1,0:T(8,128)(2,1)}, bf16[1024,1408]{1,0:T(8,128)(2,1)}, bf16[1024,1408]{1,0:T(8,128)(2,1)}...) custom-call(bf16[2048,2048]{1,0:T(8,128)(2,1)} %bitcast.208, ...), custom_call_target="tpu_custom_call" | custom-call | flops 60000002048 | bytes 100000000 | tf_op jit(solution)/shard_map/pallas_call | solution.py:1271
  396.4 3.8 all-to-all-start
  400.2 99.1 %shard_map.283 = (bf16[2048,2048]{1,0:T(8,128)(2,1)}, f32[128,2048]{1,0:T(8,128)}) custom-call(bf16[1024,1408]{1,0:T(8,128)(2,1)} %get-tuple-element.54.refs_0_.refs_3_, bf16[1024,1408]{1,0:T(8,128)(2,1)} %get-tuple-element.55.refs_1_.refs_4_, bf16[2048,1408]{1,0:T(8,128)(2,1)} %bitcast.152, bf16[2048,1408]{1,0:T(8,128)(2,1)} %bitcast.154, ...), custom_call_target="tpu_custom_call" | custom-call | tf_op jit(solution)/shard_map/pallas_call | solution.py:895
  499.3 127.0 %shard_map.284 = (f32[512,1408]{1,0:T(8,128)}, f32[512,1408]{1,0:T(8,128)}, f32[512,1408]{1,0:T(8,128)}, bf16[1,512,1408]{2,1,0:T(8,128)(2,1)}, bf16[1,512,1408]...) custom-call(bf16[1024,2048]{1,0:T(8,128)(2,1)} %get-tuple-element.59.refs_0_, ...), custom_call_target="tpu_custom_call" | custom-call | tf_op jit(solution)/shard_map/pallas_call | solution.py:1126
  627.1 6.2 fusion.1
  633.4 9.9 %convolution_convert_fusion = bf16[2048,512]{1,0:T(8,128)(2,1)} fusion(bf16[2048,2048]{1,0:T(8,128)(2,1)} %bitcast.209, bf16[2048,512]{1,0:T(8,128)(2,1)} %get-tuple-element.56.refs_5_), kind=kOutput, calls=%fused_computation.15 | convolution fusion | flops 4296015872 | bytes 12582912 | tf_op jit(solution)/shard_map/dot_general | solution.py:33
  644.7 3.3 bitcast_convert_fusion.1
  654.8 7.1 fusion.16
  663.9 2.9 fusion.40
  671.2 2.6 copy.190
  678.3 7.2 fusion.7
  688.5 2.9 convolution_add_fusion.1
  691.4 4.0 fusion.42
  705.3 145.4 %shard_map.285 = (f32[64,5248]{1,0:T(8,128)}, bf16[4,2,2,64,512]{4,3,2,1,0:T(8,128)(2,1)}, bf16[1,512,1408]{2,1,0:T(8,128)(2,1)}) custom-call(bf16[128,2048]{1,0:T(8,128)(2,1)} %copy-done.12, bf16[128,3072]{1,0:T(8,128)(2,1)} %pad_maximum_fusion.grads, bf16[128,2048]{1,0:T(8,128)(2,1)} %copy.181.mixed, bf16[128,2048]{1,0:T(8,128)(2,1)} %copy-done.13, ...), custom_call_target="tpu_custom_call" | custom-call | tf_op jit(solution)/shard_map/pallas_call | solution.py:999
  857.9 2.6 reshape.299
  860.5 2.8 copy.166
  863.3 2.6 reshape.300
  872.2 8.5 broadcast_select_fusion
  (212 shorter events, 88.7 us)
Async XLA Ops:
  7.2 8.6 copy-start.3
  7.2 9.4 %copy-start.31 = (bf16[64,512]{1,0:T(8,128)(2,1)S(1)}, bf16[64,512]{1,0:T(8,128)(2,1)}, u32[]{:S(2)}) copy-start(bf16[64,512]{1,0:T(8,128)(2,1)} %param.22) | copy-start | bytes 196612
  9.5 7.9 copy-start.30
  19.5 188.1 %copy-start.2 = (bf16[128,2048]{1,0:T(8,128)(2,1)S(1)}, bf16[128,2048]{1,0:T(8,128)(2,1)}, u32[]{:S(2)}) copy-start(bf16[128,2048]{1,0:T(8,128)(2,1)} %param.17) | copy-start | bytes 1572868
  207.8 7.1 copy-start.46
  207.8 7.1 copy-start.40
  208.1 6.9 copy-start.12
  223.7 6.8 copy-start.36
  230.5 6.0 copy-start.51
  230.5 5.8 copy-start.48
  396.4 253.2 %all-to-all-start = ((f32[16,1,128]{2,1,0:T(1,128)}), f32[16,1,128]{2,1,0:T(1,128)S(1)}, u32[]{:S(2)}, u32[]{:S(2)}) async-start(f32[16,1,128]{2,1,0:T(1,128)} %bitcast.26), calls=%async_computation | async-start | bytes 16384 | tf_op jit(solution)/shard_map/all_to_all | solution.py:1426
  400.2 480.5 %reduce-scatter.2.cloned.1.call-start = ((), (), s32[]{:S(2)}) async-start(), calls=%async_computation.2 | async-start | bytes 2162688 | tf_op jit(solution)/shard_map/reduce_scatter | solution.py:1439
  499.3 127.8 %copy-start.53 = (bf16[2048,256]{1,0:T(8,128)(2,1)S(1)}, bf16[2048,256]{1,0:T(8,128)(2,1)}, u32[]{:S(2)}) copy-start(bf16[2048,256]{1,0:T(8,128)(2,1)} %get-tuple-element.70) | copy-start | bytes 3145732
  626.4 79.0 %collective-permute-start = (bf16[512,1408]{1,0:T(8,128)(2,1)}, bf16[512,1408]{1,0:T(8,128)(2,1)}, u32[]{:S(2)}, u32[]{:S(2)}) collective-permute-start(bf16[512,1408]{1,0:T(8,128)(2,1)} %bitcast.211), channel_id=1, source_target_pairs={{0,2},{2,0},{1,3},{3,1},{4,6},{6,4},{5,7},{7,5},{8,10},{10,8},{9,1... | collective-permute-start | bytes 4325384 | tf_op jit(solution)/shard_map/ppermute | solution.py:1434
  633.3 9.9 %copy-start.1 = (bf16[128,2048]{1,0:T(8,128)(2,1)S(1)}, bf16[128,2048]{1,0:T(8,128)(2,1)}, u32[]{:S(2)}) copy-start(bf16[128,2048]{1,0:T(8,128)(2,1)} %multiply_convert_fusion.1.x_ref) | copy-start | bytes 1572868
  633.3 9.9 %copy-start.34 = (pred[128,16]{0,1:T(8,128)(4,1)S(1)}, pred[128,16]{0,1:T(8,128)(4,1)}, u32[]{:S(2)}) copy-start(pred[128,16]{0,1:T(8,128)(4,1)} %copy-done.33) | copy-start | bytes 6148
  643.3 5.3 copy-start.28
  654.8 9.2 %copy-start.20 = (bf16[128,4,64]{2,0,1:T(8,128)(2,1)S(1)}, bf16[128,4,64]{2,0,1:T(8,128)(2,1)}, u32[]{:S(2)}) copy-start(bf16[128,4,64]{2,0,1:T(8,128)(2,1)} %copy-done.19) | copy-start | bytes 196612
  654.8 9.2 %copy-start.23 = (bf16[128,4,64]{2,0,1:T(8,128)(2,1)S(1)}, bf16[128,4,64]{2,0,1:T(8,128)(2,1)}, u32[]{:S(2)}) copy-start(bf16[128,4,64]{2,0,1:T(8,128)(2,1)} %copy-done.22) | copy-start | bytes 196612
  695.5 5.4 copy-start.6
  698.4 5.2 copy-start.4
  698.4 5.2 copy-start.15
  698.4 5.2 copy-start.39
  698.4 5.2 copy-start.42
  (33 other events, 103.8 us)
Sparse Core Ops, SparseCore 0:
  633.5 14.8 reduce-scatter.1

commit v4 on v3

--- a/solution.py
+++ b/solution.py
@@ -1019,8 +1019,8 @@
     )(normed, grads, mixed, gh, small, shared, cross)
 
 
-def weight_steps(g, gp, inner, xr, dg, du, own_os, cross_os, crossed_o, scratch):
-    left_buf, right_buf, send, recv, own_buf, cross_buf, load_sem, s_sem, c_sem, l_sem = scratch
+def weight_steps(g, gp, inner, xr, dg, du, own_os, cross_os, scratch):
+    left_buf, right_buf, send, recv, own_buf, cross_buf, load_sem, s_sem, c_sem = scratch
     na, nb, nl, ns = g.sizes
     rows, ffe = own_buf.shape
     lefts, rights = (xr, xr, gp), (dg, du, inner)
@@ -1050,9 +1050,6 @@
             pltpu.make_async_copy(cross_buf.at[turn - 1], cross_os[i].at[turn - 1], c_sem.at[i, turn])
             for turn in range(1, nl)
         ]
-
-    def over(step):
-        return remote(cross_os[0].at[step - 1], crossed_o.at[step - 1], (l_sem.at[0, step - 1], l_sem.at[1, step - 1]), g.to("l", step))
 
     def sums(i):
         for turn in range(nl):
@@ -1066,9 +1063,6 @@
     def kept(i):
         for copy in keep(i):
             copy.wait()
-        if i == 0:
-            for step in range(1, nl):
-                over(step).start()
 
     load_left(0).start()
     load_right(0).start()
@@ -1099,8 +1093,6 @@
     sums(2)
     kept(2)
     yield
-    for step in range(1, nl):
-        over(step).wait()
     for turn in range(nl):
         for step in range(1, ns):
             aside(2, turn, step).wait_send()
@@ -1110,10 +1102,10 @@
     g = Grid(sizes)
     g.greet_neighbours(True)
     ins, refs = refs[: 5 + scattered], refs[5 + scattered :]
-    outs, scratch = refs[: 7 + scattered], refs[7 + scattered :]
-    programs = [weight_steps(g, *ins[:5], outs[:3], outs[3:6], outs[6], scratch[:10])]
+    outs, scratch = refs[: 6 + scattered], refs[6 + scattered :]
+    programs = [weight_steps(g, *ins[:5], outs[:3], outs[3:6], scratch[:9])]
     if scattered:
-        programs.insert(0, scattering(g, False, ins[5], outs[7], scratch[10:]))
+        programs.insert(0, scattering(g, False, ins[5], outs[6], scratch[9:]))
     run_steps(*programs)
 
 
@@ -1127,11 +1119,11 @@
         functools.partial(weights_kernel, sizes, int(together)),
         out_shape=[
             *[shape((rows, ffe), F32)] * 3,
-            *[shape((nl - 1, rows, ffe), BF16)] * 4,
+            *[shape((nl - 1, rows, ffe), BF16)] * 3,
         ]
         + [total] * together,
         in_specs=[ANY] * 5 + [VMEM] * together,
-        out_specs=[ANY] * 7 + [VMEM] * together,
+        out_specs=[ANY] * 6 + [VMEM] * together,
         scratch_shapes=[
             pltpu.VMEM(gp.shape, BF16),
             pltpu.VMEM((2, *inner.shape), BF16),
@@ -1142,13 +1134,11 @@
             DMA((3,)),
             DMA((2, 3, nl, ns - 1)),
             DMA((3, nl)),
-            DMA((2, nl - 1)),
         ]
         + (scatter_scratch(sizes, False, *total.shape) if together else []),
         compiler_params=pltpu.CompilerParams(collective_id=first_id, has_side_effects=True, vmem_limit_bytes=VMEM_LIMIT),
     )(gp, inner, xr, dg, du, *([split] if together else []))
-    own, (_, second, third, crossed) = out[:3], out[3:7]
-    return own, crossed, second, third, out[7] if together else scatter(partial, sizes, second_id)
+    return out[:3], *out[3:6], out[6] if together else scatter(partial, sizes, second_id)
 
 
 def rms_norm(values, gain_row):
@@ -1430,9 +1420,12 @@
         gp, inner_low, x_rows, dg, du, dx_part, sizes, 4, 6
     )
     ranks = sizes[2]
-    cross_up = [
-        lax.ppermute(cross_up[step - 1], "l", [(i, (i + step) % ranks) for i in range(ranks)])
-        for step in range(1, ranks)
+    crossing = [
+        [
+            lax.ppermute(cross[step - 1], "l", [(i, (i + step) % ranks) for i in range(ranks)])
+            for step in range(1, ranks)
+        ]
+        for cross in (cross_gate, cross_up)
     ]
     output = (hidden + moe_out).astype(BF16)
     shared_grads = dot_tn(x_all, dsgu).astype(BF16)
@@ -1486,7 +1479,7 @@
         [grad_router, grad_gain_attn[:, None], grad_gain_moe[:, None]], axis=1
     )
     grad_small = lane_pad(grad_small)
-    grad_small, cross_up = lax.optimization_barrier((grad_small, cross_up))
+    grad_small, crossing = lax.optimization_barrier((grad_small, crossing))
     total, blocks, cross_down = outputs_scatter(
         normed_low,
         jnp.concatenate([grad_query_low, grad_key_low, grad_value_low], axis=1),
@@ -1505,7 +1498,7 @@
     grad_shared_up = blocks[:, :, half : half + narrow].reshape(blocks.shape[0], -1)
     my_l = lax.axis_index("l")
     expert_grads = []
-    for grad, cross in zip(own_experts, (cross_gate, cross_up, cross_down)):
+    for grad, cross in zip(own_experts, (*crossing, cross_down)):
         here = jnp.arange(local_experts)[:, None, None]
         grad = grad[None]
         for step in range(1, local_experts):

time: 899 us -> 876 us (0.974)
  Pallas kernels: 702 us -> 679 us
    pallas_call x1, Pallas kernels: 127 us -> 98.5 us  [expert_weights(): pl.pallas_call(functools.partial(weights_kernel, sizes, int(together)), o...]
  transfers between devices with their start and end apart: 3 -> 4, of which waited for: 0 -> 0; matrix products, arithmetic and copies ran while one was open for 12% -> 12% of each run, Pallas kernels for 42% -> 40%
where the time goes in v4:
time: 876 us; the launch traced here: 866 us
  Pallas kernels  679 us (78%)
  matrix products  65.3 us (7%)
  local copies, waits for them, and re-layouts  58.1 us (7%)
  other arithmetic  42.5 us (5%)
  between operations  15.2 us (2%)
    pallas_call x1, Pallas kernels, inputs_gather(): pl.pallas_call(functools.partial(inputs_kernel, sizes), out_shape=[shape(...  186 us
    pallas_call x1, Pallas kernels, outputs_scatter(): pl.pallas_call(functools.partial(outputs_kernel, sizes), out_shape=[shape...  151 us
    pallas_call x1, Pallas kernels, back_rows(): pl.pallas_call(functools.partial(back_kernel, sizes, int(together)), out_...  99 us
    pallas_call x1, Pallas kernels, expert_weights(): pl.pallas_call(functools.partial(weights_kernel, sizes, int(together)), o...  98.5 us
    pallas_call x1, Pallas kernels, gather(): pl.pallas_call(functools.partial(gather_kernel, sizes), out_shape=[jax.Sh...  80.4 us
    pallas_call x1, Pallas kernels, moe(): pl.pallas_call(moe_kernel, grid=(steps,), in_specs=[rows(toks, width), ro...  64.2 us
    dot_general x5, matrix products, dot_nt(): lax.dot_general(left, right, (((1,), (1,)), ((), ())), preferred_element_...  24.1 us
  transfers between devices with their start and end apart: 4, of which 0 were waited for; matrix products, arithmetic and copies ran while one was open for 12% of the time, Pallas kernels for 40%

profile of v4, /device:TPU:0, one launch (start us, length us, event | category | flops | bytes accessed | tf_op | source)
XLA Modules:
  0.0 866.3 jit_solution(7406655104080104400)
XLA Ops:
  19.5 186.1 %shard_map.280 = (bf16[4,2,2,2,64,5248]{5,4,3,2,1,0:T(8,128)(2,1)}, bf16[4,2,2,1,128,2176]{5,4,3,2,1,0:T(8,128)(2,1)}, bf16[2,2,512,1408]{3,2,1,0:T(8,128)(2,1)}...) custom-call(bf16[64,5248]{1,0:T(8,128)(2,1)} %copy-done.14, ...), custom_call_target="tpu_custom_call" | custom-call | tf_op jit(solution)/shard_map/pallas_call | solution.py:515
  210.4 4.6 fusion.27
  225.6 4.9 multiply_reduce_fusion.3
  242.6 2.7 fusion.72
  247.4 80.4 %shard_map.281 = (bf16[4,2,2,1,128,2048]{5,4,3,2,1,0:T(8,128)(2,1)}, bf16[2,2,512,1408]{3,2,1,0:T(8,128)(2,1)}) custom-call(bf16[128,2048]{1,0:T(8,128)(2,1)} %multiply_convert_fusion.1.x_ref, bf16[2,512,1408]{2,1,0:T(8,128)(2,1)} %shard.1), custom_call_target="tpu_custom_call" | custom-call | tf_op jit(solution)/shard_map/pallas_call | solution.py:368
  327.8 3.0 fusion.19.sgu_ref.refs_4_
  330.8 64.2 %shard_map.282 = (bf16[1024,2048]{1,0:T(8,128)(2,1)}, bf16[1024,2048]{1,0:T(8,128)(2,1)}, bf16[1024,1408]{1,0:T(8,128)(2,1)}, bf16[1024,1408]{1,0:T(8,128)(2,1)}...) custom-call(bf16[2048,2048]{1,0:T(8,128)(2,1)} %bitcast.206, ...), custom_call_target="tpu_custom_call" | custom-call | flops 60000002048 | bytes 100000000 | tf_op jit(solution)/shard_map/pallas_call | solution.py:1261
  396.4 3.8 all-to-all-start
  400.3 99.0 %shard_map.283 = (bf16[2048,2048]{1,0:T(8,128)(2,1)}, f32[128,2048]{1,0:T(8,128)}) custom-call(bf16[1024,1408]{1,0:T(8,128)(2,1)} %get-tuple-element.55.refs_0_.refs_3_, bf16[1024,1408]{1,0:T(8,128)(2,1)} %get-tuple-element.56.refs_1_.refs_4_, bf16[2048,1408]{1,0:T(8,128)(2,1)} %bitcast.150, bf16[2048,1408]{1,0:T(8,128)(2,1)} %bitcast.152, ...), custom_call_target="tpu_custom_call" | custom-call | tf_op jit(solution)/shard_map/pallas_call | solution.py:895
  499.4 98.5 %shard_map.284 = (f32[512,1408]{1,0:T(8,128)}, f32[512,1408]{1,0:T(8,128)}, f32[512,1408]{1,0:T(8,128)}, bf16[1,512,1408]{2,1,0:T(8,128)(2,1)}, bf16[1,512,1408]...) custom-call(bf16[1024,2048]{1,0:T(8,128)(2,1)} %get-tuple-element.60.refs_0_, ...), custom_call_target="tpu_custom_call" | custom-call | tf_op jit(solution)/shard_map/pallas_call | solution.py:1118
  599.9 6.2 fusion.1
  606.2 9.9 %convolution_convert_fusion = bf16[2048,512]{1,0:T(8,128)(2,1)} fusion(bf16[2048,2048]{1,0:T(8,128)(2,1)} %bitcast.207, bf16[2048,512]{1,0:T(8,128)(2,1)} %get-tuple-element.57.refs_5_), kind=kOutput, calls=%fused_computation.15 | convolution fusion | flops 4296015872 | bytes 12582912 | tf_op jit(solution)/shard_map/dot_general | solution.py:33
  624.2 7.4 fusion.16
  633.7 2.9 fusion.40
  641.0 2.6 copy.190
  648.1 7.2 fusion.7
  658.3 2.9 convolution_add_fusion.1
  661.2 4.0 fusion.42
  675.0 151.1 %shard_map.285 = (f32[64,5248]{1,0:T(8,128)}, bf16[4,2,2,64,512]{4,3,2,1,0:T(8,128)(2,1)}, bf16[1,512,1408]{2,1,0:T(8,128)(2,1)}) custom-call(bf16[128,2048]{1,0:T(8,128)(2,1)} %copy-done.12, bf16[128,3072]{1,0:T(8,128)(2,1)} %pad_maximum_fusion.grads, bf16[128,2048]{1,0:T(8,128)(2,1)} %copy.181.mixed, bf16[128,2048]{1,0:T(8,128)(2,1)} %copy-done.13, ...), custom_call_target="tpu_custom_call" | custom-call | tf_op jit(solution)/shard_map/pallas_call | solution.py:999
  830.1 3.2 convert_element_type.244
  836.4 2.6 reshape.300
  839.1 2.8 copy.166
  841.9 2.6 reshape.301
  850.7 8.5 broadcast_select_fusion
  (214 shorter events, 89.9 us)
Async XLA Ops:
  7.2 8.6 copy-start.3
  7.2 9.4 %copy-start.31 = (bf16[64,512]{1,0:T(8,128)(2,1)S(1)}, bf16[64,512]{1,0:T(8,128)(2,1)}, u32[]{:S(2)}) copy-start(bf16[64,512]{1,0:T(8,128)(2,1)} %param.22) | copy-start | bytes 196612
  9.5 7.9 copy-start.30
  19.5 188.2 %copy-start.2 = (bf16[128,2048]{1,0:T(8,128)(2,1)S(1)}, bf16[128,2048]{1,0:T(8,128)(2,1)}, u32[]{:S(2)}) copy-start(bf16[128,2048]{1,0:T(8,128)(2,1)} %param.17) | copy-start | bytes 1572868
  207.9 7.1 copy-start.46
  207.9 7.1 copy-start.40
  208.1 6.9 copy-start.12
  223.8 6.8 copy-start.36
  230.6 6.0 copy-start.51
  230.6 5.8 copy-start.48
  396.4 222.7 %all-to-all-start = ((f32[16,1,128]{2,1,0:T(1,128)}), f32[16,1,128]{2,1,0:T(1,128)S(1)}, u32[]{:S(2)}, u32[]{:S(2)}) async-start(f32[16,1,128]{2,1,0:T(1,128)} %bitcast.26), calls=%async_computation | async-start | bytes 16384 | tf_op jit(solution)/shard_map/all_to_all | solution.py:1416
  400.3 459.0 %reduce-scatter.2.cloned.1.call-start = ((), (), s32[]{:S(2)}) async-start(), calls=%async_computation.2 | async-start | bytes 2162688 | tf_op jit(solution)/shard_map/reduce_scatter | solution.py:1432
  499.3 100.6 %copy-start.53 = (bf16[2048,256]{1,0:T(8,128)(2,1)S(1)}, bf16[2048,256]{1,0:T(8,128)(2,1)}, u32[]{:S(2)}) copy-start(bf16[2048,256]{1,0:T(8,128)(2,1)} %get-tuple-element.72) | copy-start | bytes 3145732
  597.8 77.2 %collective-permute-start = (bf16[512,1408]{1,0:T(8,128)(2,1)}, bf16[512,1408]{1,0:T(8,128)(2,1)}, u32[]{:S(2)}, u32[]{:S(2)}) collective-permute-start(bf16[512,1408]{1,0:T(8,128)(2,1)} %bitcast.210), channel_id=1, source_target_pairs={{0,2},{2,0},{1,3},{3,1},{4,6},{6,4},{5,7},{7,5},{8,10},{10,8},{9,1... | collective-permute-start | bytes 4325384 | tf_op jit(solution)/shard_map/ppermute | solution.py:1425
  599.8 75.3 %collective-permute-start.1 = (bf16[512,1408]{1,0:T(8,128)(2,1)}, bf16[512,1408]{1,0:T(8,128)(2,1)}, u32[]{:S(2)}, u32[]{:S(2)}) collective-permute-start(bf16[512,1408]{1,0:T(8,128)(2,1)} %bitcast.209), channel_id=1, source_target_pairs={{0,2},{2,0},{1,3},{3,1},{4,6},{6,4},{5,7},{7,5},{8,10},{10,8},{9,1... | collective-permute-start | bytes 4325384 | tf_op jit(solution)/shard_map/ppermute | solution.py:1425
  606.1 10.0 %copy-start.1 = (bf16[128,2048]{1,0:T(8,128)(2,1)S(1)}, bf16[128,2048]{1,0:T(8,128)(2,1)}, u32[]{:S(2)}) copy-start(bf16[128,2048]{1,0:T(8,128)(2,1)} %multiply_convert_fusion.1.x_ref) | copy-start | bytes 1572868
  606.1 10.0 %copy-start.34 = (pred[128,16]{0,1:T(8,128)(4,1)S(1)}, pred[128,16]{0,1:T(8,128)(4,1)}, u32[]{:S(2)}) copy-start(pred[128,16]{0,1:T(8,128)(4,1)} %copy-done.33) | copy-start | bytes 6148
  606.2 11.9 %copy-start.28 = (bf16[4,128,4,128]{3,1,2,0:T(8,128)(2,1)S(1)}, bf16[4,128,4,128]{3,1,2,0:T(8,128)(2,1)}, u32[]{:S(2)}) copy-start(bf16[4,128,4,128]{3,1,2,0:T(8,128)(2,1)} %copy-done.27) | copy-start | bytes 1572868
  624.2 9.4 %copy-start.20 = (bf16[128,4,64]{2,0,1:T(8,128)(2,1)S(1)}, bf16[128,4,64]{2,0,1:T(8,128)(2,1)}, u32[]{:S(2)}) copy-start(bf16[128,4,64]{2,0,1:T(8,128)(2,1)} %copy-done.19) | copy-start | bytes 196612
  624.2 9.4 %copy-start.23 = (bf16[128,4,64]{2,0,1:T(8,128)(2,1)S(1)}, bf16[128,4,64]{2,0,1:T(8,128)(2,1)}, u32[]{:S(2)}) copy-start(bf16[128,4,64]{2,0,1:T(8,128)(2,1)} %copy-done.22) | copy-start | bytes 196612
  665.2 5.4 copy-start.6
  668.2 5.2 copy-start.4
  668.2 5.2 copy-start.15
  668.2 5.2 copy-start.39
  (34 other events, 108.1 us)
Sparse Core Ops, SparseCore 0:
  606.3 20.6 reduce-scatter.1
